TPU v7x, 128 devices: a whole 4x4x4 slice. The times are simulated.
128 devices in a mesh: seq: 16 (over z, y), head: 8 (over x, core).
Axes of the slice: x: 4, y: 4, z: 4, core: 2. Of those that a mesh axis runs over, the one named last changes fastest.
Arguments:
- query_rows: bfloat16 [32768, 3072], P(('seq', 'head')), may hold values from -32 to 32
- key_rows: bfloat16 [32768, 3072], P(('seq', 'head')), may hold values from -32 to 32
- value_rows: bfloat16 [32768, 3072], P(('seq', 'head')), may hold values from -6 to 6
- query_cluster: int32 [24, 32768], P('head', 'seq'), may hold values from 0 to 255, as said below
- key_cluster: int32 [24, 32768], P('head', 'seq'), may hold values from 0 to 255, as said below
- cluster_pairs: int32 [24, 256, 16], P('head'), may hold values from 0 to 255, as said below
Outputs:
- attended: bfloat16 [32768, 3072], P(('seq', 'head'))
Inputs may be any that keep to these rules, and one draw needn't show every extreme that they name: `query_cluster`: for each head every cluster number names exactly 128 tokens. Cluster numbers form groups of 16 consecutive ones, numbered like the aligned blocks of 2048 token positions; for each head at most 192 tokens of one block lie in the clusters of one group, and some block and group reach it. `key_cluster`: likewise for key clusters: exactly 128 tokens a cluster, at most 192 tokens of one block in the clusters of one group, reached. `cluster_pairs`: each row names 16 different key clusters. For each head the rows of one group of 16 query clusters name at most 4 different key clusters of one group, and some pair of groups reaches it.
All inputs are finite; a program needn't handle non-finite values.
Results may differ from a plain program's by a relative error of at most 0.0047.
Values may be sent and summed in bfloat16 or wider, within the bound.
No kernel may reach another device: no remote copies, remote signals or barrier semaphores. Data moves between devices by JAX's collectives and lax.ppermute only.
A program may use at most 192 MiB of HBM per device.

v0:
```python
import math

import jax
import jax.numpy as jnp
from jax import lax
from jax.sharding import PartitionSpec as P

BLOCK = 128
PAIRS = 16
KCAP = 4


def slot_rank(labels, label_count):
    onehot = (labels[..., None] == jnp.arange(label_count, dtype=jnp.int32)).astype(jnp.int32)
    before = jnp.cumsum(onehot, axis=1) - onehot
    return jnp.sum(before * onehot, axis=-1)


def invert(where, length, source_count):
    heads_dev = where.shape[0]
    head_ids = jnp.arange(heads_dev, dtype=jnp.int32)[:, None]
    blank = jnp.full((heads_dev, length), source_count, jnp.int32)
    sources = jnp.broadcast_to(jnp.arange(source_count, dtype=jnp.int32)[None, :], where.shape)
    return blank.at[head_ids, where].set(sources, mode="drop")


def take_rows(matrix, indices):
    return jnp.take(matrix, indices, axis=0)


def gather_rows(rows, indices):
    return jax.vmap(take_rows)(rows, indices)


def pull_rows(rows, inverse):
    row_count = rows.shape[1]
    is_valid = inverse < row_count
    picked = gather_rows(rows, jnp.minimum(inverse, row_count - 1))
    return jnp.where(is_valid[..., None], picked, jnp.zeros((), rows.dtype))


def pull_ids(ids, inverse):
    row_count = ids.shape[1]
    is_valid = inverse < row_count
    picked = gather_rows(ids, jnp.minimum(inverse, row_count - 1))
    return jnp.where(is_valid, picked, -1)


def attend(query_blocks, key_recv, value_recv, fetch_rows):
    owned_count = query_blocks.shape[0]
    head_width = query_blocks.shape[2]
    received = key_recv.shape[0]
    selector = (fetch_rows[..., None] == jnp.arange(received, dtype=jnp.int32)).astype(jnp.bfloat16)
    key_used = jnp.einsum(
        "gpr,rbd->gpbd", selector, key_recv, preferred_element_type=jnp.float32
    ).astype(jnp.bfloat16)
    value_used = jnp.einsum(
        "gpr,rbd->gpbd", selector, value_recv, preferred_element_type=jnp.float32
    ).astype(jnp.bfloat16)
    key_used = key_used.reshape(owned_count, PAIRS * BLOCK, head_width)
    value_used = value_used.reshape(owned_count, PAIRS * BLOCK, head_width)
    score_scale = 1.0 / math.sqrt(head_width)
    scores = (
        jnp.einsum("gqd,gkd->gqk", query_blocks, key_used, preferred_element_type=jnp.float32)
        * score_scale
    )
    row_max = jnp.max(scores, axis=-1, keepdims=True)
    weights = jnp.exp(scores - row_max)
    total = jnp.sum(weights, axis=-1, keepdims=True)
    mixed = jnp.einsum(
        "gqk,gkd->gqd", weights.astype(jnp.bfloat16), value_used, preferred_element_type=jnp.float32
    )
    return (mixed / total).astype(jnp.bfloat16)


def attend_packed(packed):
    return attend(packed[0], packed[1], packed[2], packed[3])


def per_device(query_rows, key_rows, value_rows, query_cluster, key_cluster, cluster_pairs):
    heads_dev, tok_count = query_cluster.shape
    seq_count = lax.axis_size("seq")
    my_index = lax.axis_index("seq")
    cluster_total = cluster_pairs.shape[1]
    owned_count = cluster_total // seq_count
    capacity = 3 * tok_count // (2 * seq_count)
    slot_total = seq_count * capacity
    head_width = query_rows.shape[1] // (heads_dev * lax.axis_size("head"))
    head_ids = jnp.arange(heads_dev, dtype=jnp.int32)[:, None]
    query_tok, key_tok, value_tok = (
        lax.all_to_all(query_rows, "head", split_axis=1, concat_axis=0, tiled=True),
        lax.all_to_all(key_rows, "head", split_axis=1, concat_axis=0, tiled=True),
        lax.all_to_all(value_rows, "head", split_axis=1, concat_axis=0, tiled=True),
    )

    def by_head(rows):
        return rows.reshape(tok_count, heads_dev, head_width).transpose(1, 0, 2)

    query_dest = query_cluster // owned_count
    key_dest = key_cluster // owned_count
    query_slot = query_dest * capacity + slot_rank(query_dest, seq_count)
    key_slot = key_dest * capacity + slot_rank(key_dest, seq_count)
    query_inverse = invert(query_slot, slot_total, tok_count)
    key_inverse = invert(key_slot, slot_total, tok_count)

    def pack_rows(rows, inverse):
        return pull_rows(rows, inverse).reshape(heads_dev, seq_count, capacity, head_width)

    def pack_ids(ids, inverse):
        return pull_ids(ids, inverse).reshape(heads_dev, seq_count, capacity)

    sent = (
        pack_rows(by_head(query_tok), query_inverse),
        pack_rows(by_head(key_tok), key_inverse),
        pack_rows(by_head(value_tok), key_inverse),
        pack_ids(query_cluster, query_inverse),
        pack_ids(key_cluster, key_inverse),
    )
    query_in, key_in, value_in, qid_in, kid_in = (
        lax.all_to_all(sent[0], "seq", split_axis=1, concat_axis=1, tiled=True),
        lax.all_to_all(sent[1], "seq", split_axis=1, concat_axis=1, tiled=True),
        lax.all_to_all(sent[2], "seq", split_axis=1, concat_axis=1, tiled=True),
        lax.all_to_all(sent[3], "seq", split_axis=1, concat_axis=1, tiled=True),
        lax.all_to_all(sent[4], "seq", split_axis=1, concat_axis=1, tiled=True),
    )

    def place(ids):
        flat_ids = ids.reshape(heads_dev, slot_total)
        is_valid = flat_ids >= 0
        local_ids = jnp.where(is_valid, flat_ids - my_index * owned_count, owned_count)
        within = slot_rank(local_ids, owned_count)
        return jnp.where(is_valid, local_ids * BLOCK + within, owned_count * BLOCK)

    query_place = place(qid_in)
    key_place = place(kid_in)
    query_gather = invert(query_place, owned_count * BLOCK, slot_total)
    key_gather = invert(key_place, owned_count * BLOCK, slot_total)

    def cluster_rows(rows, inverse):
        flat_rows = rows.reshape(heads_dev, slot_total, head_width)
        return pull_rows(flat_rows, inverse).reshape(heads_dev, owned_count, BLOCK, head_width)

    query_groups = cluster_rows(query_in, query_gather)
    key_groups = cluster_rows(key_in, key_gather)
    value_groups = cluster_rows(value_in, key_gather)
    local_pairs = cluster_pairs - my_index * owned_count
    pair_match = local_pairs[..., None] == jnp.arange(owned_count, dtype=jnp.int32)
    needed = (
        jnp.any(pair_match, axis=2)
        .reshape(heads_dev, seq_count, owned_count, owned_count)
        .any(axis=2)
    )
    needed_count = needed.astype(jnp.int32)
    send_order = jnp.cumsum(needed_count, axis=2) - needed_count
    slot_hits = needed[:, :, None, :] & (
        send_order[:, :, None, :] == jnp.arange(KCAP, dtype=jnp.int32)[:, None]
    )
    pick_table = slot_hits.astype(jnp.bfloat16)

    def send_blocks(groups):
        chosen = jnp.einsum(
            "hskc,hcbd->hskbd", pick_table, groups, preferred_element_type=jnp.float32
        )
        return chosen.astype(groups.dtype)

    own_rows = lax.dynamic_slice_in_dim(cluster_pairs, my_index * owned_count, owned_count, 1)
    flat_own = own_rows.reshape(heads_dev, owned_count * PAIRS)
    wanted = jnp.any(flat_own[..., None] == jnp.arange(cluster_total, dtype=jnp.int32), axis=1)
    wanted_count = wanted.astype(jnp.int32).reshape(heads_dev, seq_count, owned_count)
    cluster_rank = jnp.cumsum(wanted_count, axis=2) - wanted_count
    position = (
        jnp.arange(seq_count, dtype=jnp.int32)[None, :, None] * KCAP + cluster_rank
    ).reshape(heads_dev, cluster_total)
    fetch_rows = position[head_ids, flat_own].reshape(heads_dev, owned_count, PAIRS)
    key_send = send_blocks(key_groups)
    value_send = send_blocks(value_groups)
    key_recv, value_recv = (
        lax.all_to_all(key_send, "seq", split_axis=1, concat_axis=1, tiled=True),
        lax.all_to_all(value_send, "seq", split_axis=1, concat_axis=1, tiled=True),
    )
    key_flat = key_recv.reshape(heads_dev, seq_count * KCAP, BLOCK, head_width)
    value_flat = value_recv.reshape(heads_dev, seq_count * KCAP, BLOCK, head_width)
    attended_heads = lax.map(attend_packed, (query_groups, key_flat, value_flat, fetch_rows))
    outputs_flat = attended_heads.reshape(heads_dev, owned_count * BLOCK, head_width)
    reply = gather_rows(outputs_flat, jnp.minimum(query_place, owned_count * BLOCK - 1))
    reply = reply.reshape(heads_dev, seq_count, capacity, head_width)
    returned = lax.all_to_all(reply, "seq", split_axis=1, concat_axis=1, tiled=True).reshape(
        heads_dev, slot_total, head_width
    )
    token_rows = gather_rows(returned, query_slot)
    token_rows = token_rows.transpose(1, 0, 2).reshape(tok_count, heads_dev * head_width)
    return lax.all_to_all(token_rows, "head", split_axis=0, concat_axis=1, tiled=True)


def solution(mesh):
    in_specs = (
        P(("seq", "head"), None),
        P(("seq", "head"), None),
        P(("seq", "head"), None),
        P("head", "seq"),
        P("head", "seq"),
        P("head", None, None),
    )
    out_specs = P(("seq", "head"), None)
    return jax.shard_map(
        per_device, mesh=mesh, in_specs=in_specs, out_specs=out_specs, check_vma=False
    )
```

profile of v0, /device:TPU:1, one launch (start us, length us, event | category | flops | bytes accessed | tf_op | source)
XLA Modules:
  0.0 1579.8 jit_solution(17963753668857756747)
XLA Ops:
  3.3 13.6 reduce-window.26
  19.5 13.6 reduce-window.34
  35.4 23.0 %scatter_custom_fusion = s32[9216]{0:T(1024)S(1)} fusion(s32[6144]{0:T(1024)S(1)} %reshape.478, s32[6144]{0:T(1024)S(1)} %reshape.480, s32[]{:T(128)} %constant.112.clone.1), kind=kCustom, calls=%fused_computation.171 | custom fusion | bytes 36868
  58.6 77.9 %gather_fusion.1 = s32[9216]{0:T(1024)S(1)} fusion(s32[3,2048]{1,0:T(4,128)S(1)} %copy-done, s32[9216]{0:T(1024)S(1)} %reshape.554), kind=kCustom, calls=%fused_computation.clone | custom fusion | bytes 147456 | tf_op jit(solution)/shard_map/vmap(jit(_take))/gather | solution.py:28
  138.0 8.6 all-to-all-start
  146.6 23.0 %scatter_custom_fusion.2 = s32[9216]{0:T(1024)S(1)} fusion(s32[6144]{0:T(1024)S(1)} %reshape.490, s32[6144]{0:T(1024)S(1)} %reshape.480, s32[]{:T(128)} %constant.112.clone.1), kind=kCustom, calls=%fused_computation.169 | custom fusion | bytes 36868
  169.8 77.9 %gather_fusion.4 = s32[9216]{0:T(1024)S(1)} fusion(s32[3,2048]{1,0:T(4,128)S(1)} %copy-done.2, s32[9216]{0:T(1024)S(1)} %reshape.569), kind=kCustom, calls=%fused_computation.3.clone | custom fusion | bytes 147456 | tf_op jit(solution)/shard_map/vmap(jit(_take))/gather | solution.py:28
  249.1 6.7 all-to-all-start.3
  257.4 4.9 all-to-all-done.3
  262.3 7.0 all-to-all-start.4
  270.8 19.1 %all-to-all-done.4 = bf16[256,8,384]{0,2,1:T(8,128)(2,1)S(1)} async-done(((bf16[256,8,384]{0,2,1:T(8,128)(2,1)}), bf16[256,8,384]{0,2,1:T(8,128)(2,1)S(1)}, u32[]{:S(2)}, u32[]{:S(2)}) %all-to-all-start.4) | async-done | bytes 1572896 | tf_op jit(solution)/shard_map/all_to_all | solution.py:92
  290.0 4.4 all-to-all-start.7
  299.6 15.5 all-to-all-done.7
  316.2 4.6 all-to-all-start.1
  325.4 26.3 %reduce-window.30 = s32[3,16,24,128]{3,2,1,0:T(8,128)} reduce-window(s32[3,16,24,128]{3,2,1,0:T(8,128)} %fusion.32, s32[]{:T(128)} %copy.211), window={size=1x1x1x128 pad=0_0x0_0x0_0x127_0}, to_apply=%region_4.6 | reduce-window | flops 18726912 | bytes 1179652 | tf_op jit(solution)/shard_map/reduce-window.2
  366.2 89.7 %gather_fusion.5 = bf16[9216,128]{1,0:T(8,128)(2,1)} fusion(bf16[3,2048,128]{2,1,0:T(8,128)(2,1)S(1)} %bitcast.208, s32[9216]{0:T(1024)S(1)} %reshape.569), kind=kCustom, calls=%fused_computation.4.clone | custom fusion | bytes 4792320 | tf_op jit(solution)/shard_map/vmap(jit(_take))/gather | solution.py:28
  462.2 89.7 %gather_fusion.7 = bf16[9216,128]{1,0:T(8,128)(2,1)} fusion(bf16[3,2048,128]{2,1,0:T(8,128)(2,1)S(1)} %bitcast.206, s32[9216]{0:T(1024)S(1)} %reshape.569), kind=kCustom, calls=%fused_computation.5.clone | custom fusion | bytes 4792320 | tf_op jit(solution)/shard_map/vmap(jit(_take))/gather | solution.py:28
  551.9 9.7 select_select_fusion
  568.9 24.0 %reduce-window.36 = s32[3,16,24,128]{3,2,1,0:T(8,128)S(1)} reduce-window(s32[3,16,24,128]{3,2,1,0:T(8,128)} %fusion.33, s32[]{:T(128)} %copy.211), window={size=1x1x1x128 pad=0_0x0_0x0_0x127_0}, to_apply=%region_15.19 | reduce-window | flops 18726912 | bytes 1179652 | tf_op jit(solution)/shard_map/reduce-window.6
  605.7 4.4 all-to-all-start.8
  610.6 34.8 %scatter_custom_fusion.3 = s32[6144]{0:T(1024)S(1)} fusion(s32[9216]{0:T(1024)S(1)} %reshape.496, s32[9216]{0:T(1024)} %reshape.486, s32[]{:T(128)} %constant.111.clone.1), kind=kCustom, calls=%fused_computation.179 | custom fusion | bytes 25088
  654.6 89.6 %gather_fusion.2 = bf16[9216,128]{1,0:T(8,128)(2,1)} fusion(bf16[3,2048,128]{2,1,0:T(8,128)(2,1)S(1)} %bitcast.207, s32[9216]{0:T(1024)S(1)} %reshape.554), kind=kCustom, calls=%fused_computation.1.clone | custom fusion | bytes 4792320 | tf_op jit(solution)/shard_map/vmap(jit(_take))/gather | solution.py:28
  744.2 7.7 select_select_fusion.2
  753.5 6.6 all-to-all-start.2
  762.1 60.1 %gather_fusion.6 = bf16[6144,128]{1,0:T(8,128)(2,1)} fusion(bf16[3,3072,128]{2,1,0:T(8,128)(2,1)S(1)} %bitcast.214, s32[6144]{0:T(1024)S(1)} %reshape.579), kind=kCustom, calls=%fused_computation.7.clone | custom fusion | bytes 3194880 | tf_op jit(solution)/shard_map/vmap(jit(_take))/gather | solution.py:28
  824.0 60.7 %gather_fusion.8 = bf16[6144,128]{1,0:T(8,128)(2,1)} fusion(bf16[3,3072,128]{2,1,0:T(8,128)(2,1)S(1)} %bitcast.211, s32[6144]{0:T(1024)S(1)} %reshape.579), kind=kCustom, calls=%fused_computation.8.clone | custom fusion | bytes 3194880 | tf_op jit(solution)/shard_map/vmap(jit(_take))/gather | solution.py:28
  884.8 5.7 select_select_fusion.3
  896.6 6.8 all-to-all-start.6
  909.5 84.7 %all-to-all-done.6 = bf16[3,16,4,128,128]{4,3,2,0,1:T(8,128)(2,1)} async-done(((bf16[3,16,4,128,128]{4,3,2,0,1:T(8,128)(2,1)}), bf16[3,16,4,128,128]{4,3,2,0,1:T(8,128)(2,1)}, u32[]{:S(2)}, u32[]{:S(2)}) %all-to-all-start.6) | async-done | bytes 6291488 | tf_op jit(solution)/shard_map/all_to_all | solution.py:178
  994.2 4.7 all-to-all-start.9
  1000.3 6.7 gather_fusion
  1007.7 34.4 %scatter_custom_fusion.1 = s32[6144]{0:T(1024)S(1)} fusion(s32[9216]{0:T(1024)S(1)} %reshape.484, s32[9216]{0:T(1024)} %reshape.486, s32[]{:T(128)} %constant.111.clone.1), kind=kCustom, calls=%fused_computation.181 | custom fusion | bytes 25088
  1046.3 100.8 %gather_fusion.3 = bf16[6144,128]{1,0:T(8,128)(2,1)} fusion(bf16[3,3072,128]{2,1,0:T(8,128)(2,1)} %bitcast.212, s32[6144]{0:T(1024)S(1)} %reshape.564), kind=kCustom, calls=%fused_computation.2.clone | custom fusion | bytes 3194880 | tf_op jit(solution)/shard_map/vmap(jit(_take))/gather | solution.py:28
  1147.0 5.2 select_select_fusion.5
  1152.2 8.0 copy.153
  1160.2 8.0 copy.161
  1168.3 182.6 %while.10 = (s32[]{:T(128)}, bf16[3,16,128,128]{3,2,1,0:T(8,128)(2,1)S(1)}, bf16[3,16,128,128]{3,2,1,0:T(8,128)(2,1)S(1)}, s32[3,16,16]{2,1,0:T(8,128)S(1)}, bf1...) while((s32[]{:T(128)}, bf16[3,16,128,128]{3,2,1,0:T(8,128)(2,1)S(1)}, ...), condition=%wide.region_24.28_spmd, body=%wide.region_21.27_spmd.sunk | while | flops 3263721472 | bytes 198226064 | solution.py:183
  1171.2 5.7 convolution_convert_fusion.6
  1176.9 9.1 copy.201
  1186.0 5.7 convolution_convert_fusion.7
  1191.7 9.1 copy.202
  1200.8 11.4 multiply_reduce_fusion.6
  1212.2 8.5 fusion.83
  1222.9 6.2 fusion.84
  1231.9 5.7 convolution_convert_fusion.6
  1237.6 9.1 copy.201
  1246.7 5.7 convolution_convert_fusion.7
  1252.4 9.1 copy.202
  1261.5 11.4 multiply_reduce_fusion.6
  1273.0 8.5 fusion.83
  1283.6 6.2 fusion.84
  1292.6 5.7 convolution_convert_fusion.6
  1298.3 9.1 copy.201
  1307.4 5.7 convolution_convert_fusion.7
  1313.1 9.1 copy.202
  1322.2 11.4 multiply_reduce_fusion.6
  1333.7 8.5 fusion.83
  1344.3 6.2 fusion.84
  1350.9 89.8 %gather_fusion.9 = bf16[9216,128]{1,0:T(8,128)(2,1)} fusion(bf16[3,2048,128]{2,1,0:T(8,128)(2,1)S(1)} %bitcast.209, s32[9216]{0:T(1024)} %reshape.594), kind=kCustom, calls=%fused_computation.6.clone | custom fusion | bytes 4792320 | tf_op jit(solution)/shard_map/vmap(jit(_take))/gather | solution.py:28
  1440.7 5.0 broadcast_select_fusion
  1447.2 7.0 all-to-all-start.10
  1454.4 27.3 %all-to-all-done.10 = bf16[3,16,192,128]{3,2,0,1:T(8,128)(2,1)} async-done(((bf16[3,16,192,128]{3,2,0,1:T(8,128)(2,1)}), bf16[3,16,192,128]{3,2,0,1:T(8,128)(2,1)}, u32[]{:S(2)}, u32[]{:S(2)}) %all-to-all-start.10) | async-done | bytes 2359328 | tf_op jit(solution)/shard_map/all_to_all | solution.py:187
  1483.5 60.7 %gather_fusion.10 = bf16[6144,128]{1,0:T(8,128)(2,1)} fusion(bf16[3,3072,128]{2,1,0:T(8,128)(2,1)S(1)} %bitcast.213, s32[6144]{0:T(1024)S(1)} %reshape.599), kind=kCustom, calls=%fused_computation.9.clone | custom fusion | bytes 3194880 | tf_op jit(solution)/shard_map/vmap(jit(_take))/gather | solution.py:28
  1547.0 30.6 %all_to_all.107 = bf16[8,256,384]{1,2,0:T(8,128)(2,1)S(1)} all-to-all(bf16[8,256,384]{1,2,0:T(8,128)(2,1)S(1)} %copy.167), channel_id=1, replica_groups=mesh['seq'=16,'head'=8] {'head'}, dimensions={0} | all-to-all | bytes 3145728 | tf_op jit(solution)/shard_map/all_to_all | solution.py:192
  (234 shorter events, 121.7 us)
Async XLA Ops:
  0.0 18.9 %copy-start = (s32[3,2048]{1,0:T(4,128)S(1)}, s32[3,2048]{1,0:T(4,128)}, u32[]{:S(2)}) copy-start(s32[3,2048]{1,0:T(4,128)} %param.17) | copy-start | bytes 73732
  16.9 18.1 %copy-start.2 = (s32[3,2048]{1,0:T(4,128)S(1)}, s32[3,2048]{1,0:T(4,128)}, u32[]{:S(2)}) copy-start(s32[3,2048]{1,0:T(4,128)} %param.18) | copy-start | bytes 73732
  16.9 18.2 %copy-start.27 = (s32[2]{0:T(128)S(1)}, s32[2]{0:T(128)}, u32[]{:S(2)}) copy-start(s32[2]{0:T(128)} %constant.132) | copy-start | bytes 28
  18.0 17.3 %copy-start.26 = (s32[2]{0:T(128)S(1)}, s32[2]{0:T(128)}, u32[]{:S(2)}) copy-start(s32[2]{0:T(128)} %constant.129) | copy-start | bytes 28
  18.9 0.6 copy-start.9
  58.5 78.1 %copy-start.13 = (pred[3,3072]{1,0:T(4,128)(4,1)}, pred[3,3072]{1,0:T(4,128)(4,1)S(1)}, u32[]{:S(2)}) copy-start(pred[3,3072]{1,0:T(4,128)(4,1)S(1)} %reshape.396) | copy-start | bytes 27652
  138.0 111.2 %all-to-all-start = ((s32[3,16,192]{2,0,1:T(4,128)}), s32[3,16,192]{2,0,1:T(4,128)S(1)}, u32[]{:S(2)}, u32[]{:S(2)}) async-start(s32[3,16,192]{2,0,1:T(4,128)} %copy.127), calls=%async_computation | async-start | bytes 131072 | tf_op jit(solution)/shard_map/all_to_all | solution.py:123
  169.6 78.1 %copy-start.17 = (pred[3,3072]{1,0:T(4,128)(4,1)}, pred[3,3072]{1,0:T(4,128)(4,1)S(1)}, u32[]{:S(2)}) copy-start(pred[3,3072]{1,0:T(4,128)(4,1)S(1)} %reshape.405) | copy-start | bytes 27652
  169.7 86.0 %copy-start.7 = (bf16[256,3072]{1,0:T(8,128)(2,1)S(1)}, bf16[256,3072]{1,0:T(8,128)(2,1)}, u32[]{:S(2)}) copy-start(bf16[256,3072]{1,0:T(8,128)(2,1)} %param.15) | copy-start | bytes 4718596
  249.1 13.2 all-to-all-start.3
  255.8 13.5 copy-start.8
  262.3 27.7 %all-to-all-start.4 = ((bf16[256,8,384]{0,2,1:T(8,128)(2,1)}), bf16[256,8,384]{0,2,1:T(8,128)(2,1)S(1)}, u32[]{:S(2)}, u32[]{:S(2)}) async-start(bf16[256,8,384]{0,2,1:T(8,128)(2,1)} %bitcast.35), calls=%async_computation.4 | async-start | bytes 3145728 | tf_op jit(solution)/shard_map/all_to_all | solution.py:92
  269.2 25.7 %copy-start.15 = (s32[3,256,16]{1,2,0:T(8,128)S(1)}, s32[3,256,16]{1,2,0:T(8,128)}, u32[]{:S(2)}) copy-start(s32[3,256,16]{1,2,0:T(8,128)} %param.19) | copy-start | bytes 147460
  290.0 25.1 %all-to-all-start.7 = ((bf16[256,8,384]{0,2,1:T(8,128)(2,1)}), bf16[256,8,384]{0,2,1:T(8,128)(2,1)S(1)}, u32[]{:S(2)}, u32[]{:S(2)}) async-start(bf16[256,8,384]{0,2,1:T(8,128)(2,1)} %bitcast.230), calls=%async_computation.7 | async-start | bytes 3145728 | tf_op jit(solution)/shard_map/all_to_all | solution.py:93
  315.1 1.2 copy-start.6
  316.2 247.0 %all-to-all-start.1 = ((bf16[256,8,384]{0,2,1:T(8,128)(2,1)}), bf16[256,8,384]{0,2,1:T(8,128)(2,1)S(1)}, u32[]{:S(2)}, u32[]{:S(2)}) async-start(bf16[256,8,384]{0,2,1:T(8,128)(2,1)} %bitcast.229), calls=%async_computation.1 | async-start | bytes 3145728 | tf_op jit(solution)/shard_map/all_to_all | solution.py:91
  462.2 89.7 %copy-start.18 = (pred[3,3072]{1,0:T(4,128)(4,1)S(1)}, pred[3,3072]{1,0:T(4,128)(4,1)}, u32[]{:S(2)}) copy-start(pred[3,3072]{1,0:T(4,128)(4,1)} %copy-done.17) | copy-start | bytes 27652
  462.2 89.7 %copy-start.23 = (pred[3,3072]{1,0:T(4,128)(4,1)S(1)}, pred[3,3072]{1,0:T(4,128)(4,1)}, u32[]{:S(2)}) copy-start(pred[3,3072]{1,0:T(4,128)(4,1)} %get-tuple-element.100) | copy-start | bytes 27652
  563.2 4.9 copy-start.12
  563.2 1.1 copy-start.5
  564.3 41.4 %all-to-all-start.5 = ((bf16[3,16,192,128]{3,2,0,1:T(8,128)(2,1)}), bf16[3,16,192,128]{3,2,0,1:T(8,128)(2,1)S(1)}, u32[]{:S(2)}, u32[]{:S(2)}) async-start(bf16[3,16,192,128]{3,2,0,1:T(8,128)(2,1)} %copy.149), calls=%async_computation.5 | async-start | bytes 4718592 | tf_op jit(solution)/shard_map/all_to_all | solution.py:121
  568.1 30.0 %copy-start.11 = (s32[3,3072]{1,0:T(4,128)S(1)}, s32[3,3072]{1,0:T(4,128)}, u32[]{:S(2)}) copy-start(s32[3,3072]{1,0:T(4,128)} %select_n.182) | copy-start | bytes 110596
  568.1 30.2 %copy-start.20 = (pred[3,3072,1]{1,0,2:T(4,128)(4,1)S(1)}, pred[3,3072,1]{1,0,2:T(4,128)(4,1)}, u32[]{:S(2)}) copy-start(pred[3,3072,1]{1,0,2:T(4,128)(4,1)} %ge.56) | copy-start | bytes 27652
  601.6 8.6 copy-start.21
  601.6 8.6 copy-start.25
  601.6 8.8 copy-start.24
  605.7 43.2 %copy-start.4 = (bf16[3,16,192,128]{3,2,0,1:T(8,128)(2,1)}, bf16[3,16,192,128]{3,2,0,1:T(8,128)(2,1)S(1)}, u32[]{:S(2)}) copy-start(bf16[3,16,192,128]{3,2,0,1:T(8,128)(2,1)S(1)} %all-to-all-done.5) | copy-start | bytes 7077892
  605.7 147.8 %all-to-all-start.8 = ((bf16[3,16,192,128]{3,2,0,1:T(8,128)(2,1)}), bf16[3,16,192,128]{3,2,0,1:T(8,128)(2,1)}, u32[]{:S(2)}, u32[]{:S(2)}) async-start(bf16[3,16,192,128]{3,2,0,1:T(8,128)(2,1)} %copy.157), calls=%async_computation.8 | async-start | bytes 4718592 | tf_op jit(solution)/shard_map/all_to_all | solution.py:122
  654.6 89.7 %copy-start.14 = (pred[3,3072]{1,0:T(4,128)(4,1)S(1)}, pred[3,3072]{1,0:T(4,128)(4,1)}, u32[]{:S(2)}) copy-start(pred[3,3072]{1,0:T(4,128)(4,1)} %copy-done.13) | copy-start | bytes 27652
  654.6 89.7 %copy-start.19 = (pred[3,3072]{1,0:T(4,128)(4,1)S(1)}, pred[3,3072]{1,0:T(4,128)(4,1)}, u32[]{:S(2)}) copy-start(pred[3,3072]{1,0:T(4,128)(4,1)} %get-tuple-element.95) | copy-start | bytes 27652
  753.5 143.1 %all-to-all-start.2 = ((bf16[3,16,192,128]{3,2,0,1:T(8,128)(2,1)}), bf16[3,16,192,128]{3,2,0,1:T(8,128)(2,1)}, u32[]{:S(2)}, u32[]{:S(2)}) async-start(bf16[3,16,192,128]{3,2,0,1:T(8,128)(2,1)} %copy.136), calls=%async_computation.2 | async-start | bytes 4718592 | tf_op jit(solution)/shard_map/all_to_all | solution.py:120
  896.6 97.6 %all-to-all-start.6 = ((bf16[3,16,4,128,128]{4,3,2,0,1:T(8,128)(2,1)}), bf16[3,16,4,128,128]{4,3,2,0,1:T(8,128)(2,1)}, u32[]{:S(2)}, u32[]{:S(2)}) async-start(bf16[3,16,4,128,128]{4,3,2,0,1:T(8,128)(2,1)} %copy.152), calls=%async_computation.6 | async-start | bytes 12582912 | tf_op jit(solution)/shard_map/all_to_all | solution.py:178
  909.5 89.4 %copy-start.16 = (s32[3,256,16]{1,2,0:T(8,128)S(1)}, s32[3,256,16]{1,2,0:T(8,128)}, u32[]{:S(2)}) copy-start(s32[3,256,16]{1,2,0:T(8,128)} %param.19) | copy-start | bytes 147460
  994.2 166.1 %all-to-all-start.9 = ((bf16[3,16,4,128,128]{4,3,2,0,1:T(8,128)(2,1)}), bf16[3,16,4,128,128]{4,3,2,0,1:T(8,128)(2,1)}, u32[]{:S(2)}, u32[]{:S(2)}) async-start(bf16[3,16,4,128,128]{4,3,2,0,1:T(8,128)(2,1)} %copy.160), calls=%async_computation.9 | async-start | bytes 12582912 | tf_op jit(solution)/shard_map/all_to_all | solution.py:179
  1212.2 10.7 copy-start.3
  1273.0 10.7 copy-start.3
  1333.7 10.7 copy-start.3
  1350.9 89.8 %copy-start.22 = (pred[3,3072]{1,0:T(4,128)(4,1)S(1)}, pred[3,3072]{1,0:T(4,128)(4,1)}, u32[]{:S(2)}) copy-start(pred[3,3072]{1,0:T(4,128)(4,1)} %compare_and_fusion) | copy-start | bytes 27652
  1447.2 7.0 copy-start.1
  1447.2 7.0 copy-start.10
  1447.2 34.5 %all-to-all-start.10 = ((bf16[3,16,192,128]{3,2,0,1:T(8,128)(2,1)}), bf16[3,16,192,128]{3,2,0,1:T(8,128)(2,1)}, u32[]{:S(2)}, u32[]{:S(2)}) async-start(bf16[3,16,192,128]{3,2,0,1:T(8,128)(2,1)} %copy.164), calls=%async_computation.10 | async-start | bytes 4718592 | tf_op jit(solution)/shard_map/all_to_all | solution.py:187
where the time goes:
time: 1590 us; the launch traced here: 1580 us
  local copies, waits for them, and re-layouts  1080 us (68%)
  waiting for transfers between devices  156 us (10%)
  other arithmetic  154 us (10%)
  matrix products  90.9 us (6%)
  starting transfers between devices  64.4 us (4%)
  blocking collectives  30.6 us (2%)
    gather x19, local copies, waits for them, and re-layouts, take_rows(): return jnp.take(matrix, indices, axis=0)  799 us
    unnamed x68, local copies, waits for them, and re-layouts  124 us
    all_to_all x1, waiting for transfers between devices, per_device(): lax.all_to_all(key_send, 'seq', split_axis=1, concat_axis=1, tiled=True)  84.7 us
    another operation x12, other arithmetic  83.2 us
    dot_general x3, matrix products, attend(): jnp.einsum('gqd,gkd->gqk', query_blocks, key_used, preferred_element_type...  34.3 us
  transfers between devices with their start and end apart: 11, of which 6 were waited for; matrix products, arithmetic and copies ran while one was open for 53% of the time, Pallas kernels for 0%

commit v1 on v0

v1 whole, which is shorter than its diff:
```python
import functools
import math

import jax
import jax.numpy as jnp
from jax import lax
from jax.experimental import pallas as pl
from jax.experimental.pallas import tpu as pltpu
from jax.sharding import PartitionSpec as P

BLOCK = 128
PAIRS = 16
KCAP = 4
LANES = 128
META = 16
VMEM_LIMIT = 56 * 1024 * 1024
BF16 = jnp.bfloat16
F32 = jnp.float32
I32 = jnp.int32


def dot(left, right):
    return jnp.dot(left, right, preferred_element_type=F32)


def iota(shape, dim):
    return lax.broadcasted_iota(I32, shape, dim)


def params():
    return pltpu.CompilerParams(vmem_limit_bytes=VMEM_LIMIT)


def slot_kernel(ids_ref, slot_ref, count_ref, *, groups, owned, capacity):
    clusters = groups * owned
    chunks = ids_ref.shape[1]
    row = iota((clusters, LANES), 0)
    lane = iota((clusters, LANES), 1)
    before = iota((LANES, 2 * LANES), 0)
    after = iota((LANES, 2 * LANES), 1)
    running = ((after >= LANES) | (before <= after)).astype(BF16)
    every = jnp.ones((LANES, LANES), BF16)
    counts = jnp.zeros((clusters, LANES), F32)
    for chunk in range(chunks):
        hit = (ids_ref[0, chunk : chunk + 1, :] == row).astype(BF16)
        counts = counts + dot(hit, every)
    first = iota((clusters, clusters), 0)
    second = iota((clusters, clusters), 1)
    inside = ((second < first) & (second // owned == first // owned)).astype(BF16)
    carry = dot(inside, counts.astype(BF16)) + ((row // owned) * capacity - 1).astype(F32)
    own = jnp.where(lane == row % owned, counts, 0.0).astype(BF16)
    of_group = (iota((groups, clusters), 0) == iota((groups, clusters), 1) // owned).astype(BF16)
    count_ref[0] = dot(of_group, own)
    for chunk in range(chunks):
        match = ids_ref[0, chunk : chunk + 1, :] == row
        sums = dot(match.astype(BF16), running)
        picked = jnp.where(match, sums[:, :LANES] + carry, 0.0)
        slot_ref[0, chunk : chunk + 1, :] = jnp.sum(picked, axis=0, keepdims=True).astype(I32)
        carry = carry + sums[:, LANES:]


def spread(index, rows, store, slots, step):
    flat = jnp.concatenate([index[i : i + 1, :] for i in range(index.shape[0])], axis=1)
    count = flat.shape[1]
    within = iota((step, count), 0)

    def body(i, carry):
        onehot = (flat - i * step == within).astype(BF16)
        store(i, dot(onehot, rows).astype(BF16))
        return carry

    lax.fori_loop(0, slots // step, body, 0)


def collect(index, packed, wide_ref, store, step):
    turned = index.astype(F32).T
    chunks = index.shape[0]
    for i in range(chunks):
        wide_ref[i * LANES : (i + 1) * LANES, :] = jnp.broadcast_to(
            turned[:, i : i + 1], (LANES, LANES)
        ).astype(I32)
    lane = iota((step, LANES), 1)
    tiles = packed.shape[0] // LANES

    def body(i, carry):
        wide = wide_ref[pl.ds(pl.multiple_of(i * step, step), step), :] - lane
        onehot = jnp.concatenate([(wide == t * LANES).astype(BF16) for t in range(tiles)], axis=1)
        store(i, dot(onehot, packed).astype(BF16))
        return carry

    lax.fori_loop(0, chunks * LANES // step, body, 0)


def pack_kv_kernel(slot_ref, key_count_ref, query_count_ref, key_ref, value_ref, out_ref):
    groups, _, rows, _ = out_ref.shape
    capacity = rows - META
    tokens = key_ref.shape[0] * key_ref.shape[2]
    keys = key_ref[:, 0].reshape(tokens, LANES)
    values = value_ref[:, 0].reshape(tokens, LANES)

    def store(i, block):
        out_ref[pl.ds(2 * i, 2), 0, :capacity, :] = block.reshape(2, capacity, 2 * LANES)

    both = jnp.concatenate([keys, values], axis=1)
    spread(slot_ref[0], both, store, groups * capacity, 2 * capacity)
    for group in range(groups):
        key_count = jnp.broadcast_to(key_count_ref[0, group : group + 1, :], (META, LANES))
        query_count = jnp.broadcast_to(query_count_ref[0, group : group + 1, :], (META, LANES))
        out_ref[group, 0, capacity:, :LANES] = key_count.astype(BF16)
        out_ref[group, 0, capacity:, LANES:] = query_count.astype(BF16)


def pack_q_kernel(slot_ref, query_ref, out_ref):
    groups, _, capacity, _ = out_ref.shape
    tokens = query_ref.shape[0] * query_ref.shape[1]

    def store(i, block):
        out_ref[pl.ds(2 * i, 2), 0] = block.reshape(2, capacity, LANES)

    queries = query_ref[...].reshape(tokens, LANES)
    spread(slot_ref[0], queries, store, groups * capacity, 2 * capacity)


def sources(counts, capacity):
    groups = counts.shape[0]
    padded = jnp.concatenate([counts, jnp.zeros((LANES - groups, LANES), F32)], axis=0).astype(BF16)
    row = iota((LANES, LANES), 0)
    col = iota((LANES, LANES), 1)
    below = dot((col < row).astype(BF16), padded)
    offset = dot(padded, (row < col).astype(BF16))
    start = (row * capacity).astype(F32) + offset - below
    below_t = below.T[:groups]
    start_t = start.T[:groups]
    place = iota((groups, LANES), 1).astype(F32)
    found = jnp.broadcast_to(start_t[:, 0:1], (groups, LANES))
    for source in range(1, groups):
        found = jnp.where(below_t[:, source : source + 1] <= place, start_t[:, source : source + 1], found)
    return (found + place).astype(I32)


def unpack_kv_kernel(pick_ref, in_ref, out_ref, query_source_ref, wide_ref, sorted_ref, *, first):
    head = pl.program_id(0) + first
    groups, _, rows, _ = in_ref.shape
    capacity = rows - META
    counts = in_ref[:, 0, capacity:, :].astype(F32)
    counts = jnp.max(counts, axis=1)
    query_source_ref[0] = sources(counts[:, LANES:], capacity)
    packed = in_ref[:, 0, :capacity, :].reshape(groups * capacity, 2 * LANES)

    def store(i, block):
        sorted_ref[pl.ds(4 * i, 4)] = block.reshape(4, BLOCK, 2 * LANES)

    collect(sources(counts[:, :LANES], capacity), packed, wide_ref, store, 4 * BLOCK)

    def copy(i, carry):
        for j in range(KCAP):
            out_ref[i, 0, j] = sorted_ref[pick_ref[head, i, j]]
        return carry

    lax.fori_loop(0, groups, copy, 0)


def unpack_q_kernel(index_ref, in_ref, out_ref, wide_ref):
    groups, _, capacity, _ = in_ref.shape
    packed = in_ref[:, 0].reshape(groups * capacity, LANES)
    step = 4 * BLOCK

    def store(i, block):
        out_ref[0, pl.ds(pl.multiple_of(i * step, step), step), :] = block

    collect(index_ref[0], packed, wide_ref, store, step)


def final_kernel(index_ref, in_ref, out_ref, wide_ref):
    groups, _, capacity, _ = in_ref.shape
    packed = in_ref[:, 0].reshape(groups * capacity, LANES)
    part = out_ref.shape[1]

    def store(i, block):
        out_ref[pl.ds(2 * i, 2)] = block.reshape(2, part, LANES)

    collect(index_ref[0], packed, wide_ref, store, 2 * part)


def attend_kernel(fetch_ref, index_ref, query_ref, recv_ref, out_ref, attended_ref, *, first):
    head = pl.program_id(0) + first
    groups, _, capacity, _ = out_ref.shape
    owned = query_ref.shape[1] // BLOCK
    scale = 1.0 / math.sqrt(LANES)

    def one(cluster):
        rows = pl.ds(pl.multiple_of(cluster * BLOCK, BLOCK), BLOCK)
        queries = query_ref[0, rows, :]
        blocks = []
        for pair in range(PAIRS):
            at = fetch_ref[head, cluster, pair]
            blocks.append((at // KCAP, at % KCAP))
        keys = jnp.concatenate([recv_ref[b, 0, j, :, :LANES] for b, j in blocks], axis=0)
        values = jnp.concatenate([recv_ref[b, 0, j, :, LANES:] for b, j in blocks], axis=0)
        scores = lax.dot_general(
            queries, keys, (((1,), (1,)), ((), ())), preferred_element_type=F32
        )
        scores = scores * scale
        weights = jnp.exp(scores - jnp.max(scores, axis=1, keepdims=True))
        total = jnp.sum(weights, axis=1, keepdims=True)
        mixed = dot(weights.astype(BF16), values)
        attended_ref[rows, :] = (mixed / total).astype(BF16)

    def body(i, carry):
        one(2 * i)
        one(2 * i + 1)
        return carry

    lax.fori_loop(0, owned // 2, body, 0)

    def store(i, block):
        out_ref[pl.ds(2 * i, 2), 0] = block.reshape(2, capacity, LANES)

    spread(index_ref[0], attended_ref[...], store, groups * capacity, 2 * capacity)


def shape_of(shape, dtype):
    return jax.ShapeDtypeStruct(shape, dtype)


def cost(flops, moved, exps=0):
    return pl.CostEstimate(flops=int(flops), bytes_accessed=int(moved), transcendentals=int(exps))


def exchange(array, axis):
    return lax.all_to_all(array, axis, split_axis=0, concat_axis=0, tiled=True)


def tables(cluster_pairs, my_index, groups):
    heads, clusters, _ = cluster_pairs.shape
    owned = clusters // groups
    by_group = cluster_pairs.reshape(heads, groups, owned * PAIRS)
    local = jnp.arange(owned, dtype=I32)
    earlier = (local[:, None] < local[None, :]).astype(F32)
    needed = jnp.any(by_group[:, :, None, :] == (my_index * owned + local)[None, None, :, None], axis=3)
    order = jnp.einsum("hac,cd->had", needed.astype(F32), earlier).astype(I32)
    hits = needed[:, :, None, :] & (order[:, :, None, :] == jnp.arange(KCAP, dtype=I32)[:, None])
    pick = jnp.sum(jnp.where(hits, local, 0), axis=3)
    own = lax.dynamic_index_in_dim(by_group, my_index, 1, keepdims=False)
    every = jnp.arange(clusters, dtype=I32)
    same = own[:, :, None] == every
    wanted = jnp.any(same, axis=1).reshape(heads, groups, owned)
    rank = jnp.einsum("hac,cd->had", wanted.astype(F32), earlier).astype(I32)
    position = (rank + jnp.arange(groups, dtype=I32)[None, :, None] * KCAP).reshape(heads, 1, clusters)
    fetch = jnp.sum(jnp.where(same, position, 0), axis=2)
    return pick, fetch.reshape(heads, owned, PAIRS)


def per_device(query_rows, key_rows, value_rows, query_cluster, key_cluster, cluster_pairs):
    heads, tokens = query_cluster.shape
    groups = lax.axis_size("seq")
    parts = lax.axis_size("head")
    my_index = lax.axis_index("seq")
    clusters = cluster_pairs.shape[1]
    owned = clusters // groups
    capacity = 3 * tokens // (2 * groups)
    slots = groups * capacity
    part = tokens // parts
    width = heads * LANES
    chunks = tokens // LANES

    def by_part(rows):
        return rows.reshape(part, parts, width).transpose(1, 0, 2)

    kv_sent = jnp.stack([by_part(key_rows), by_part(value_rows)], axis=1)
    kv_tok = exchange(kv_sent, "head")
    q_tok = exchange(by_part(query_rows), "head")

    ids = jnp.concatenate([query_cluster, key_cluster], axis=0).reshape(2 * heads, chunks, LANES)
    slot, count = pl.pallas_call(
        functools.partial(slot_kernel, groups=groups, owned=owned, capacity=capacity),
        grid=(2 * heads,),
        in_specs=[pl.BlockSpec((1, chunks, LANES), lambda h: (h, 0, 0))],
        out_specs=[
            pl.BlockSpec((1, chunks, LANES), lambda h: (h, 0, 0)),
            pl.BlockSpec((1, groups, LANES), lambda h: (h, 0, 0)),
        ],
        out_shape=[
            shape_of((2 * heads, chunks, LANES), I32),
            shape_of((2 * heads, groups, LANES), F32),
        ],
        compiler_params=params(),
        cost_estimate=cost(2e9 * heads, 1e6),
        name="slots",
    )(ids)
    pick, fetch = tables(cluster_pairs, my_index, groups)

    kv_packed = pl.pallas_call(
        pack_kv_kernel,
        grid=(heads,),
        in_specs=[
            pl.BlockSpec((1, chunks, LANES), lambda h: (h + heads, 0, 0)),
            pl.BlockSpec((1, groups, LANES), lambda h: (h + heads, 0, 0)),
            pl.BlockSpec((1, groups, LANES), lambda h: (h, 0, 0)),
            pl.BlockSpec((parts, 1, part, LANES), lambda h: (0, 0, 0, h)),
            pl.BlockSpec((parts, 1, part, LANES), lambda h: (0, 1, 0, h)),
        ],
        out_specs=pl.BlockSpec((groups, 1, capacity + META, 2 * LANES), lambda h: (0, h, 0, 0)),
        out_shape=shape_of((groups, heads, capacity + META, 2 * LANES), BF16),
        compiler_params=params(),
        cost_estimate=cost(heads * 4.0 * slots * tokens * LANES, 8e6),
        name="pack_kv",
    )(slot, count, count, kv_tok, kv_tok)
    kv_recv = exchange(kv_packed, "seq")

    q_packed = pl.pallas_call(
        pack_q_kernel,
        grid=(heads,),
        in_specs=[
            pl.BlockSpec((1, chunks, LANES), lambda h: (h, 0, 0)),
            pl.BlockSpec((parts, part, LANES), lambda h: (0, 0, h)),
        ],
        out_specs=pl.BlockSpec((groups, 1, capacity, LANES), lambda h: (0, h, 0, 0)),
        out_shape=shape_of((groups, heads, capacity, LANES), BF16),
        compiler_params=params(),
        cost_estimate=cost(heads * 4.0 * slots * tokens * LANES, 4e6),
        name="pack_q",
    )(slot, q_tok)
    q_recv = exchange(q_packed, "seq")

    def unpack_kv(first, count_heads):
        return pl.pallas_call(
            functools.partial(unpack_kv_kernel, first=first),
            grid_spec=pltpu.PrefetchScalarGridSpec(
                num_scalar_prefetch=1,
                grid=(count_heads,),
                in_specs=[
                    pl.BlockSpec(
                        (groups, 1, capacity + META, 2 * LANES), lambda h, pick: (0, h + first, 0, 0)
                    ),
                ],
                out_specs=[
                    pl.BlockSpec(
                        (groups, 1, KCAP, BLOCK, 2 * LANES), lambda h, pick: (0, h, 0, 0, 0)
                    ),
                    pl.BlockSpec((1, owned, BLOCK), lambda h, pick: (h, 0, 0)),
                ],
                scratch_shapes=[
                    pltpu.VMEM((owned * BLOCK, LANES), I32),
                    pltpu.VMEM((owned, BLOCK, 2 * LANES), BF16),
                ],
            ),
            out_shape=[
                shape_of((groups, count_heads, KCAP, BLOCK, 2 * LANES), BF16),
                shape_of((count_heads, owned, BLOCK), I32),
            ],
            compiler_params=params(),
            cost_estimate=cost(count_heads * 4.0 * slots * tokens * LANES, count_heads * 6e6),
            name=f"unpack_kv_{first}",
        )(pick, kv_recv)

    splits = ((0, 1), (1, heads - 1))
    received = []
    indices = []
    for first, count_heads in splits:
        sent, index = unpack_kv(first, count_heads)
        indices.append(index)
        received.append(exchange(sent, "seq"))
    index = jnp.concatenate(indices, axis=0)

    q_sorted = pl.pallas_call(
        unpack_q_kernel,
        grid=(heads,),
        in_specs=[
            pl.BlockSpec((1, owned, BLOCK), lambda h: (h, 0, 0)),
            pl.BlockSpec((groups, 1, capacity, LANES), lambda h: (0, h, 0, 0)),
        ],
        out_specs=pl.BlockSpec((1, owned * BLOCK, LANES), lambda h: (h, 0, 0)),
        out_shape=shape_of((heads, owned * BLOCK, LANES), BF16),
        scratch_shapes=[pltpu.VMEM((owned * BLOCK, LANES), I32)],
        compiler_params=params(),
        cost_estimate=cost(heads * 4.0 * slots * tokens * LANES, 4e6),
        name="unpack_q",
    )(index, q_recv)

    replies = []
    for (first, count_heads), recv in zip(splits, received, strict=True):
        replies.append(
            pl.pallas_call(
                functools.partial(attend_kernel, first=first),
                grid_spec=pltpu.PrefetchScalarGridSpec(
                    num_scalar_prefetch=1,
                    grid=(count_heads,),
                    in_specs=[
                        pl.BlockSpec((1, owned, BLOCK), lambda h, fetch, first=first: (h + first, 0, 0)),
                        pl.BlockSpec(
                            (1, owned * BLOCK, LANES), lambda h, fetch, first=first: (h + first, 0, 0)
                        ),
                        pl.BlockSpec(
                            (groups, 1, KCAP, BLOCK, 2 * LANES), lambda h, fetch: (0, h, 0, 0, 0)
                        ),
                    ],
                    out_specs=pl.BlockSpec(
                        (groups, 1, capacity, LANES), lambda h, fetch: (0, h, 0, 0)
                    ),
                    scratch_shapes=[pltpu.VMEM((owned * BLOCK, LANES), BF16)],
                ),
                out_shape=shape_of((groups, count_heads, capacity, LANES), BF16),
                compiler_params=params(),
                cost_estimate=cost(
                    count_heads * 4.0 * owned * BLOCK * PAIRS * BLOCK * LANES,
                    count_heads * 6e6,
                    count_heads * owned * BLOCK * PAIRS * BLOCK,
                ),
                name=f"attend_{first}",
            )(fetch, index, q_sorted, recv)
        )
    reply = jnp.concatenate(replies, axis=1)
    returned = exchange(reply, "seq")
    token_rows = pl.pallas_call(
        final_kernel,
        grid=(heads,),
        in_specs=[
            pl.BlockSpec((1, chunks, LANES), lambda h: (h, 0, 0)),
            pl.BlockSpec((groups, 1, capacity, LANES), lambda h: (0, h, 0, 0)),
        ],
        out_specs=pl.BlockSpec((parts, part, LANES), lambda h: (0, 0, h)),
        out_shape=shape_of((parts, part, width), BF16),
        scratch_shapes=[pltpu.VMEM((tokens, LANES), I32)],
        compiler_params=params(),
        cost_estimate=cost(heads * 4.0 * slots * tokens * LANES, 4e6),
        name="final",
    )(slot, returned)
    rows = exchange(token_rows, "head")
    return rows.transpose(1, 0, 2).reshape(part, parts * width)


def solution(mesh):
    in_specs = (
        P(("seq", "head"), None),
        P(("seq", "head"), None),
        P(("seq", "head"), None),
        P("head", "seq"),
        P("head", "seq"),
        P("head", None, None),
    )
    out_specs = P(("seq", "head"), None)
    return jax.shard_map(
        per_device, mesh=mesh, in_specs=in_specs, out_specs=out_specs, check_vma=False
    )
```

time: 1590 us -> 516 us (0.32)
  local copies, waits for them, and re-layouts: 1080 us -> 16.4 us
  Pallas kernels: 0 us -> 156 us
  other arithmetic: 154 us -> 6.81 us
  matrix products: 90.9 us -> 0.2 us
  waiting for transfers between devices: 156 us -> 240 us
  blocking collectives: 30.6 us -> 62.6 us
  starting transfers between devices: 64.4 us -> 32.9 us
    gather x20 -> x0, local copies, waits for them, and re-layouts: 806 us -> none  [the longest x19 799 us: take_rows(): return jnp.take(matrix, indices, axis=0)]
    pallas_call x0 -> x9, Pallas kernels: none -> 156 us  [the longest x2 55.3 us: per_device(): pl.pallas_call(functools.partial(attend_kernel, first=first), grid_spec=p...]
    unnamed x68 -> x27, local copies, waits for them, and re-layouts: 124 us -> 8.11 us
    dot_general x14 -> x2, matrix products: 90.9 us -> 0.2 us  [the longest x1 0.13 us: tables(): order = jnp.einsum('hac,cd->had', needed.astype(F32), earlier).astype(I32)]
    all_to_all x11 -> x6, waiting for transfers between devices: 156 us -> 240 us  [exchange(): return lax.all_to_all(array, axis, split_axis=0, concat_axis=0, tiled=True)]
    another operation x14 -> x1, other arithmetic: 84.3 us -> 3.39 us  [per_device(): kv_sent = jnp.stack([by_part(key_rows), by_part(value_rows)], axis=1)]
    convert_element_type x9 -> x0, local copies, waits for them, and re-layouts: 63.3 us -> none  [the longest x3 27.3 us: attend(): value_used = jnp.einsum('gpr,rbd->gpbd', selector, value_recv, preferred_...]
    select_n x14 -> x0, other arithmetic: 37 us -> none  [the longest x4 28.2 us: pull_rows(): return jnp.where(is_valid[..., None], picked, jnp.zeros((), rows.dtype))]
  transfers between devices with their start and end apart: 11 -> 6, of which waited for: 6 -> 5; matrix products, arithmetic and copies ran while one was open for 53% -> 1% of each run, Pallas kernels for 0% -> 20%
where the time goes in v1:
time: 516 us; the launch traced here: 515 us
  waiting for transfers between devices  240 us (47%)
  Pallas kernels  156 us (30%)
  blocking collectives  62.6 us (12%)
  starting transfers between devices  32.9 us (6%)
  local copies, waits for them, and re-layouts  16.4 us (3%)
  other arithmetic  6.81 us (1%)
    all_to_all x6, waiting for transfers between devices, exchange(): return lax.all_to_all(array, axis, split_axis=0, concat_axis=0, tiled=True)  240 us
    all_to_all x2, blocking collectives, exchange(): return lax.all_to_all(array, axis, split_axis=0, concat_axis=0, tiled=True)  62.6 us
    pallas_call x2, Pallas kernels, per_device(): pl.pallas_call(functools.partial(attend_kernel, first=first), grid_spec=p...  55.3 us
    all_to_all x6, starting transfers between devices, exchange(): return lax.all_to_all(array, axis, split_axis=0, concat_axis=0, tiled=True)  32.9 us
    pallas_call x2, Pallas kernels, unpack_kv(): pl.pallas_call(functools.partial(unpack_kv_kernel, first=first), grid_spe...  25.1 us
    pallas_call x1, Pallas kernels, per_device(): pl.pallas_call(pack_kv_kernel, grid=(heads,), in_specs=[pl.BlockSpec((1,...  16.7 us
    pallas_call x1, Pallas kernels, per_device(): pl.pallas_call(pack_q_kernel, grid=(heads,), in_specs=[pl.BlockSpec((1, c...  16.1 us
    pallas_call x1, Pallas kernels, per_device(): pl.pallas_call(final_kernel, grid=(heads,), in_specs=[pl.BlockSpec((1, ch...  15.5 us
  transfers between devices with their start and end apart: 6, of which 5 were waited for; matrix products, arithmetic and copies ran while one was open for 1% of the time, Pallas kernels for 20%

profile of v1, /device:TPU:1, one launch (start us, length us, event | category | flops | bytes accessed | tf_op | source)
XLA Modules:
  0.0 515.0 jit_solution(2384015485887781841)
XLA Ops:
  0.0 1.7 copy.17
  1.7 0.9 copy.18
  2.6 1.7 copy.19
  4.3 1.6 copy.20
  5.9 3.4 pad_maximum_fusion
  9.3 0.0 copy-start.5
  9.3 0.0 copy-start.6
  9.3 0.0 copy-start.1
  9.3 5.9 %all-to-all-start = ((bf16[8,2,256,384]{3,2,1,0:T(8,128)(2,1)}), bf16[8,2,256,384]{3,2,1,0:T(8,128)(2,1)}, u32[]{:S(2)}, u32[]{:S(2)}) async-start(bf16[8,2,256,384]{3,2,1,0:T(8,128)(2,1)} %pad_maximum_fusion), calls=%async_computation | async-start | bytes 6291456 | tf_op jit(solution)/shard_map/all_to_all | solution.py:231
  15.2 0.0 copy-done.5
  15.2 0.0 copy-done.6
  15.2 0.6 copy.31
  15.8 0.0 copy-done.1
  15.9 0.7 copy.23
  16.5 1.6 copy.24
  18.1 34.7 %all-to-all-done.key_ref.value_ref = bf16[8,2,256,384]{3,2,1,0:T(8,128)(2,1)} async-done(((bf16[8,2,256,384]{3,2,1,0:T(8,128)(2,1)}), bf16[8,2,256,384]{3,2,1,0:T(8,128)(2,1)}, u32[]{:S(2)}, u32[]{:S(2)}) %all-to-all-start) | async-done | bytes 3145760 | tf_op jit(solution)/shard_map/all_to_all | solution.py:231
  52.9 4.4 all-to-all-start.2
  57.2 11.5 %slots.1 = (s32[6,16,128]{2,1,0:T(8,128)}, f32[6,16,128]{2,1,0:T(8,128)}) custom-call(s32[6,16,128]{2,1,0:T(8,128)} %bitcast.33), custom_call_target="tpu_custom_call" | custom-call | flops 6000000000 | bytes 1000000 | tf_op jit(solution)/shard_map/slots/pallas_call | solution.py:275
  68.7 16.7 %pack_kv.1 = bf16[16,3,208,256]{3,2,1,0:T(8,128)(2,1)} custom-call(s32[6,16,128]{2,1,0:T(8,128)} %get-tuple-element.11.slot_ref.index_ref, f32[6,16,128]{2,1,0:T(8,128)} %get-tuple-element.12.key_count_ref.query_count_ref, f32[6,16,128]{2,1,0:T(8,128)} %get-tuple-element.12.key_count_ref.query_count_ref, ...), custom_call_target="tpu_custom_call" | custom-call | flops 9663676416 | bytes 8000000 | tf_op jit(solution)/shard_map/pack_kv/pallas_call | solution.py:293
  85.3 0.0 all-to-all-done.2.query_ref
  85.4 0.0 copy-start.2
  85.4 1.1 copy-done.2
  86.5 7.9 %all-to-all-start.1 = ((bf16[16,3,208,256]{3,2,1,0:T(8,128)(2,1)}), bf16[16,3,208,256]{3,2,1,0:T(8,128)(2,1)}, u32[]{:S(2)}, u32[]{:S(2)}) async-start(bf16[16,3,208,256]{3,2,1,0:T(8,128)(2,1)} %pack_kv.1), calls=%async_computation.1 | async-start | bytes 10223616 | tf_op jit(solution)/shard_map/all_to_all | solution.py:231
  94.4 16.1 %pack_q.1 = bf16[16,3,192,128]{3,2,1,0:T(8,128)(2,1)} custom-call(s32[6,16,128]{2,1,0:T(8,128)} %get-tuple-element.11.slot_ref.index_ref, bf16[8,256,384]{2,1,0:T(8,128)(2,1)} %copy-done.2), custom_call_target="tpu_custom_call" | custom-call | flops 9663676416 | bytes 4000000 | tf_op jit(solution)/shard_map/pack_q/pallas_call | solution.py:311
  110.4 0.0 copy-start.4
  110.4 60.5 %all-to-all-done.1.in_ref = bf16[16,3,208,256]{3,2,1,0:T(8,128)(2,1)} async-done(((bf16[16,3,208,256]{3,2,1,0:T(8,128)(2,1)}), bf16[16,3,208,256]{3,2,1,0:T(8,128)(2,1)}, u32[]{:S(2)}, u32[]{:S(2)}) %all-to-all-start.1) | async-done | bytes 5111840 | tf_op jit(solution)/shard_map/all_to_all | solution.py:231
  170.9 4.7 all-to-all-start.3
  175.6 0.0 copy-done.4
  175.6 0.2 copy.16
  175.8 0.2 reshape.41
  176.0 1.0 compare_reduce_fusion
  177.0 0.1 convolution_convert_fusion
  177.1 0.3 select_reduce_fusion.1
  177.4 0.7 copy.21.pick_ref
  178.1 9.9 %unpack_kv_0.1 = (bf16[16,1,4,128,256]{4,3,2,1,0:T(8,128)(2,1)}, s32[1,16,128]{2,1,0:T(8,128)}) custom-call(s32[3,16,4]{2,1,0:T(8,128)} %copy.21.pick_ref, bf16[16,3,208,256]{3,2,1,0:T(8,128)(2,1)} %all-to-all-done.1.in_ref), custom_call_target="tpu_custom_call" | custom-call | flops 3221225472 | bytes 6000000 | tf_op jit(solution)/shard_map/unpack_kv_0/pallas_call | solution.py:327
  188.0 20.4 %all-to-all-done.3.in_ref = bf16[16,3,192,128]{3,2,1,0:T(8,128)(2,1)S(1)} async-done(((bf16[16,3,192,128]{3,2,1,0:T(8,128)(2,1)}), bf16[16,3,192,128]{3,2,1,0:T(8,128)(2,1)S(1)}, u32[]{:S(2)}, u32[]{:S(2)}) %all-to-all-start.3) | async-done | bytes 2359328 | tf_op jit(solution)/shard_map/all_to_all | solution.py:231
  208.4 1.5 copy-done
  209.8 5.0 all-to-all-start.4
  214.8 15.3 %unpack_kv_1.1 = (bf16[16,2,4,128,256]{4,3,2,1,0:T(8,128)(2,1)}, s32[2,16,128]{2,1,0:T(8,128)}) custom-call(s32[3,16,4]{2,1,0:T(8,128)} %copy.21.pick_ref, bf16[16,3,208,256]{3,2,1,0:T(8,128)(2,1)} %all-to-all-done.1.in_ref), custom_call_target="tpu_custom_call" | custom-call | flops 6442450944 | bytes 12000000 | tf_op jit(solution)/shard_map/unpack_kv_1/pallas_call | solution.py:327
  230.1 43.8 %all-to-all-done.4.recv_ref = bf16[16,1,4,128,256]{4,3,2,1,0:T(8,128)(2,1)} async-done(((bf16[16,1,4,128,256]{4,3,2,1,0:T(8,128)(2,1)}), bf16[16,1,4,128,256]{4,3,2,1,0:T(8,128)(2,1)}, u32[]{:S(2)}, u32[]{:S(2)}) %all-to-all-start.4) | async-done | bytes 4194336 | tf_op jit(solution)/shard_map/all_to_all | solution.py:231
  273.9 0.0 copy-start.7
  273.9 5.1 all-to-all-start.5
  279.0 0.2 fusion.1
  279.2 0.1 reshape.42
  279.3 0.1 fusion
  279.4 0.1 broadcast_in_dim.30
  279.5 0.3 select_reduce_fusion
  279.9 0.7 reshape.43.fetch_ref
  280.6 0.0 copy-done.8
  280.6 0.0 copy-done.7
  280.6 0.0 copy-start.9
  280.6 0.6 copy-done.9
  281.2 15.5 %unpack_q.1.query_ref = bf16[3,2048,128]{2,1,0:T(8,128)(2,1)} custom-call(s32[3,16,128]{2,1,0:T(8,128)} %copy-done.9, bf16[16,3,192,128]{3,2,1,0:T(8,128)(2,1)} %copy-done), custom_call_target="tpu_custom_call" | custom-call | flops 9663676416 | bytes 4000000 | tf_op jit(solution)/shard_map/unpack_q/pallas_call | solution.py:366
  296.6 20.1 %attend_0.1 = bf16[16,1,192,128]{3,2,1,0:T(8,128)(2,1)} custom-call(s32[3,16,16]{2,1,0:T(8,128)} %reshape.43.fetch_ref, s32[3,16,128]{2,1,0:T(8,128)} %copy-done.9, bf16[3,2048,128]{2,1,0:T(8,128)(2,1)} %unpack_q.1.query_ref, bf16[16,1,4,128,256]{4,3,2,1,0:T(8,128)(2,1)} %all-to-all-done.4.recv_ref), custom_call_target="tpu_custom_call" | custom-call | flops 2147483648 | bytes 6000000 | tf_op jit(solution)/shard_map/attend_0/pallas_call | solution.py:384
  316.7 0.0 copy-start.3
  316.7 80.9 %all-to-all-done.5.recv_ref = bf16[16,2,4,128,256]{4,3,2,1,0:T(8,128)(2,1)} async-done(((bf16[16,2,4,128,256]{4,3,2,1,0:T(8,128)(2,1)}), bf16[16,2,4,128,256]{4,3,2,1,0:T(8,128)(2,1)}, u32[]{:S(2)}, u32[]{:S(2)}) %all-to-all-start.5) | async-done | bytes 8388640 | tf_op jit(solution)/shard_map/all_to_all | solution.py:231
  397.6 35.2 %attend_1.1 = bf16[16,2,192,128]{3,2,1,0:T(8,128)(2,1)} custom-call(s32[3,16,16]{2,1,0:T(8,128)} %reshape.43.fetch_ref, s32[3,16,128]{2,1,0:T(8,128)} %copy-done.9, bf16[3,2048,128]{2,1,0:T(8,128)(2,1)} %unpack_q.1.query_ref, bf16[16,2,4,128,256]{4,3,2,1,0:T(8,128)(2,1)} %all-to-all-done.5.recv_ref), custom_call_target="tpu_custom_call" | custom-call | flops 4294967296 | bytes 12000000 | tf_op jit(solution)/shard_map/attend_1/pallas_call | solution.py:384
  432.8 0.0 copy-done.3
  432.9 1.6 pad_maximum_fusion.1
  434.5 31.6 %all_to_all.40.in_ref = bf16[16,3,192,128]{3,2,1,0:T(8,128)(2,1)} all-to-all(bf16[16,3,192,128]{3,2,1,0:T(8,128)(2,1)S(1)} %pad_maximum_fusion.1), channel_id=1, replica_groups=mesh['seq'=16,'head'=8] {'seq'}, dimensions={0} | all-to-all | bytes 4718592 | tf_op jit(solution)/shard_map/all_to_all | solution.py:231
  466.0 15.5 %final.1 = bf16[8,256,384]{2,1,0:T(8,128)(2,1)} custom-call(s32[6,16,128]{2,1,0:T(8,128)} %get-tuple-element.11.slot_ref.index_ref, bf16[16,3,192,128]{3,2,1,0:T(8,128)(2,1)} %all_to_all.40.in_ref), custom_call_target="tpu_custom_call" | custom-call | flops 9663676416 | bytes 4000000 | tf_op jit(solution)/shard_map/final/pallas_call | solution.py:415
  481.5 31.0 %all_to_all.41 = bf16[8,256,384]{2,1,0:T(8,128)(2,1)S(1)} all-to-all(bf16[8,256,384]{2,1,0:T(8,128)(2,1)} %final.1), channel_id=1, replica_groups=mesh['seq'=16,'head'=8] {'head'}, dimensions={0} | all-to-all | bytes 3145728 | tf_op jit(solution)/shard_map/all_to_all | solution.py:231
  512.5 0.7 copy.25
  513.3 1.7 copy.26
  (9 shorter events, 0.0 us)
Async XLA Ops:
  9.3 5.9 %copy-start.5 = (s32[3,2048]{1,0:T(4,128)S(1)}, s32[3,2048]{1,0:T(4,128)}, u32[]{:S(2)}) copy-start(s32[3,2048]{1,0:T(4,128)} %param.10) | copy-start | bytes 73732
  9.3 5.9 %copy-start.6 = (s32[3,2048]{1,0:T(4,128)S(1)}, s32[3,2048]{1,0:T(4,128)}, u32[]{:S(2)}) copy-start(s32[3,2048]{1,0:T(4,128)} %param.9) | copy-start | bytes 73732
  9.3 6.6 %copy-start.1 = (bf16[256,3072]{1,0:T(8,128)(2,1)S(1)}, bf16[256,3072]{1,0:T(8,128)(2,1)}, u32[]{:S(2)}) copy-start(bf16[256,3072]{1,0:T(8,128)(2,1)} %param.6) | copy-start | bytes 4718596
  9.3 43.6 %all-to-all-start = ((bf16[8,2,256,384]{3,2,1,0:T(8,128)(2,1)}), bf16[8,2,256,384]{3,2,1,0:T(8,128)(2,1)}, u32[]{:S(2)}, u32[]{:S(2)}) async-start(bf16[8,2,256,384]{3,2,1,0:T(8,128)(2,1)} %pad_maximum_fusion), calls=%async_computation | async-start | bytes 6291456 | tf_op jit(solution)/shard_map/all_to_all | solution.py:231
  52.9 32.5 %all-to-all-start.2 = ((bf16[8,256,384]{2,1,0:T(8,128)(2,1)}), bf16[8,256,384]{2,1,0:T(8,128)(2,1)S(1)}, u32[]{:S(2)}, u32[]{:S(2)}) async-start(bf16[8,256,384]{2,1,0:T(8,128)(2,1)} %bitcast.8), calls=%async_computation.2 | async-start | bytes 3145728 | tf_op jit(solution)/shard_map/all_to_all | solution.py:231
  85.4 1.1 copy-start.2
  86.5 84.4 %all-to-all-start.1 = ((bf16[16,3,208,256]{3,2,1,0:T(8,128)(2,1)}), bf16[16,3,208,256]{3,2,1,0:T(8,128)(2,1)}, u32[]{:S(2)}, u32[]{:S(2)}) async-start(bf16[16,3,208,256]{3,2,1,0:T(8,128)(2,1)} %pack_kv.1), calls=%async_computation.1 | async-start | bytes 10223616 | tf_op jit(solution)/shard_map/all_to_all | solution.py:231
  110.4 65.2 %copy-start.4 = (s32[3,256,16]{1,2,0:T(8,128)S(1)}, s32[3,256,16]{1,2,0:T(8,128)}, u32[]{:S(2)}) copy-start(s32[3,256,16]{1,2,0:T(8,128)} %param.11) | copy-start | bytes 147460
  170.9 37.4 %all-to-all-start.3 = ((bf16[16,3,192,128]{3,2,1,0:T(8,128)(2,1)}), bf16[16,3,192,128]{3,2,1,0:T(8,128)(2,1)S(1)}, u32[]{:S(2)}, u32[]{:S(2)}) async-start(bf16[16,3,192,128]{3,2,1,0:T(8,128)(2,1)} %pack_q.1), calls=%async_computation.3 | async-start | bytes 4718592 | tf_op jit(solution)/shard_map/all_to_all | solution.py:231
  208.4 1.5 copy-start
  209.8 64.1 %all-to-all-start.4 = ((bf16[16,1,4,128,256]{4,3,2,1,0:T(8,128)(2,1)}), bf16[16,1,4,128,256]{4,3,2,1,0:T(8,128)(2,1)}, u32[]{:S(2)}, u32[]{:S(2)}) async-start(bf16[16,1,4,128,256]{4,3,2,1,0:T(8,128)(2,1)} %get-tuple-element.15), calls=%async_computation.4 | async-start | bytes 8388608 | tf_op jit(solution)/shard_map/all_to_all | solution.py:231
  273.9 6.7 %copy-start.8 = (s32[1,16,128]{2,1,0:T(8,128)S(1)}, s32[1,16,128]{2,1,0:T(8,128)}, u32[]{:S(2)}) copy-start(s32[1,16,128]{2,1,0:T(8,128)} %get-tuple-element.13) | copy-start | bytes 24580
  273.9 6.7 %copy-start.7 = (s32[2,16,128]{2,1,0:T(8,128)S(1)}, s32[2,16,128]{2,1,0:T(8,128)}, u32[]{:S(2)}) copy-start(s32[2,16,128]{2,1,0:T(8,128)} %get-tuple-element.14) | copy-start | bytes 49156
  273.9 123.7 %all-to-all-start.5 = ((bf16[16,2,4,128,256]{4,3,2,1,0:T(8,128)(2,1)}), bf16[16,2,4,128,256]{4,3,2,1,0:T(8,128)(2,1)}, u32[]{:S(2)}, u32[]{:S(2)}) async-start(bf16[16,2,4,128,256]{4,3,2,1,0:T(8,128)(2,1)} %get-tuple-element.16), calls=%async_computation.5 | async-start | bytes 16777216 | tf_op jit(solution)/shard_map/all_to_all | solution.py:231
  280.6 0.6 copy-start.9
  316.7 116.1 %copy-start.3 = (bf16[16,1,192,128]{3,2,1,0:T(8,128)(2,1)S(1)}, bf16[16,1,192,128]{3,2,1,0:T(8,128)(2,1)}, u32[]{:S(2)}) copy-start(bf16[16,1,192,128]{3,2,1,0:T(8,128)(2,1)} %attend_0.1) | copy-start | bytes 2359300

commit v2 on v1

--- a/solution.py
+++ b/solution.py
@@ -91,6 +91,11 @@
     lax.fori_loop(0, chunks * LANES // step, body, 0)
 
 
+def split_kernel(key_ref, value_ref, out_ref):
+    out_ref[0, 0] = key_ref[...]
+    out_ref[0, 1] = value_ref[...]
+
+
 def pack_kv_kernel(slot_ref, key_count_ref, query_count_ref, key_ref, value_ref, out_ref):
     groups, _, rows, _ = out_ref.shape
     capacity = rows - META
@@ -171,7 +176,8 @@
     collect(index_ref[0], packed, wide_ref, store, step)
 
 
-def final_kernel(index_ref, in_ref, out_ref, wide_ref):
+def final_kernel(index_ref, in_ref, *refs):
+    out_ref, wide_ref = refs[-2:]
     groups, _, capacity, _ = in_ref.shape
     packed = in_ref[:, 0].reshape(groups * capacity, LANES)
     part = out_ref.shape[1]
@@ -186,7 +192,7 @@
     head = pl.program_id(0) + first
     groups, _, capacity, _ = out_ref.shape
     owned = query_ref.shape[1] // BLOCK
-    scale = 1.0 / math.sqrt(LANES)
+    scale = math.log2(math.e) / math.sqrt(LANES)
 
     def one(cluster):
         rows = pl.ds(pl.multiple_of(cluster * BLOCK, BLOCK), BLOCK)
@@ -200,18 +206,17 @@
         scores = lax.dot_general(
             queries, keys, (((1,), (1,)), ((), ())), preferred_element_type=F32
         )
-        scores = scores * scale
-        weights = jnp.exp(scores - jnp.max(scores, axis=1, keepdims=True))
+        weights = jnp.exp2((scores - jnp.max(scores, axis=1, keepdims=True)) * scale)
         total = jnp.sum(weights, axis=1, keepdims=True)
         mixed = dot(weights.astype(BF16), values)
         attended_ref[rows, :] = (mixed / total).astype(BF16)
 
     def body(i, carry):
-        one(2 * i)
-        one(2 * i + 1)
+        for j in range(4):
+            one(4 * i + j)
         return carry
 
-    lax.fori_loop(0, owned // 2, body, 0)
+    lax.fori_loop(0, owned // 4, body, 0)
 
     def store(i, block):
         out_ref[pl.ds(2 * i, 2), 0] = block.reshape(2, capacity, LANES)
@@ -267,7 +272,16 @@
     def by_part(rows):
         return rows.reshape(part, parts, width).transpose(1, 0, 2)
 
-    kv_sent = jnp.stack([by_part(key_rows), by_part(value_rows)], axis=1)
+    kv_sent = pl.pallas_call(
+        split_kernel,
+        grid=(parts,),
+        in_specs=[pl.BlockSpec((part, width), lambda i: (0, i))] * 2,
+        out_specs=pl.BlockSpec((1, 2, part, width), lambda i: (i, 0, 0, 0)),
+        out_shape=shape_of((parts, 2, part, width), BF16),
+        compiler_params=params(),
+        cost_estimate=cost(0, 6e6),
+        name="split_kv",
+    )(key_rows, value_rows)
     kv_tok = exchange(kv_sent, "head")
     q_tok = exchange(by_part(query_rows), "head")
 
@@ -303,7 +317,7 @@
         out_specs=pl.BlockSpec((groups, 1, capacity + META, 2 * LANES), lambda h: (0, h, 0, 0)),
         out_shape=shape_of((groups, heads, capacity + META, 2 * LANES), BF16),
         compiler_params=params(),
-        cost_estimate=cost(heads * 4.0 * slots * tokens * LANES, 8e6),
+        cost_estimate=cost(heads * 16.0 * slots * tokens * LANES, 8e6),
         name="pack_kv",
     )(slot, count, count, kv_tok, kv_tok)
     kv_recv = exchange(kv_packed, "seq")
@@ -354,7 +368,7 @@
             name=f"unpack_kv_{first}",
         )(pick, kv_recv)
 
-    splits = ((0, 1), (1, heads - 1))
+    splits = ((0, heads - 1), (heads - 1, 1))
     received = []
     indices = []
     for first, count_heads in splits:
@@ -378,54 +392,52 @@
         name="unpack_q",
     )(index, q_recv)
 
-    replies = []
+    token_rows = None
     for (first, count_heads), recv in zip(splits, received, strict=True):
-        replies.append(
-            pl.pallas_call(
-                functools.partial(attend_kernel, first=first),
-                grid_spec=pltpu.PrefetchScalarGridSpec(
-                    num_scalar_prefetch=1,
-                    grid=(count_heads,),
-                    in_specs=[
-                        pl.BlockSpec((1, owned, BLOCK), lambda h, fetch, first=first: (h + first, 0, 0)),
-                        pl.BlockSpec(
-                            (1, owned * BLOCK, LANES), lambda h, fetch, first=first: (h + first, 0, 0)
-                        ),
-                        pl.BlockSpec(
-                            (groups, 1, KCAP, BLOCK, 2 * LANES), lambda h, fetch: (0, h, 0, 0, 0)
-                        ),
-                    ],
-                    out_specs=pl.BlockSpec(
-                        (groups, 1, capacity, LANES), lambda h, fetch: (0, h, 0, 0)
+        reply = pl.pallas_call(
+            functools.partial(attend_kernel, first=first),
+            grid_spec=pltpu.PrefetchScalarGridSpec(
+                num_scalar_prefetch=1,
+                grid=(count_heads,),
+                in_specs=[
+                    pl.BlockSpec((1, owned, BLOCK), lambda h, fetch, first=first: (h + first, 0, 0)),
+                    pl.BlockSpec(
+                        (1, owned * BLOCK, LANES), lambda h, fetch, first=first: (h + first, 0, 0)
                     ),
-                    scratch_shapes=[pltpu.VMEM((owned * BLOCK, LANES), BF16)],
-                ),
-                out_shape=shape_of((groups, count_heads, capacity, LANES), BF16),
-                compiler_params=params(),
-                cost_estimate=cost(
-                    count_heads * 4.0 * owned * BLOCK * PAIRS * BLOCK * LANES,
-                    count_heads * 6e6,
-                    count_heads * owned * BLOCK * PAIRS * BLOCK,
-                ),
-                name=f"attend_{first}",
-            )(fetch, index, q_sorted, recv)
-        )
-    reply = jnp.concatenate(replies, axis=1)
-    returned = exchange(reply, "seq")
-    token_rows = pl.pallas_call(
-        final_kernel,
-        grid=(heads,),
-        in_specs=[
-            pl.BlockSpec((1, chunks, LANES), lambda h: (h, 0, 0)),
-            pl.BlockSpec((groups, 1, capacity, LANES), lambda h: (0, h, 0, 0)),
-        ],
-        out_specs=pl.BlockSpec((parts, part, LANES), lambda h: (0, 0, h)),
-        out_shape=shape_of((parts, part, width), BF16),
-        scratch_shapes=[pltpu.VMEM((tokens, LANES), I32)],
-        compiler_params=params(),
-        cost_estimate=cost(heads * 4.0 * slots * tokens * LANES, 4e6),
-        name="final",
-    )(slot, returned)
+                    pl.BlockSpec(
+                        (groups, 1, KCAP, BLOCK, 2 * LANES), lambda h, fetch: (0, h, 0, 0, 0)
+                    ),
+                ],
+                out_specs=pl.BlockSpec((groups, 1, capacity, LANES), lambda h, fetch: (0, h, 0, 0)),
+                scratch_shapes=[pltpu.VMEM((owned * BLOCK, LANES), BF16)],
+            ),
+            out_shape=shape_of((groups, count_heads, capacity, LANES), BF16),
+            compiler_params=params(),
+            cost_estimate=cost(
+                count_heads * 4.0 * owned * BLOCK * PAIRS * BLOCK * LANES,
+                count_heads * 6e6,
+                count_heads * owned * BLOCK * PAIRS * BLOCK,
+            ),
+            name=f"attend_{first}",
+        )(fetch, index, q_sorted, recv)
+        returned = exchange(reply, "seq")
+        operands = (slot, returned) + (() if token_rows is None else (token_rows,))
+        token_rows = pl.pallas_call(
+            final_kernel,
+            grid=(count_heads,),
+            in_specs=[
+                pl.BlockSpec((1, chunks, LANES), lambda h, first=first: (h + first, 0, 0)),
+                pl.BlockSpec((groups, 1, capacity, LANES), lambda h: (0, h, 0, 0)),
+            ]
+            + [pl.BlockSpec(memory_space=pl.ANY)] * (len(operands) - 2),
+            out_specs=pl.BlockSpec((parts, part, LANES), lambda h, first=first: (0, 0, h + first)),
+            out_shape=shape_of((parts, part, width), BF16),
+            scratch_shapes=[pltpu.VMEM((tokens, LANES), I32)],
+            input_output_aliases={} if token_rows is None else {2: 0},
+            compiler_params=params(),
+            cost_estimate=cost(count_heads * 4.0 * slots * tokens * LANES, 2e6),
+            name=f"final_{first}",
+        )(*operands)
     rows = exchange(token_rows, "head")
     return rows.transpose(1, 0, 2).reshape(part, parts * width)
 

time: 516 us -> 464 us (0.90)
  blocking collectives: 62.6 us -> 27.4 us
  waiting for transfers between devices: 240 us -> 218 us
  starting transfers between devices: 32.9 us -> 46.3 us
  Pallas kernels: 156 us -> 148 us
  local copies, waits for them, and re-layouts: 16.4 us -> 10.8 us
    all_to_all x2 -> x1, blocking collectives: 62.6 us -> 27.4 us  [exchange(): return lax.all_to_all(array, axis, split_axis=0, concat_axis=0, tiled=True)]
    all_to_all x6 -> x8, waiting for transfers between devices: 240 us -> 218 us  [exchange(): return lax.all_to_all(array, axis, split_axis=0, concat_axis=0, tiled=True)]
    all_to_all x6 -> x8, starting transfers between devices: 32.9 us -> 46.3 us  [exchange(): return lax.all_to_all(array, axis, split_axis=0, concat_axis=0, tiled=True)]
    pallas_call x0 -> x1, other arithmetic: none -> 9.8 us  [unpack_kv(): pl.pallas_call(functools.partial(unpack_kv_kernel, first=first), grid_spe...]
    pallas_call x2 -> x1, Pallas kernels: 25.1 us -> 15.3 us  [unpack_kv(): pl.pallas_call(functools.partial(unpack_kv_kernel, first=first), grid_spe...]
    pallas_call x1 -> x3, Pallas kernels: 15.5 us -> 23.8 us  [the longest x2 17.5 us: per_device(): pl.pallas_call(final_kernel, grid=(count_heads,), in_specs=[pl.BlockSpec(...]
    pallas_call x2, Pallas kernels: 55.3 us -> 49.5 us  [per_device(): pl.pallas_call(functools.partial(attend_kernel, first=first), grid_spec=p...]
  transfers between devices with their start and end apart: 6 -> 8, of which waited for: 5 -> 8; matrix products, arithmetic and copies ran while one was open for 1% -> 4% of each run, Pallas kernels for 20% -> 29%
where the time goes in v2:
time: 464 us; the launch traced here: 463 us
  waiting for transfers between devices  218 us (47%)
  Pallas kernels  148 us (32%)
  starting transfers between devices  46.3 us (10%)
  blocking collectives  27.4 us (6%)
  other arithmetic  11.6 us (2%)
  local copies, waits for them, and re-layouts  10.8 us (2%)
    all_to_all x8, waiting for transfers between devices, exchange(): return lax.all_to_all(array, axis, split_axis=0, concat_axis=0, tiled=True)  218 us
    pallas_call x2, Pallas kernels, per_device(): pl.pallas_call(functools.partial(attend_kernel, first=first), grid_spec=p...  49.5 us
    all_to_all x8, starting transfers between devices, exchange(): return lax.all_to_all(array, axis, split_axis=0, concat_axis=0, tiled=True)  46.3 us
    all_to_all x1, blocking collectives, exchange(): return lax.all_to_all(array, axis, split_axis=0, concat_axis=0, tiled=True)  27.4 us
    pallas_call x2, Pallas kernels, per_device(): pl.pallas_call(final_kernel, grid=(count_heads,), in_specs=[pl.BlockSpec(...  17.5 us
    pallas_call x1, Pallas kernels, per_device(): pl.pallas_call(pack_kv_kernel, grid=(heads,), in_specs=[pl.BlockSpec((1,...  16.6 us
    pallas_call x1, Pallas kernels, per_device(): pl.pallas_call(pack_q_kernel, grid=(heads,), in_specs=[pl.BlockSpec((1, c...  16 us
    pallas_call x1, Pallas kernels, per_device(): pl.pallas_call(unpack_q_kernel, grid=(heads,), in_specs=[pl.BlockSpec((1,...  15.5 us
  transfers between devices with their start and end apart: 8, of which 8 were waited for; matrix products, arithmetic and copies ran while one was open for 4% of the time, Pallas kernels for 29%

profile of v2, /device:TPU:1, one launch (start us, length us, event | category | flops | bytes accessed | tf_op | source)
XLA Modules:
  0.0 462.8 jit_solution(15665807395106860756)
XLA Ops:
  0.0 6.3 %split_kv.1 = bf16[8,2,256,384]{3,2,1,0:T(8,128)(2,1)} custom-call(bf16[256,3072]{1,0:T(8,128)(2,1)} %key_ref.1, bf16[256,3072]{1,0:T(8,128)(2,1)} %value_ref.1), custom_call_target="tpu_custom_call" | custom-call | bytes 6000000 | tf_op jit(solution)/shard_map/split_kv/pallas_call | solution.py:275
  6.3 0.0 copy-start.6
  6.3 0.0 copy-start.7
  6.3 0.0 copy-start.1
  6.3 5.9 %all-to-all-start = ((bf16[8,2,256,384]{3,2,1,0:T(8,128)(2,1)}), bf16[8,2,256,384]{3,2,1,0:T(8,128)(2,1)}, u32[]{:S(2)}, u32[]{:S(2)}) async-start(bf16[8,2,256,384]{3,2,1,0:T(8,128)(2,1)} %split_kv.1), calls=%async_computation | async-start | bytes 6291456 | tf_op jit(solution)/shard_map/all_to_all | solution.py:236
  12.3 0.0 copy-done.6
  12.3 0.0 copy-done.7
  12.3 0.6 copy.24
  12.9 0.0 copy-done.1
  12.9 0.7 copy.16
  13.6 1.6 copy.17
  15.2 11.5 %slots.1 = (s32[6,16,128]{2,1,0:T(8,128)}, f32[6,16,128]{2,1,0:T(8,128)}) custom-call(s32[6,16,128]{2,1,0:T(8,128)} %bitcast.21), custom_call_target="tpu_custom_call" | custom-call | flops 6000000000 | bytes 1000000 | tf_op jit(solution)/shard_map/slots/pallas_call | solution.py:289
  26.7 23.3 %all-to-all-done.key_ref.value_ref = bf16[8,2,256,384]{3,2,1,0:T(8,128)(2,1)} async-done(((bf16[8,2,256,384]{3,2,1,0:T(8,128)(2,1)}), bf16[8,2,256,384]{3,2,1,0:T(8,128)(2,1)}, u32[]{:S(2)}, u32[]{:S(2)}) %all-to-all-start) | async-done | bytes 3145760 | tf_op jit(solution)/shard_map/all_to_all | solution.py:236
  49.9 4.4 all-to-all-start.2
  54.3 16.6 %pack_kv.1 = bf16[16,3,208,256]{3,2,1,0:T(8,128)(2,1)} custom-call(s32[6,16,128]{2,1,0:T(8,128)} %get-tuple-element.11.slot_ref.index_ref, f32[6,16,128]{2,1,0:T(8,128)} %get-tuple-element.12.key_count_ref.query_count_ref, f32[6,16,128]{2,1,0:T(8,128)} %get-tuple-element.12.key_count_ref.query_count_ref, ...), custom_call_target="tpu_custom_call" | custom-call | flops 38654705664 | bytes 8000000 | tf_op jit(solution)/shard_map/pack_kv/pallas_call | solution.py:307
  70.9 4.1 all-to-all-done.2.query_ref
  75.0 0.0 copy-start.3
  75.0 1.1 copy-done.3
  76.2 7.9 %all-to-all-start.1 = ((bf16[16,3,208,256]{3,2,1,0:T(8,128)(2,1)}), bf16[16,3,208,256]{3,2,1,0:T(8,128)(2,1)}, u32[]{:S(2)}, u32[]{:S(2)}) async-start(bf16[16,3,208,256]{3,2,1,0:T(8,128)(2,1)} %pack_kv.1), calls=%async_computation.1 | async-start | bytes 10223616 | tf_op jit(solution)/shard_map/all_to_all | solution.py:236
  84.1 16.0 %pack_q.1 = bf16[16,3,192,128]{3,2,1,0:T(8,128)(2,1)} custom-call(s32[6,16,128]{2,1,0:T(8,128)} %get-tuple-element.11.slot_ref.index_ref, bf16[8,256,384]{2,1,0:T(8,128)(2,1)} %copy-done.3), custom_call_target="tpu_custom_call" | custom-call | flops 9663676416 | bytes 4000000 | tf_op jit(solution)/shard_map/pack_q/pallas_call | solution.py:325
  100.1 0.0 copy-start.5
  100.1 59.2 %all-to-all-done.1.in_ref = bf16[16,3,208,256]{3,2,1,0:T(8,128)(2,1)} async-done(((bf16[16,3,208,256]{3,2,1,0:T(8,128)(2,1)}), bf16[16,3,208,256]{3,2,1,0:T(8,128)(2,1)}, u32[]{:S(2)}, u32[]{:S(2)}) %all-to-all-start.1) | async-done | bytes 5111840 | tf_op jit(solution)/shard_map/all_to_all | solution.py:236
  159.3 4.7 %all-to-all-start.3 = ((bf16[16,3,192,128]{3,2,1,0:T(8,128)(2,1)}), bf16[16,3,192,128]{3,2,1,0:T(8,128)(2,1)S(1)}, u32[]{:S(2)}, u32[]{:S(2)}) async-start(bf16[16,3,192,128]{3,2,1,0:T(8,128)(2,1)} %pack_q.1), calls=%async_computation.3 | async-start | bytes 4718592 | tf_op jit(solution)/shard_map/all_to_all | solution.py:236
  164.0 0.0 copy-done.5
  164.0 0.2 copy.13
  164.2 0.2 reshape.35
  164.4 1.0 compare_reduce_fusion
  165.4 0.1 convolution_convert_fusion
  165.5 0.3 select_reduce_fusion.1
  165.8 0.7 copy.14.pick_ref
  166.5 15.3 %unpack_kv_0.1 = (bf16[16,2,4,128,256]{4,3,2,1,0:T(8,128)(2,1)}, s32[2,16,128]{2,1,0:T(8,128)}) custom-call(s32[3,16,4]{2,1,0:T(8,128)} %copy.14.pick_ref, bf16[16,3,208,256]{3,2,1,0:T(8,128)(2,1)} %all-to-all-done.1.in_ref), custom_call_target="tpu_custom_call" | custom-call | flops 6442450944 | bytes 12000000 | tf_op jit(solution)/shard_map/unpack_kv_0/pallas_call | solution.py:341
  181.8 12.3 %all-to-all-done.3.in_ref = bf16[16,3,192,128]{3,2,1,0:T(8,128)(2,1)S(1)} async-done(((bf16[16,3,192,128]{3,2,1,0:T(8,128)(2,1)}), bf16[16,3,192,128]{3,2,1,0:T(8,128)(2,1)S(1)}, u32[]{:S(2)}, u32[]{:S(2)}) %all-to-all-start.3) | async-done | bytes 2359328 | tf_op jit(solution)/shard_map/all_to_all | solution.py:236
  194.1 0.0 copy-start
  194.1 0.0 copy-start.9
  194.1 0.0 copy-start.8
  194.1 1.4 copy-done
  195.5 6.8 %all-to-all-start.6 = ((bf16[16,2,4,128,256]{4,3,2,1,0:T(8,128)(2,1)}), bf16[16,2,4,128,256]{4,3,2,1,0:T(8,128)(2,1)}, u32[]{:S(2)}, u32[]{:S(2)}) async-start(bf16[16,2,4,128,256]{4,3,2,1,0:T(8,128)(2,1)} %get-tuple-element.16), calls=%async_computation.6 | async-start | bytes 16777216 | tf_op jit(solution)/shard_map/all_to_all | solution.py:236
  202.3 0.0 copy-done.9
  202.3 0.0 copy-done.8
  202.4 9.8 %unpack_kv_2.1 = (s32[3,16,128]{2,1,0:T(8,128)S(1)}, bf16[16,1,4,128,256]{4,3,2,1,0:T(8,128)(2,1)}) fusion(s32[3,16,128]{2,1,0:T(8,128)S(1)} %constant_dynamic-update-slice_fusion.1, s32[3,16,4]{2,1,0:T(8,128)S(1)} %copy-done.8, bf16[16,3,208,256]{3,2,1,0:T(8,128)(2,1)} %all-to-all-done.1.in_ref), kind=kCustom, calls=%fused_computation.14 | custom fusion | flops 3221225472 | bytes 9338880 | tf_op jit(solution)/shard_map/unpack_kv_2/pallas_call | solution.py:341
  212.2 110.4 %all-to-all-done.6.recv_ref = bf16[16,2,4,128,256]{4,3,2,1,0:T(8,128)(2,1)} async-done(((bf16[16,2,4,128,256]{4,3,2,1,0:T(8,128)(2,1)}), bf16[16,2,4,128,256]{4,3,2,1,0:T(8,128)(2,1)}, u32[]{:S(2)}, u32[]{:S(2)}) %all-to-all-start.6) | async-done | bytes 8388640 | tf_op jit(solution)/shard_map/all_to_all | solution.py:236
  322.6 0.0 copy-done.10
  322.6 4.8 %all-to-all-start.4 = ((bf16[16,1,4,128,256]{4,3,2,1,0:T(8,128)(2,1)}), bf16[16,1,4,128,256]{4,3,2,1,0:T(8,128)(2,1)}, u32[]{:S(2)}, u32[]{:S(2)}) async-start(bf16[16,1,4,128,256]{4,3,2,1,0:T(8,128)(2,1)} %get-tuple-element.20), calls=%async_computation.4 | async-start | bytes 8388608 | tf_op jit(solution)/shard_map/all_to_all | solution.py:236
  327.4 0.2 fusion.1
  327.6 0.1 reshape.36
  327.7 0.1 fusion
  327.8 0.1 broadcast_in_dim.30
  327.9 0.3 select_reduce_fusion
  328.2 0.7 reshape.37.fetch_ref
  328.9 15.5 %unpack_q.1.query_ref = bf16[3,2048,128]{2,1,0:T(8,128)(2,1)} custom-call(s32[3,16,128]{2,1,0:T(8,128)} %copy-done.10, bf16[16,3,192,128]{3,2,1,0:T(8,128)(2,1)} %copy-done), custom_call_target="tpu_custom_call" | custom-call | flops 9663676416 | bytes 4000000 | tf_op jit(solution)/shard_map/unpack_q/pallas_call | solution.py:380
  344.4 31.3 %attend_0.1 = bf16[16,2,192,128]{3,2,1,0:T(8,128)(2,1)} custom-call(s32[3,16,16]{2,1,0:T(8,128)} %reshape.37.fetch_ref, s32[3,16,128]{2,1,0:T(8,128)} %copy-done.10, bf16[3,2048,128]{2,1,0:T(8,128)(2,1)} %unpack_q.1.query_ref, bf16[16,2,4,128,256]{4,3,2,1,0:T(8,128)(2,1)} %all-to-all-done.6.recv_ref), custom_call_target="tpu_custom_call" | custom-call | flops 4294967296 | bytes 12000000 | tf_op jit(solution)/shard_map/attend_0/pallas_call | solution.py:397
  375.7 5.4 %all-to-all-done.4.recv_ref = bf16[16,1,4,128,256]{4,3,2,1,0:T(8,128)(2,1)} async-done(((bf16[16,1,4,128,256]{4,3,2,1,0:T(8,128)(2,1)}), bf16[16,1,4,128,256]{4,3,2,1,0:T(8,128)(2,1)}, u32[]{:S(2)}, u32[]{:S(2)}) %all-to-all-start.4) | async-done | bytes 4194336 | tf_op jit(solution)/shard_map/all_to_all | solution.py:236
  381.1 6.6 %all-to-all-start.7 = ((bf16[16,2,192,128]{3,2,1,0:T(8,128)(2,1)}), bf16[16,2,192,128]{3,2,1,0:T(8,128)(2,1)S(1)}, u32[]{:S(2)}, u32[]{:S(2)}) async-start(bf16[16,2,192,128]{3,2,1,0:T(8,128)(2,1)} %attend_0.1), calls=%async_computation.7 | async-start | bytes 3145728 | tf_op jit(solution)/shard_map/all_to_all | solution.py:236
  387.7 18.2 %attend_2.1 = bf16[16,1,192,128]{3,2,1,0:T(8,128)(2,1)} custom-call(s32[3,16,16]{2,1,0:T(8,128)} %reshape.37.fetch_ref, s32[3,16,128]{2,1,0:T(8,128)} %copy-done.10, bf16[3,2048,128]{2,1,0:T(8,128)(2,1)} %unpack_q.1.query_ref, bf16[16,1,4,128,256]{4,3,2,1,0:T(8,128)(2,1)} %all-to-all-done.4.recv_ref), custom_call_target="tpu_custom_call" | custom-call | flops 2147483648 | bytes 6000000 | tf_op jit(solution)/shard_map/attend_2/pallas_call | solution.py:397
  405.9 2.1 all-to-all-done.7.in_ref
  408.0 5.3 %all-to-all-start.5 = ((bf16[16,1,192,128]{3,2,1,0:T(8,128)(2,1)}), bf16[16,1,192,128]{3,2,1,0:T(8,128)(2,1)S(1)}, u32[]{:S(2)}, u32[]{:S(2)}) async-start(bf16[16,1,192,128]{3,2,1,0:T(8,128)(2,1)} %attend_2.1), calls=%async_computation.5 | async-start | bytes 1572864 | tf_op jit(solution)/shard_map/all_to_all | solution.py:236
  413.3 0.0 copy-done.2
  413.3 11.1 %final_0.1.refs_0_ = bf16[8,256,384]{2,1,0:T(8,128)(2,1)} custom-call(s32[6,16,128]{2,1,0:T(8,128)} %get-tuple-element.11.slot_ref.index_ref, bf16[16,2,192,128]{3,2,1,0:T(8,128)(2,1)} %copy-done.2), custom_call_target="tpu_custom_call" | custom-call | flops 6442450944 | bytes 2000000 | tf_op jit(solution)/shard_map/final_0/pallas_call | solution.py:425
  424.4 1.1 all-to-all-done.5.in_ref
  425.6 0.9 copy-done.4
  426.4 6.5 %final_2.1 = bf16[8,256,384]{2,1,0:T(8,128)(2,1)} custom-call(s32[6,16,128]{2,1,0:T(8,128)} %get-tuple-element.11.slot_ref.index_ref, bf16[16,1,192,128]{3,2,1,0:T(8,128)(2,1)} %copy-done.4, bf16[8,256,384]{2,1,0:T(8,128)(2,1)} %final_0.1.refs_0_), custom_call_target="tpu_custom_call", output_to_operand_aliasing={{}: (2, {})} | custom-call | flops 3221225472 | bytes 2000000 | tf_op jit(solution)/shard_map/final_2/pallas_call | solution.py:425
  432.9 27.4 %all_to_all.45 = bf16[8,256,384]{2,1,0:T(8,128)(2,1)S(1)} all-to-all(bf16[8,256,384]{2,1,0:T(8,128)(2,1)} %final_2.1), channel_id=1, replica_groups=mesh['seq'=16,'head'=8] {'head'}, dimensions={0} | all-to-all | bytes 3145728 | tf_op jit(solution)/shard_map/all_to_all | solution.py:236
  460.3 0.7 copy.18
  461.1 1.7 copy.19
  (9 shorter events, 0.0 us)
Async XLA Ops:
  6.3 6.0 %copy-start.6 = (s32[3,2048]{1,0:T(4,128)S(1)}, s32[3,2048]{1,0:T(4,128)}, u32[]{:S(2)}) copy-start(s32[3,2048]{1,0:T(4,128)} %param.10) | copy-start | bytes 73732
  6.3 6.0 %copy-start.7 = (s32[3,2048]{1,0:T(4,128)S(1)}, s32[3,2048]{1,0:T(4,128)}, u32[]{:S(2)}) copy-start(s32[3,2048]{1,0:T(4,128)} %param.9) | copy-start | bytes 73732
  6.3 6.6 %copy-start.1 = (bf16[256,3072]{1,0:T(8,128)(2,1)S(1)}, bf16[256,3072]{1,0:T(8,128)(2,1)}, u32[]{:S(2)}) copy-start(bf16[256,3072]{1,0:T(8,128)(2,1)} %param.6) | copy-start | bytes 4718596
  6.3 43.6 %all-to-all-start = ((bf16[8,2,256,384]{3,2,1,0:T(8,128)(2,1)}), bf16[8,2,256,384]{3,2,1,0:T(8,128)(2,1)}, u32[]{:S(2)}, u32[]{:S(2)}) async-start(bf16[8,2,256,384]{3,2,1,0:T(8,128)(2,1)} %split_kv.1), calls=%async_computation | async-start | bytes 6291456 | tf_op jit(solution)/shard_map/all_to_all | solution.py:236
  49.9 25.1 %all-to-all-start.2 = ((bf16[8,256,384]{2,1,0:T(8,128)(2,1)}), bf16[8,256,384]{2,1,0:T(8,128)(2,1)S(1)}, u32[]{:S(2)}, u32[]{:S(2)}) async-start(bf16[8,256,384]{2,1,0:T(8,128)(2,1)} %bitcast.2), calls=%async_computation.2 | async-start | bytes 3145728 | tf_op jit(solution)/shard_map/all_to_all | solution.py:236
  75.0 1.1 copy-start.3
  76.2 83.1 %all-to-all-start.1 = ((bf16[16,3,208,256]{3,2,1,0:T(8,128)(2,1)}), bf16[16,3,208,256]{3,2,1,0:T(8,128)(2,1)}, u32[]{:S(2)}, u32[]{:S(2)}) async-start(bf16[16,3,208,256]{3,2,1,0:T(8,128)(2,1)} %pack_kv.1), calls=%async_computation.1 | async-start | bytes 10223616 | tf_op jit(solution)/shard_map/all_to_all | solution.py:236
  100.1 63.9 %copy-start.5 = (s32[3,256,16]{1,2,0:T(8,128)S(1)}, s32[3,256,16]{1,2,0:T(8,128)}, u32[]{:S(2)}) copy-start(s32[3,256,16]{1,2,0:T(8,128)} %param.11) | copy-start | bytes 147460
  159.3 34.8 %all-to-all-start.3 = ((bf16[16,3,192,128]{3,2,1,0:T(8,128)(2,1)}), bf16[16,3,192,128]{3,2,1,0:T(8,128)(2,1)S(1)}, u32[]{:S(2)}, u32[]{:S(2)}) async-start(bf16[16,3,192,128]{3,2,1,0:T(8,128)(2,1)} %pack_q.1), calls=%async_computation.3 | async-start | bytes 4718592 | tf_op jit(solution)/shard_map/all_to_all | solution.py:236
  194.1 1.4 copy-start
  194.1 8.2 %copy-start.9 = (s32[2,16,128]{2,1,0:T(8,128)S(1)}, s32[2,16,128]{2,1,0:T(8,128)}, u32[]{:S(2)}) copy-start(s32[2,16,128]{2,1,0:T(8,128)} %get-tuple-element.13) | copy-start | bytes 49156
  194.1 8.2 %copy-start.8 = (s32[3,16,4]{2,1,0:T(8,128)S(1)}, s32[3,16,4]{2,1,0:T(8,128)}, u32[]{:S(2)}) copy-start(s32[3,16,4]{2,1,0:T(8,128)} %copy.14.pick_ref) | copy-start | bytes 2308
  195.5 127.1 %all-to-all-start.6 = ((bf16[16,2,4,128,256]{4,3,2,1,0:T(8,128)(2,1)}), bf16[16,2,4,128,256]{4,3,2,1,0:T(8,128)(2,1)}, u32[]{:S(2)}, u32[]{:S(2)}) async-start(bf16[16,2,4,128,256]{4,3,2,1,0:T(8,128)(2,1)} %get-tuple-element.16), calls=%async_computation.6 | async-start | bytes 16777216 | tf_op jit(solution)/shard_map/all_to_all | solution.py:236
  212.2 110.4 %copy-start.10 = (s32[3,16,128]{2,1,0:T(8,128)}, s32[3,16,128]{2,1,0:T(8,128)S(1)}, u32[]{:S(2)}) copy-start(s32[3,16,128]{2,1,0:T(8,128)S(1)} %get-tuple-element.19.index_ref) | copy-start | bytes 73732
  322.6 58.5 %all-to-all-start.4 = ((bf16[16,1,4,128,256]{4,3,2,1,0:T(8,128)(2,1)}), bf16[16,1,4,128,256]{4,3,2,1,0:T(8,128)(2,1)}, u32[]{:S(2)}, u32[]{:S(2)}) async-start(bf16[16,1,4,128,256]{4,3,2,1,0:T(8,128)(2,1)} %get-tuple-element.20), calls=%async_computation.4 | async-start | bytes 8388608 | tf_op jit(solution)/shard_map/all_to_all | solution.py:236
  381.1 26.9 %all-to-all-start.7 = ((bf16[16,2,192,128]{3,2,1,0:T(8,128)(2,1)}), bf16[16,2,192,128]{3,2,1,0:T(8,128)(2,1)S(1)}, u32[]{:S(2)}, u32[]{:S(2)}) async-start(bf16[16,2,192,128]{3,2,1,0:T(8,128)(2,1)} %attend_0.1), calls=%async_computation.7 | async-start | bytes 3145728 | tf_op jit(solution)/shard_map/all_to_all | solution.py:236
  408.0 5.4 %copy-start.2 = (bf16[16,2,192,128]{3,2,1,0:T(8,128)(2,1)}, bf16[16,2,192,128]{3,2,1,0:T(8,128)(2,1)S(1)}, u32[]{:S(2)}) copy-start(bf16[16,2,192,128]{3,2,1,0:T(8,128)(2,1)S(1)} %all-to-all-done.7.in_ref) | copy-start | bytes 4718596
  408.0 17.6 %all-to-all-start.5 = ((bf16[16,1,192,128]{3,2,1,0:T(8,128)(2,1)}), bf16[16,1,192,128]{3,2,1,0:T(8,128)(2,1)S(1)}, u32[]{:S(2)}, u32[]{:S(2)}) async-start(bf16[16,1,192,128]{3,2,1,0:T(8,128)(2,1)} %attend_2.1), calls=%async_computation.5 | async-start | bytes 1572864 | tf_op jit(solution)/shard_map/all_to_all | solution.py:236
  425.5 0.9 copy-start.4

commit v3 on v2

--- a/solution.py
+++ b/solution.py
@@ -92,27 +92,39 @@
 
 
 def split_kernel(key_ref, value_ref, out_ref):
-    out_ref[0, 0] = key_ref[...]
-    out_ref[0, 1] = value_ref[...]
-
-
-def pack_kv_kernel(slot_ref, key_count_ref, query_count_ref, key_ref, value_ref, out_ref):
-    groups, _, rows, _ = out_ref.shape
-    capacity = rows - META
+    parts, _, _, width = out_ref.shape
+    for part in range(parts):
+        columns = slice(part * width, (part + 1) * width)
+        out_ref[part, 0] = key_ref[:, columns]
+        out_ref[part, 1] = value_ref[:, columns]
+
+
+def pack_kv_kernel(slot_ref, count_ref, key_ref, value_ref, out_ref):
+    head = pl.program_id(0)
+    heads = pl.num_programs(0)
+    groups, rows, _ = out_ref.shape
+    of_heads = count_ref.shape[0] // 2
+    capacity = (rows - META) // of_heads
     tokens = key_ref.shape[0] * key_ref.shape[2]
     keys = key_ref[:, 0].reshape(tokens, LANES)
     values = value_ref[:, 0].reshape(tokens, LANES)
-
-    def store(i, block):
-        out_ref[pl.ds(2 * i, 2), 0, :capacity, :] = block.reshape(2, capacity, 2 * LANES)
+    at = pl.ds(pl.multiple_of(head * capacity, META), capacity)
+
+    def store(i, block):
+        out_ref[pl.ds(2 * i, 2), at, :] = block.reshape(2, capacity, 2 * LANES)
 
     both = jnp.concatenate([keys, values], axis=1)
     spread(slot_ref[0], both, store, groups * capacity, 2 * capacity)
-    for group in range(groups):
-        key_count = jnp.broadcast_to(key_count_ref[0, group : group + 1, :], (META, LANES))
-        query_count = jnp.broadcast_to(query_count_ref[0, group : group + 1, :], (META, LANES))
-        out_ref[group, 0, capacity:, :LANES] = key_count.astype(BF16)
-        out_ref[group, 0, capacity:, LANES:] = query_count.astype(BF16)
+
+    @pl.when(head == heads - 1)
+    def _():
+        row = iota((groups, META, LANES), 1)
+        for side in range(2):
+            block = jnp.zeros((groups, META, LANES), F32)
+            for h in range(of_heads):
+                counts = count_ref[(1 - side) * of_heads + h]
+                block = jnp.where(row == h, counts[:, None, :], block)
+            out_ref[:, of_heads * capacity :, side * LANES : (side + 1) * LANES] = block.astype(BF16)
 
 
 def pack_q_kernel(slot_ref, query_ref, out_ref):
@@ -143,26 +155,37 @@
     return (found + place).astype(I32)
 
 
-def unpack_kv_kernel(pick_ref, in_ref, out_ref, query_source_ref, wide_ref, sorted_ref, *, first):
-    head = pl.program_id(0) + first
-    groups, _, rows, _ = in_ref.shape
-    capacity = rows - META
-    counts = in_ref[:, 0, capacity:, :].astype(F32)
-    counts = jnp.max(counts, axis=1)
+def unpack_kv_kernel(
+    pick_ref, in_ref, meta_ref, first_ref, last_ref, query_source_ref, wide_ref, sorted_ref
+):
+    head = pl.program_id(0)
+    heads = pl.num_programs(0)
+    groups, capacity, _ = in_ref.shape
+    row = iota(meta_ref.shape, 1)
+    counts = jnp.sum(jnp.where(row == head, meta_ref[...].astype(F32), 0.0), axis=1)
     query_source_ref[0] = sources(counts[:, LANES:], capacity)
-    packed = in_ref[:, 0, :capacity, :].reshape(groups * capacity, 2 * LANES)
+    packed = in_ref[...].reshape(groups * capacity, 2 * LANES)
 
     def store(i, block):
         sorted_ref[pl.ds(4 * i, 4)] = block.reshape(4, BLOCK, 2 * LANES)
 
     collect(sources(counts[:, :LANES], capacity), packed, wide_ref, store, 4 * BLOCK)
 
-    def copy(i, carry):
-        for j in range(KCAP):
-            out_ref[i, 0, j] = sorted_ref[pick_ref[head, i, j]]
-        return carry
-
-    lax.fori_loop(0, groups, copy, 0)
+    def send(out_ref):
+        def copy(i, carry):
+            for j in range(KCAP):
+                out_ref[i, 0, j] = sorted_ref[pick_ref[head, i, j]]
+            return carry
+
+        lax.fori_loop(0, groups, copy, 0)
+
+    @pl.when(head < heads - 1)
+    def _():
+        send(first_ref)
+
+    @pl.when(head == heads - 1)
+    def _():
+        send(last_ref)
 
 
 def unpack_q_kernel(index_ref, in_ref, out_ref, wide_ref):
@@ -274,9 +297,9 @@
 
     kv_sent = pl.pallas_call(
         split_kernel,
-        grid=(parts,),
-        in_specs=[pl.BlockSpec((part, width), lambda i: (0, i))] * 2,
-        out_specs=pl.BlockSpec((1, 2, part, width), lambda i: (i, 0, 0, 0)),
+        grid=(4,),
+        in_specs=[pl.BlockSpec((part // 4, parts * width), lambda i: (i, 0))] * 2,
+        out_specs=pl.BlockSpec((parts, 2, part // 4, width), lambda i: (0, 0, i, 0)),
         out_shape=shape_of((parts, 2, part, width), BF16),
         compiler_params=params(),
         cost_estimate=cost(0, 6e6),
@@ -309,17 +332,16 @@
         grid=(heads,),
         in_specs=[
             pl.BlockSpec((1, chunks, LANES), lambda h: (h + heads, 0, 0)),
-            pl.BlockSpec((1, groups, LANES), lambda h: (h + heads, 0, 0)),
-            pl.BlockSpec((1, groups, LANES), lambda h: (h, 0, 0)),
+            pl.BlockSpec((2 * heads, groups, LANES), lambda h: (0, 0, 0)),
             pl.BlockSpec((parts, 1, part, LANES), lambda h: (0, 0, 0, h)),
             pl.BlockSpec((parts, 1, part, LANES), lambda h: (0, 1, 0, h)),
         ],
-        out_specs=pl.BlockSpec((groups, 1, capacity + META, 2 * LANES), lambda h: (0, h, 0, 0)),
-        out_shape=shape_of((groups, heads, capacity + META, 2 * LANES), BF16),
+        out_specs=pl.BlockSpec((groups, heads * capacity + META, 2 * LANES), lambda h: (0, 0, 0)),
+        out_shape=shape_of((groups, heads * capacity + META, 2 * LANES), BF16),
         compiler_params=params(),
         cost_estimate=cost(heads * 16.0 * slots * tokens * LANES, 8e6),
         name="pack_kv",
-    )(slot, count, count, kv_tok, kv_tok)
+    )(slot, count, kv_tok, kv_tok)
     kv_recv = exchange(kv_packed, "seq")
 
     q_packed = pl.pallas_call(
@@ -337,45 +359,42 @@
     )(slot, q_tok)
     q_recv = exchange(q_packed, "seq")
 
-    def unpack_kv(first, count_heads):
-        return pl.pallas_call(
-            functools.partial(unpack_kv_kernel, first=first),
-            grid_spec=pltpu.PrefetchScalarGridSpec(
-                num_scalar_prefetch=1,
-                grid=(count_heads,),
-                in_specs=[
-                    pl.BlockSpec(
-                        (groups, 1, capacity + META, 2 * LANES), lambda h, pick: (0, h + first, 0, 0)
-                    ),
-                ],
-                out_specs=[
-                    pl.BlockSpec(
-                        (groups, 1, KCAP, BLOCK, 2 * LANES), lambda h, pick: (0, h, 0, 0, 0)
-                    ),
-                    pl.BlockSpec((1, owned, BLOCK), lambda h, pick: (h, 0, 0)),
-                ],
-                scratch_shapes=[
-                    pltpu.VMEM((owned * BLOCK, LANES), I32),
-                    pltpu.VMEM((owned, BLOCK, 2 * LANES), BF16),
-                ],
-            ),
-            out_shape=[
-                shape_of((groups, count_heads, KCAP, BLOCK, 2 * LANES), BF16),
-                shape_of((count_heads, owned, BLOCK), I32),
+    splits = ((0, heads - 1), (heads - 1, 1))
+    block = (groups, 1, KCAP, BLOCK, 2 * LANES)
+    first_sent, last_sent, index = pl.pallas_call(
+        unpack_kv_kernel,
+        grid_spec=pltpu.PrefetchScalarGridSpec(
+            num_scalar_prefetch=1,
+            grid=(heads,),
+            in_specs=[
+                pl.BlockSpec((groups, capacity, 2 * LANES), lambda h, pick: (0, h, 0)),
+                pl.BlockSpec(
+                    (groups, META, 2 * LANES), lambda h, pick: (0, heads * capacity // META, 0)
+                ),
             ],
-            compiler_params=params(),
-            cost_estimate=cost(count_heads * 4.0 * slots * tokens * LANES, count_heads * 6e6),
-            name=f"unpack_kv_{first}",
-        )(pick, kv_recv)
-
-    splits = ((0, heads - 1), (heads - 1, 1))
-    received = []
-    indices = []
-    for first, count_heads in splits:
-        sent, index = unpack_kv(first, count_heads)
-        indices.append(index)
-        received.append(exchange(sent, "seq"))
-    index = jnp.concatenate(indices, axis=0)
+            out_specs=[
+                pl.BlockSpec(block, lambda h, pick: (0, jnp.minimum(h, heads - 2), 0, 0, 0)),
+                pl.BlockSpec(block, lambda h, pick: (0, 0, 0, 0, 0)),
+                pl.BlockSpec((1, owned, BLOCK), lambda h, pick: (h, 0, 0)),
+            ],
+            scratch_shapes=[
+                pltpu.VMEM((owned * BLOCK, LANES), I32),
+                pltpu.VMEM((owned, BLOCK, 2 * LANES), BF16),
+            ],
+        ),
+        out_shape=[
+            shape_of((groups, heads - 1, KCAP, BLOCK, 2 * LANES), BF16),
+            shape_of(block, BF16),
+            shape_of((heads, owned, BLOCK), I32),
+        ],
+        compiler_params=params(),
+        cost_estimate=cost(heads * 4.0 * slots * tokens * LANES, heads * 6e6),
+        name="unpack_kv",
+    )(pick, kv_recv, kv_recv)
+    first_recv = exchange(first_sent, "seq")
+    last_recv = exchange(last_sent, "seq")
+    received = (first_recv, last_recv)
+    q_recv, index, _ = lax.optimization_barrier((q_recv, index, first_recv))
 
     q_sorted = pl.pallas_call(
         unpack_q_kernel,

time: 464 us -> 431 us (0.929)
  waiting for transfers between devices: 218 us -> 96.5 us
  blocking collectives: 27.4 us -> 129 us
  other arithmetic: 11.6 us -> 1.81 us
  starting transfers between devices: 46.3 us -> 38.7 us
  Pallas kernels: 148 us -> 154 us
    all_to_all x8 -> x7, waiting for transfers between devices: 218 us -> 96.5 us  [exchange(): return lax.all_to_all(array, axis, split_axis=0, concat_axis=0, tiled=True)]
    all_to_all x1 -> x2, blocking collectives: 27.4 us -> 129 us  [exchange(): return lax.all_to_all(array, axis, split_axis=0, concat_axis=0, tiled=True)]
    pallas_call x1 -> x0, other arithmetic: 9.8 us -> none  [unpack_kv(): pl.pallas_call(functools.partial(unpack_kv_kernel, first=first), grid_spe...]
    all_to_all x8 -> x7, starting transfers between devices: 46.3 us -> 38.7 us  [exchange(): return lax.all_to_all(array, axis, split_axis=0, concat_axis=0, tiled=True)]
  transfers between devices with their start and end apart: 8 -> 7, of which waited for: 8 -> 7; matrix products, arithmetic and copies ran while one was open for 4% -> 2% of each run, Pallas kernels for 29% -> 33%
where the time goes in v3:
time: 431 us; the launch traced here: 430 us
  Pallas kernels  154 us (36%)
  blocking collectives  129 us (30%)
  waiting for transfers between devices  96.5 us (22%)
  starting transfers between devices  38.7 us (9%)
  local copies, waits for them, and re-layouts  9.42 us (2%)
    all_to_all x2, blocking collectives, exchange(): return lax.all_to_all(array, axis, split_axis=0, concat_axis=0, tiled=True)  129 us
    all_to_all x7, waiting for transfers between devices, exchange(): return lax.all_to_all(array, axis, split_axis=0, concat_axis=0, tiled=True)  96.5 us
    pallas_call x2, Pallas kernels, per_device(): pl.pallas_call(functools.partial(attend_kernel, first=first), grid_spec=p...  49.5 us
    all_to_all x7, starting transfers between devices, exchange(): return lax.all_to_all(array, axis, split_axis=0, concat_axis=0, tiled=True)  38.7 us
    pallas_call x1, Pallas kernels, per_device(): pl.pallas_call(unpack_kv_kernel, grid_spec=pltpu.PrefetchScalarGridSpec(n...  22 us
    pallas_call x1, Pallas kernels, per_device(): pl.pallas_call(pack_kv_kernel, grid=(heads,), in_specs=[pl.BlockSpec((1,...  17.5 us
    pallas_call x2, Pallas kernels, per_device(): pl.pallas_call(final_kernel, grid=(count_heads,), in_specs=[pl.BlockSpec(...  17.5 us
    pallas_call x1, Pallas kernels, per_device(): pl.pallas_call(pack_q_kernel, grid=(heads,), in_specs=[pl.BlockSpec((1, c...  16.1 us
  transfers between devices with their start and end apart: 7, of which 7 were waited for; matrix products, arithmetic and copies ran while one was open for 2% of the time, Pallas kernels for 33%

profile of v3, /device:TPU:1, one launch (start us, length us, event | category | flops | bytes accessed | tf_op | source)
XLA Modules:
  0.0 430.1 jit_solution(2172212553554299987)
XLA Ops:
  0.0 4.3 split_kv.1
  4.3 0.0 copy-start.6
  4.3 0.0 copy-start.7
  4.3 0.0 copy-start.1
  4.3 5.9 %all-to-all-start.2 = ((bf16[8,2,256,384]{3,2,1,0:T(8,128)(2,1)}), bf16[8,2,256,384]{3,2,1,0:T(8,128)(2,1)}, u32[]{:S(2)}, u32[]{:S(2)}) async-start(bf16[8,2,256,384]{3,2,1,0:T(8,128)(2,1)} %split_kv.1), calls=%async_computation.2 | async-start | bytes 6291456 | tf_op jit(solution)/shard_map/all_to_all | solution.py:259
  10.2 0.0 copy-done.6
  10.2 0.0 copy-done.7
  10.3 0.6 copy.23
  10.9 0.0 copy-done.1
  10.9 0.7 copy.14
  11.6 1.6 copy.15
  13.2 11.5 %slots.1 = (s32[6,16,128]{2,1,0:T(8,128)}, f32[6,16,128]{2,1,0:T(8,128)}) custom-call(s32[6,16,128]{2,1,0:T(8,128)} %bitcast.21), custom_call_target="tpu_custom_call" | custom-call | flops 6000000000 | bytes 1000000 | tf_op jit(solution)/shard_map/slots/pallas_call | solution.py:312
  24.6 23.3 %all-to-all-done.2.key_ref.value_ref = bf16[8,2,256,384]{3,2,1,0:T(8,128)(2,1)} async-done(((bf16[8,2,256,384]{3,2,1,0:T(8,128)(2,1)}), bf16[8,2,256,384]{3,2,1,0:T(8,128)(2,1)}, u32[]{:S(2)}, u32[]{:S(2)}) %all-to-all-start.2) | async-done | bytes 3145760 | tf_op jit(solution)/shard_map/all_to_all | solution.py:259
  47.9 4.4 %all-to-all-start = ((bf16[8,256,384]{2,1,0:T(8,128)(2,1)}), bf16[8,256,384]{2,1,0:T(8,128)(2,1)S(1)}, u32[]{:S(2)}, u32[]{:S(2)}) async-start(bf16[8,256,384]{2,1,0:T(8,128)(2,1)} %bitcast.2), calls=%async_computation | async-start | bytes 3145728 | tf_op jit(solution)/shard_map/all_to_all | solution.py:259
  52.3 17.5 %pack_kv.1 = bf16[16,592,256]{2,1,0:T(8,128)(2,1)} custom-call(s32[6,16,128]{2,1,0:T(8,128)} %get-tuple-element.12.slot_ref.index_ref, f32[6,16,128]{2,1,0:T(8,128)} %get-tuple-element.13.count_ref, bf16[8,2,256,384]{3,2,1,0:T(8,128)(2,1)} %all-to-all-done.2.key_ref.value_ref, bf16[8,2,256,384]{3,2,1,0:T(8,128)(2,1)} %all-to-all-done.2.key_ref.value_ref), custom_call_target="tpu_custom_call" | custom-call | flops 38654705664 | bytes 8000000 | tf_op jit(solution)/shard_map/pack_kv/pallas_call | solution.py:330
  69.8 3.2 all-to-all-done.query_ref
  73.0 0.0 copy-start.3
  73.0 1.1 copy-done.3
  74.1 7.9 %all-to-all-start.3 = ((bf16[16,592,256]{2,1,0:T(8,128)(2,1)}), bf16[16,592,256]{2,1,0:T(8,128)(2,1)}, u32[]{:S(2)}, u32[]{:S(2)}) async-start(bf16[16,592,256]{2,1,0:T(8,128)(2,1)} %pack_kv.1), calls=%async_computation.3 | async-start | bytes 9699328 | tf_op jit(solution)/shard_map/all_to_all | solution.py:259
  82.0 16.1 %pack_q.1 = bf16[16,3,192,128]{3,2,1,0:T(8,128)(2,1)} custom-call(s32[6,16,128]{2,1,0:T(8,128)} %get-tuple-element.12.slot_ref.index_ref, bf16[8,256,384]{2,1,0:T(8,128)(2,1)} %copy-done.3), custom_call_target="tpu_custom_call" | custom-call | flops 9663676416 | bytes 4000000 | tf_op jit(solution)/shard_map/pack_q/pallas_call | solution.py:347
  98.1 0.0 copy-start.5
  98.1 55.4 %all-to-all-done.3.in_ref.meta_ref = bf16[16,592,256]{2,1,0:T(8,128)(2,1)} async-done(((bf16[16,592,256]{2,1,0:T(8,128)(2,1)}), bf16[16,592,256]{2,1,0:T(8,128)(2,1)}, u32[]{:S(2)}, u32[]{:S(2)}) %all-to-all-start.3) | async-done | bytes 4849696 | tf_op jit(solution)/shard_map/all_to_all | solution.py:259
  153.5 4.5 %all-to-all-start.1 = ((bf16[16,3,192,128]{3,2,1,0:T(8,128)(2,1)}), bf16[16,3,192,128]{3,2,1,0:T(8,128)(2,1)S(1)}, u32[]{:S(2)}, u32[]{:S(2)}) async-start(bf16[16,3,192,128]{3,2,1,0:T(8,128)(2,1)} %pack_q.1), calls=%async_computation.1 | async-start | bytes 4718592 | tf_op jit(solution)/shard_map/all_to_all | solution.py:259
  158.0 0.0 copy-done.5
  158.0 0.2 copy.13
  158.2 0.2 reshape.35
  158.4 1.0 compare_reduce_fusion
  159.4 0.1 convolution_convert_fusion
  159.5 0.3 select_reduce_fusion.1
  159.8 0.7 copy.16.pick_ref
  160.5 22.0 %unpack_kv.1 = (bf16[16,2,4,128,256]{4,3,2,1,0:T(8,128)(2,1)}, bf16[16,1,4,128,256]{4,3,2,1,0:T(8,128)(2,1)}, s32[3,16,128]{2,1,0:T(8,128)}) custom-call(s32[3,16,4]{2,1,0:T(8,128)} %copy.16.pick_ref, bf16[16,592,256]{2,1,0:T(8,128)(2,1)} %all-to-all-done.3.in_ref.meta_ref, bf16[16,592,256]{2,1,0:T(8,128)(2,1)} %all-to-all-done.3.in_ref.meta_ref), custom_call_target="tpu_custom_call" | custom-call | flops 9663676416 | bytes 18000000 | tf_op jit(solution)/shard_map/unpack_kv/pallas_call | solution.py:364
  182.5 5.6 %all-to-all-done.1.in_ref = bf16[16,3,192,128]{3,2,1,0:T(8,128)(2,1)S(1)} async-done(((bf16[16,3,192,128]{3,2,1,0:T(8,128)(2,1)}), bf16[16,3,192,128]{3,2,1,0:T(8,128)(2,1)S(1)}, u32[]{:S(2)}, u32[]{:S(2)}) %all-to-all-start.1) | async-done | bytes 2359328 | tf_op jit(solution)/shard_map/all_to_all | solution.py:259
  188.1 0.0 copy-start
  188.1 101.8 %all_to_all.45.recv_ref = bf16[16,2,4,128,256]{4,3,2,1,0:T(8,128)(2,1)} all-to-all(bf16[16,2,4,128,256]{4,3,2,1,0:T(8,128)(2,1)} %get-tuple-element.15), channel_id=1, replica_groups=mesh['seq'=16,'head'=8] {'seq'}, dimensions={0} | all-to-all | bytes 16777216 | tf_op jit(solution)/shard_map/all_to_all | solution.py:259
  290.0 0.0 copy-done
  290.0 4.5 %all-to-all-start.5 = ((bf16[16,1,4,128,256]{4,3,2,1,0:T(8,128)(2,1)}), bf16[16,1,4,128,256]{4,3,2,1,0:T(8,128)(2,1)}, u32[]{:S(2)}, u32[]{:S(2)}) async-start(bf16[16,1,4,128,256]{4,3,2,1,0:T(8,128)(2,1)} %get-tuple-element.18), calls=%async_computation.5 | async-start | bytes 8388608 | tf_op jit(solution)/shard_map/all_to_all | solution.py:259
  294.6 0.2 fusion.1
  294.7 0.1 reshape.36
  294.8 0.1 fusion
  294.9 0.1 broadcast_in_dim.30
  295.1 0.3 select_reduce_fusion
  295.4 0.7 reshape.37.fetch_ref
  296.1 15.5 %unpack_q.1.query_ref = bf16[3,2048,128]{2,1,0:T(8,128)(2,1)} custom-call(s32[3,16,128]{2,1,0:T(8,128)} %get-tuple-element.16.index_ref, bf16[16,3,192,128]{3,2,1,0:T(8,128)(2,1)} %copy-done), custom_call_target="tpu_custom_call" | custom-call | flops 9663676416 | bytes 4000000 | tf_op jit(solution)/shard_map/unpack_q/pallas_call | solution.py:399
  311.6 31.3 %attend_0.1 = bf16[16,2,192,128]{3,2,1,0:T(8,128)(2,1)} custom-call(s32[3,16,16]{2,1,0:T(8,128)} %reshape.37.fetch_ref, s32[3,16,128]{2,1,0:T(8,128)} %get-tuple-element.16.index_ref, bf16[3,2048,128]{2,1,0:T(8,128)(2,1)} %unpack_q.1.query_ref, bf16[16,2,4,128,256]{4,3,2,1,0:T(8,128)(2,1)} %all_to_all.45.recv_ref), custom_call_target="tpu_custom_call" | custom-call | flops 4294967296 | bytes 12000000 | tf_op jit(solution)/shard_map/attend_0/pallas_call | solution.py:416
  342.8 6.1 %all-to-all-done.5.recv_ref = bf16[16,1,4,128,256]{4,3,2,1,0:T(8,128)(2,1)} async-done(((bf16[16,1,4,128,256]{4,3,2,1,0:T(8,128)(2,1)}), bf16[16,1,4,128,256]{4,3,2,1,0:T(8,128)(2,1)}, u32[]{:S(2)}, u32[]{:S(2)}) %all-to-all-start.5) | async-done | bytes 4194336 | tf_op jit(solution)/shard_map/all_to_all | solution.py:259
  349.0 6.2 %all-to-all-start.7 = ((bf16[16,2,192,128]{3,2,1,0:T(8,128)(2,1)}), bf16[16,2,192,128]{3,2,1,0:T(8,128)(2,1)S(1)}, u32[]{:S(2)}, u32[]{:S(2)}) async-start(bf16[16,2,192,128]{3,2,1,0:T(8,128)(2,1)} %attend_0.1), calls=%async_computation.7 | async-start | bytes 3145728 | tf_op jit(solution)/shard_map/all_to_all | solution.py:259
  355.1 18.2 %attend_2.1 = bf16[16,1,192,128]{3,2,1,0:T(8,128)(2,1)} custom-call(s32[3,16,16]{2,1,0:T(8,128)} %reshape.37.fetch_ref, s32[3,16,128]{2,1,0:T(8,128)} %get-tuple-element.16.index_ref, bf16[3,2048,128]{2,1,0:T(8,128)(2,1)} %unpack_q.1.query_ref, bf16[16,1,4,128,256]{4,3,2,1,0:T(8,128)(2,1)} %all-to-all-done.5.recv_ref), custom_call_target="tpu_custom_call" | custom-call | flops 2147483648 | bytes 6000000 | tf_op jit(solution)/shard_map/attend_2/pallas_call | solution.py:416
  373.4 1.9 all-to-all-done.7.in_ref
  375.2 0.0 copy-start.2
  375.2 5.4 %all-to-all-start.6 = ((bf16[16,1,192,128]{3,2,1,0:T(8,128)(2,1)}), bf16[16,1,192,128]{3,2,1,0:T(8,128)(2,1)S(1)}, u32[]{:S(2)}, u32[]{:S(2)}) async-start(bf16[16,1,192,128]{3,2,1,0:T(8,128)(2,1)} %attend_2.1), calls=%async_computation.6 | async-start | bytes 1572864 | tf_op jit(solution)/shard_map/all_to_all | solution.py:259
  380.6 0.0 copy-done.2
  380.7 11.0 %final_0.1.refs_0_ = bf16[8,256,384]{2,1,0:T(8,128)(2,1)} custom-call(s32[6,16,128]{2,1,0:T(8,128)} %get-tuple-element.12.slot_ref.index_ref, bf16[16,2,192,128]{3,2,1,0:T(8,128)(2,1)} %copy-done.2), custom_call_target="tpu_custom_call" | custom-call | flops 6442450944 | bytes 2000000 | tf_op jit(solution)/shard_map/final_0/pallas_call | solution.py:444
  391.7 0.9 all-to-all-done.6.in_ref
  392.6 0.0 copy-start.4
  392.6 0.9 copy-done.4
  393.5 6.5 %final_2.1 = bf16[8,256,384]{2,1,0:T(8,128)(2,1)} custom-call(s32[6,16,128]{2,1,0:T(8,128)} %get-tuple-element.12.slot_ref.index_ref, bf16[16,1,192,128]{3,2,1,0:T(8,128)(2,1)} %copy-done.4, bf16[8,256,384]{2,1,0:T(8,128)(2,1)} %final_0.1.refs_0_), custom_call_target="tpu_custom_call", output_to_operand_aliasing={{}: (2, {})} | custom-call | flops 3221225472 | bytes 2000000 | tf_op jit(solution)/shard_map/final_2/pallas_call | solution.py:444
  400.0 27.6 %all_to_all.46 = bf16[8,256,384]{2,1,0:T(8,128)(2,1)S(1)} all-to-all(bf16[8,256,384]{2,1,0:T(8,128)(2,1)} %final_2.1), channel_id=1, replica_groups=mesh['seq'=16,'head'=8] {'head'}, dimensions={0} | all-to-all | bytes 3145728 | tf_op jit(solution)/shard_map/all_to_all | solution.py:259
  427.6 0.7 copy.17
  428.4 1.7 copy.18
  (5 shorter events, 0.0 us)
Async XLA Ops:
  4.3 6.0 %copy-start.6 = (s32[3,2048]{1,0:T(4,128)S(1)}, s32[3,2048]{1,0:T(4,128)}, u32[]{:S(2)}) copy-start(s32[3,2048]{1,0:T(4,128)} %param.10) | copy-start | bytes 73732
  4.3 6.0 %copy-start.7 = (s32[3,2048]{1,0:T(4,128)S(1)}, s32[3,2048]{1,0:T(4,128)}, u32[]{:S(2)}) copy-start(s32[3,2048]{1,0:T(4,128)} %param.9) | copy-start | bytes 73732
  4.3 6.6 %copy-start.1 = (bf16[256,3072]{1,0:T(8,128)(2,1)S(1)}, bf16[256,3072]{1,0:T(8,128)(2,1)}, u32[]{:S(2)}) copy-start(bf16[256,3072]{1,0:T(8,128)(2,1)} %param.6) | copy-start | bytes 4718596
  4.3 43.6 %all-to-all-start.2 = ((bf16[8,2,256,384]{3,2,1,0:T(8,128)(2,1)}), bf16[8,2,256,384]{3,2,1,0:T(8,128)(2,1)}, u32[]{:S(2)}, u32[]{:S(2)}) async-start(bf16[8,2,256,384]{3,2,1,0:T(8,128)(2,1)} %split_kv.1), calls=%async_computation.2 | async-start | bytes 6291456 | tf_op jit(solution)/shard_map/all_to_all | solution.py:259
  47.9 25.1 %all-to-all-start = ((bf16[8,256,384]{2,1,0:T(8,128)(2,1)}), bf16[8,256,384]{2,1,0:T(8,128)(2,1)S(1)}, u32[]{:S(2)}, u32[]{:S(2)}) async-start(bf16[8,256,384]{2,1,0:T(8,128)(2,1)} %bitcast.2), calls=%async_computation | async-start | bytes 3145728 | tf_op jit(solution)/shard_map/all_to_all | solution.py:259
  73.0 1.1 copy-start.3
  74.1 79.4 %all-to-all-start.3 = ((bf16[16,592,256]{2,1,0:T(8,128)(2,1)}), bf16[16,592,256]{2,1,0:T(8,128)(2,1)}, u32[]{:S(2)}, u32[]{:S(2)}) async-start(bf16[16,592,256]{2,1,0:T(8,128)(2,1)} %pack_kv.1), calls=%async_computation.3 | async-start | bytes 9699328 | tf_op jit(solution)/shard_map/all_to_all | solution.py:259
  98.1 59.9 %copy-start.5 = (s32[3,256,16]{1,2,0:T(8,128)S(1)}, s32[3,256,16]{1,2,0:T(8,128)}, u32[]{:S(2)}) copy-start(s32[3,256,16]{1,2,0:T(8,128)} %param.11) | copy-start | bytes 147460
  153.5 34.6 %all-to-all-start.1 = ((bf16[16,3,192,128]{3,2,1,0:T(8,128)(2,1)}), bf16[16,3,192,128]{3,2,1,0:T(8,128)(2,1)S(1)}, u32[]{:S(2)}, u32[]{:S(2)}) async-start(bf16[16,3,192,128]{3,2,1,0:T(8,128)(2,1)} %pack_q.1), calls=%async_computation.1 | async-start | bytes 4718592 | tf_op jit(solution)/shard_map/all_to_all | solution.py:259
  188.1 101.8 %copy-start = (bf16[16,3,192,128]{3,2,1,0:T(8,128)(2,1)}, bf16[16,3,192,128]{3,2,1,0:T(8,128)(2,1)S(1)}, u32[]{:S(2)}) copy-start(bf16[16,3,192,128]{3,2,1,0:T(8,128)(2,1)S(1)} %all-to-all-done.1.in_ref) | copy-start | bytes 7077892
  290.0 59.0 %all-to-all-start.5 = ((bf16[16,1,4,128,256]{4,3,2,1,0:T(8,128)(2,1)}), bf16[16,1,4,128,256]{4,3,2,1,0:T(8,128)(2,1)}, u32[]{:S(2)}, u32[]{:S(2)}) async-start(bf16[16,1,4,128,256]{4,3,2,1,0:T(8,128)(2,1)} %get-tuple-element.18), calls=%async_computation.5 | async-start | bytes 8388608 | tf_op jit(solution)/shard_map/all_to_all | solution.py:259
  349.0 26.3 %all-to-all-start.7 = ((bf16[16,2,192,128]{3,2,1,0:T(8,128)(2,1)}), bf16[16,2,192,128]{3,2,1,0:T(8,128)(2,1)S(1)}, u32[]{:S(2)}, u32[]{:S(2)}) async-start(bf16[16,2,192,128]{3,2,1,0:T(8,128)(2,1)} %attend_0.1), calls=%async_computation.7 | async-start | bytes 3145728 | tf_op jit(solution)/shard_map/all_to_all | solution.py:259
  375.2 5.4 %copy-start.2 = (bf16[16,2,192,128]{3,2,1,0:T(8,128)(2,1)}, bf16[16,2,192,128]{3,2,1,0:T(8,128)(2,1)S(1)}, u32[]{:S(2)}) copy-start(bf16[16,2,192,128]{3,2,1,0:T(8,128)(2,1)S(1)} %all-to-all-done.7.in_ref) | copy-start | bytes 4718596
  375.2 17.4 %all-to-all-start.6 = ((bf16[16,1,192,128]{3,2,1,0:T(8,128)(2,1)}), bf16[16,1,192,128]{3,2,1,0:T(8,128)(2,1)S(1)}, u32[]{:S(2)}, u32[]{:S(2)}) async-start(bf16[16,1,192,128]{3,2,1,0:T(8,128)(2,1)} %attend_2.1), calls=%async_computation.6 | async-start | bytes 1572864 | tf_op jit(solution)/shard_map/all_to_all | solution.py:259
  392.6 0.9 copy-start.4

commit v4 on v3

--- a/solution.py
+++ b/solution.py
@@ -93,10 +93,34 @@
 
 def split_kernel(key_ref, value_ref, out_ref):
     parts, _, _, width = out_ref.shape
+    stride = key_ref.shape[1] // parts
     for part in range(parts):
-        columns = slice(part * width, (part + 1) * width)
+        columns = slice(part * stride, part * stride + width)
         out_ref[part, 0] = key_ref[:, columns]
         out_ref[part, 1] = value_ref[:, columns]
+
+
+def split_rest_kernel(me_ref, key_ref, value_ref, query_ref, *out_refs):
+    parts = len(out_refs) // 2
+    stride = key_ref.shape[1] // parts
+    me = me_ref[0]
+    for k in range(parts):
+        start = jnp.bitwise_xor(me, k) * stride
+        last = pl.ds(pl.multiple_of(start + stride - LANES, LANES), LANES)
+        out_refs[k][0] = key_ref[:, last]
+        out_refs[k][1] = value_ref[:, last]
+        out_refs[parts + k][...] = query_ref[:, pl.ds(pl.multiple_of(start, LANES), stride)]
+
+
+def partner_order(me, index, parts):
+    each = index.shape[0] // parts
+    row = iota(index.shape, 0)
+    rows = []
+    for k in range(parts):
+        for j in range(each):
+            wanted = jnp.bitwise_xor(me, k) * each + j
+            rows.append(jnp.sum(jnp.where(row == wanted, index, 0), axis=0, keepdims=True))
+    return jnp.concatenate(rows, axis=0)
 
 
 def pack_kv_kernel(slot_ref, count_ref, key_ref, value_ref, out_ref):
@@ -104,7 +128,7 @@
     heads = pl.num_programs(0)
     groups, rows, _ = out_ref.shape
     of_heads = count_ref.shape[0] // 2
-    capacity = (rows - META) // of_heads
+    capacity = (rows - META) // (of_heads - 1)
     tokens = key_ref.shape[0] * key_ref.shape[2]
     keys = key_ref[:, 0].reshape(tokens, LANES)
     values = value_ref[:, 0].reshape(tokens, LANES)
@@ -124,18 +148,33 @@
             for h in range(of_heads):
                 counts = count_ref[(1 - side) * of_heads + h]
                 block = jnp.where(row == h, counts[:, None, :], block)
-            out_ref[:, of_heads * capacity :, side * LANES : (side + 1) * LANES] = block.astype(BF16)
-
-
-def pack_q_kernel(slot_ref, query_ref, out_ref):
+            out_ref[:, rows - META :, side * LANES : (side + 1) * LANES] = block.astype(BF16)
+
+
+def pack_last_kernel(me_ref, slot_ref, *refs):
+    *part_refs, out_ref = refs
+    groups, capacity, _ = out_ref.shape
+    index = partner_order(me_ref[0], slot_ref[0], len(part_refs))
+    keys = jnp.concatenate([ref[0] for ref in part_refs], axis=0)
+    values = jnp.concatenate([ref[1] for ref in part_refs], axis=0)
+
+    def store(i, block):
+        out_ref[pl.ds(2 * i, 2)] = block.reshape(2, capacity, 2 * LANES)
+
+    both = jnp.concatenate([keys, values], axis=1)
+    spread(index, both, store, groups * capacity, 2 * capacity)
+
+
+def pack_q_kernel(me_ref, slot_ref, *refs):
+    *part_refs, out_ref = refs
     groups, _, capacity, _ = out_ref.shape
-    tokens = query_ref.shape[0] * query_ref.shape[1]
+    index = partner_order(me_ref[0], slot_ref[0], len(part_refs))
+    queries = jnp.concatenate([ref[...] for ref in part_refs], axis=0)
 
     def store(i, block):
         out_ref[pl.ds(2 * i, 2), 0] = block.reshape(2, capacity, LANES)
 
-    queries = query_ref[...].reshape(tokens, LANES)
-    spread(slot_ref[0], queries, store, groups * capacity, 2 * capacity)
+    spread(index, queries, store, groups * capacity, 2 * capacity)
 
 
 def sources(counts, capacity):
@@ -156,7 +195,15 @@
 
 
 def unpack_kv_kernel(
-    pick_ref, in_ref, meta_ref, first_ref, last_ref, query_source_ref, wide_ref, sorted_ref
+    pick_ref,
+    in_ref,
+    last_in_ref,
+    meta_ref,
+    first_ref,
+    last_ref,
+    query_source_ref,
+    wide_ref,
+    sorted_ref,
 ):
     head = pl.program_id(0)
     heads = pl.num_programs(0)
@@ -164,14 +211,15 @@
     row = iota(meta_ref.shape, 1)
     counts = jnp.sum(jnp.where(row == head, meta_ref[...].astype(F32), 0.0), axis=1)
     query_source_ref[0] = sources(counts[:, LANES:], capacity)
-    packed = in_ref[...].reshape(groups * capacity, 2 * LANES)
+    key_source = sources(counts[:, :LANES], capacity)
 
     def store(i, block):
         sorted_ref[pl.ds(4 * i, 4)] = block.reshape(4, BLOCK, 2 * LANES)
 
-    collect(sources(counts[:, :LANES], capacity), packed, wide_ref, store, 4 * BLOCK)
-
-    def send(out_ref):
+    def send(packed_ref, out_ref):
+        packed = packed_ref[...].reshape(groups * capacity, 2 * LANES)
+        collect(key_source, packed, wide_ref, store, 4 * BLOCK)
+
         def copy(i, carry):
             for j in range(KCAP):
                 out_ref[i, 0, j] = sorted_ref[pick_ref[head, i, j]]
@@ -181,11 +229,11 @@
 
     @pl.when(head < heads - 1)
     def _():
-        send(first_ref)
+        send(in_ref, first_ref)
 
     @pl.when(head == heads - 1)
     def _():
-        send(last_ref)
+        send(last_in_ref, last_ref)
 
 
 def unpack_q_kernel(index_ref, in_ref, out_ref, wide_ref):
@@ -292,22 +340,36 @@
     width = heads * LANES
     chunks = tokens // LANES
 
-    def by_part(rows):
-        return rows.reshape(part, parts, width).transpose(1, 0, 2)
+    most = heads - 1
+    me = lax.axis_index("head").astype(I32).reshape(1)
 
     kv_sent = pl.pallas_call(
         split_kernel,
         grid=(4,),
         in_specs=[pl.BlockSpec((part // 4, parts * width), lambda i: (i, 0))] * 2,
-        out_specs=pl.BlockSpec((parts, 2, part // 4, width), lambda i: (0, 0, i, 0)),
-        out_shape=shape_of((parts, 2, part, width), BF16),
+        out_specs=pl.BlockSpec((parts, 2, part // 4, most * LANES), lambda i: (0, 0, i, 0)),
+        out_shape=shape_of((parts, 2, part, most * LANES), BF16),
         compiler_params=params(),
         cost_estimate=cost(0, 6e6),
         name="split_kv",
     )(key_rows, value_rows)
     kv_tok = exchange(kv_sent, "head")
-    q_tok = exchange(by_part(query_rows), "head")
-
+    last_parts = [shape_of((2, part, LANES), BF16)] * parts
+    query_parts = [shape_of((part, width), BF16)] * parts
+    pieces = pl.pallas_call(
+        split_rest_kernel,
+        grid_spec=pltpu.PrefetchScalarGridSpec(
+            num_scalar_prefetch=1,
+            grid=(2,),
+            in_specs=[pl.BlockSpec((part // 2, parts * width), lambda i, me: (i, 0))] * 3,
+            out_specs=[pl.BlockSpec((2, part // 2, LANES), lambda i, me: (0, i, 0))] * parts
+            + [pl.BlockSpec((part // 2, width), lambda i, me: (i, 0))] * parts,
+        ),
+        out_shape=last_parts + query_parts,
+        compiler_params=params(),
+        cost_estimate=cost(0, 6e6),
+        name="split_rest",
+    )(me, key_rows, value_rows, query_rows)
     ids = jnp.concatenate([query_cluster, key_cluster], axis=0).reshape(2 * heads, chunks, LANES)
     slot, count = pl.pallas_call(
         functools.partial(slot_kernel, groups=groups, owned=owned, capacity=capacity),
@@ -327,36 +389,65 @@
     )(ids)
     pick, fetch = tables(cluster_pairs, my_index, groups)
 
+    *pieces, kv_tok = lax.optimization_barrier((*pieces, kv_tok))
     kv_packed = pl.pallas_call(
         pack_kv_kernel,
-        grid=(heads,),
+        grid=(most,),
         in_specs=[
             pl.BlockSpec((1, chunks, LANES), lambda h: (h + heads, 0, 0)),
             pl.BlockSpec((2 * heads, groups, LANES), lambda h: (0, 0, 0)),
             pl.BlockSpec((parts, 1, part, LANES), lambda h: (0, 0, 0, h)),
             pl.BlockSpec((parts, 1, part, LANES), lambda h: (0, 1, 0, h)),
         ],
-        out_specs=pl.BlockSpec((groups, heads * capacity + META, 2 * LANES), lambda h: (0, 0, 0)),
-        out_shape=shape_of((groups, heads * capacity + META, 2 * LANES), BF16),
-        compiler_params=params(),
-        cost_estimate=cost(heads * 16.0 * slots * tokens * LANES, 8e6),
+        out_specs=pl.BlockSpec((groups, most * capacity + META, 2 * LANES), lambda h: (0, 0, 0)),
+        out_shape=shape_of((groups, most * capacity + META, 2 * LANES), BF16),
+        compiler_params=params(),
+        cost_estimate=cost(most * 4.0 * slots * tokens * LANES, 8e6),
         name="pack_kv",
     )(slot, count, kv_tok, kv_tok)
     kv_recv = exchange(kv_packed, "seq")
 
+    def to_partner(array, k):
+        return lax.ppermute(array, "head", [(i, i ^ k) for i in range(parts)])
+
+    *pieces, _ = lax.optimization_barrier((*pieces, kv_packed))
+    last_tok = [to_partner(piece, k) if k else piece for k, piece in enumerate(pieces[:parts])]
+    both = lax.optimization_barrier((*last_tok, *pieces[parts:]))
+    last_tok, q_sent = both[:parts], both[parts:]
+    q_tok = [to_partner(piece, k) if k else piece for k, piece in enumerate(q_sent)]
+
+    last_packed = pl.pallas_call(
+        pack_last_kernel,
+        grid_spec=pltpu.PrefetchScalarGridSpec(
+            num_scalar_prefetch=1,
+            grid=(1,),
+            in_specs=[pl.BlockSpec((1, chunks, LANES), lambda i, me: (2 * heads - 1, 0, 0))]
+            + [pl.BlockSpec((2, part, LANES), lambda i, me: (0, 0, 0))] * parts,
+            out_specs=pl.BlockSpec((groups, capacity, 2 * LANES), lambda i, me: (0, 0, 0)),
+        ),
+        out_shape=shape_of((groups, capacity, 2 * LANES), BF16),
+        compiler_params=params(),
+        cost_estimate=cost(4.0 * slots * tokens * LANES, 3e6),
+        name="pack_last",
+    )(me, slot, *last_tok)
+    last_packed, kv_recv, *q_tok = lax.optimization_barrier((last_packed, kv_recv, *q_tok))
+    last_kv_recv = exchange(last_packed, "seq")
+
     q_packed = pl.pallas_call(
         pack_q_kernel,
-        grid=(heads,),
-        in_specs=[
-            pl.BlockSpec((1, chunks, LANES), lambda h: (h, 0, 0)),
-            pl.BlockSpec((parts, part, LANES), lambda h: (0, 0, h)),
-        ],
-        out_specs=pl.BlockSpec((groups, 1, capacity, LANES), lambda h: (0, h, 0, 0)),
+        grid_spec=pltpu.PrefetchScalarGridSpec(
+            num_scalar_prefetch=1,
+            grid=(heads,),
+            in_specs=[pl.BlockSpec((1, chunks, LANES), lambda h, me: (h, 0, 0))]
+            + [pl.BlockSpec((part, LANES), lambda h, me: (0, h))] * parts,
+            out_specs=pl.BlockSpec((groups, 1, capacity, LANES), lambda h, me: (0, h, 0, 0)),
+        ),
         out_shape=shape_of((groups, heads, capacity, LANES), BF16),
         compiler_params=params(),
         cost_estimate=cost(heads * 4.0 * slots * tokens * LANES, 4e6),
         name="pack_q",
-    )(slot, q_tok)
+    )(me, slot, *q_tok)
+    q_packed, last_kv_recv = lax.optimization_barrier((q_packed, last_kv_recv))
     q_recv = exchange(q_packed, "seq")
 
     splits = ((0, heads - 1), (heads - 1, 1))
@@ -367,9 +458,12 @@
             num_scalar_prefetch=1,
             grid=(heads,),
             in_specs=[
-                pl.BlockSpec((groups, capacity, 2 * LANES), lambda h, pick: (0, h, 0)),
                 pl.BlockSpec(
-                    (groups, META, 2 * LANES), lambda h, pick: (0, heads * capacity // META, 0)
+                    (groups, capacity, 2 * LANES), lambda h, pick: (0, jnp.minimum(h, most - 1), 0)
+                ),
+                pl.BlockSpec((groups, capacity, 2 * LANES), lambda h, pick: (0, 0, 0)),
+                pl.BlockSpec(
+                    (groups, META, 2 * LANES), lambda h, pick: (0, most * capacity // META, 0)
                 ),
             ],
             out_specs=[
@@ -390,7 +484,7 @@
         compiler_params=params(),
         cost_estimate=cost(heads * 4.0 * slots * tokens * LANES, heads * 6e6),
         name="unpack_kv",
-    )(pick, kv_recv, kv_recv)
+    )(pick, kv_recv, last_kv_recv, kv_recv)
     first_recv = exchange(first_sent, "seq")
     last_recv = exchange(last_sent, "seq")
     received = (first_recv, last_recv)

time: 431 us -> 417 us (0.968)
  waiting for transfers between devices: 96.5 us -> 58.5 us
  starting transfers between devices: 38.7 us -> 58.9 us
  Pallas kernels: 154 us -> 160 us
    all_to_all x7, waiting for transfers between devices: 96.5 us -> 38.1 us  [exchange(): return lax.all_to_all(array, axis, split_axis=0, concat_axis=0, tiled=True)]
    ppermute x0 -> x14, waiting for transfers between devices: none -> 20.4 us  [to_partner(): return lax.ppermute(array, 'head', [(i, i ^ k) for i in range(parts)])]
    ppermute x0 -> x14, starting transfers between devices: none -> 18.4 us  [to_partner(): return lax.ppermute(array, 'head', [(i, i ^ k) for i in range(parts)])]
    pallas_call x2 -> x4, Pallas kernels: 33.6 us -> 39.2 us  [the longest x1 16.1 us: per_device(): pl.pallas_call(pack_q_kernel, grid_spec=pltpu.PrefetchScalarGridSpec(num_...]
  transfers between devices with their start and end apart: 7 -> 21, of which waited for: 7 -> 16; matrix products, arithmetic and copies ran while one was open for 2% -> 1% of each run, Pallas kernels for 33% -> 33%
where the time goes in v4:
time: 417 us; the launch traced here: 416 us
  Pallas kernels  160 us (38%)
  blocking collectives  128 us (31%)
  starting transfers between devices  58.9 us (14%)
  waiting for transfers between devices  58.5 us (14%)
  local copies, waits for them, and re-layouts  8.84 us (2%)
    all_to_all x2, blocking collectives, exchange(): return lax.all_to_all(array, axis, split_axis=0, concat_axis=0, tiled=True)  128 us
    pallas_call x2, Pallas kernels, per_device(): pl.pallas_call(functools.partial(attend_kernel, first=first), grid_spec=p...  49.5 us
    all_to_all x7, starting transfers between devices, exchange(): return lax.all_to_all(array, axis, split_axis=0, concat_axis=0, tiled=True)  40.5 us
    all_to_all x7, waiting for transfers between devices, exchange(): return lax.all_to_all(array, axis, split_axis=0, concat_axis=0, tiled=True)  38.1 us
    pallas_call x1, Pallas kernels, per_device(): pl.pallas_call(unpack_kv_kernel, grid_spec=pltpu.PrefetchScalarGridSpec(n...  22.5 us
    ppermute x14, waiting for transfers between devices, to_partner(): return lax.ppermute(array, 'head', [(i, i ^ k) for i in range(parts)])  20.4 us
    ppermute x14, starting transfers between devices, to_partner(): return lax.ppermute(array, 'head', [(i, i ^ k) for i in range(parts)])  18.4 us
    pallas_call x2, Pallas kernels, per_device(): pl.pallas_call(final_kernel, grid=(count_heads,), in_specs=[pl.BlockSpec(...  17.5 us
  transfers between devices with their start and end apart: 21, of which 16 were waited for; matrix products, arithmetic and copies ran while one was open for 1% of the time, Pallas kernels for 33%

profile of v4, /device:TPU:1, one launch (start us, length us, event | category | flops | bytes accessed | tf_op | source)
XLA Modules:
  0.0 415.8 jit_solution(1759781850153570022)
XLA Ops:
  0.0 3.9 split_kv.1
  3.9 5.9 %all-to-all-start = ((bf16[8,2,256,256]{3,2,1,0:T(8,128)(2,1)}), bf16[8,2,256,256]{3,2,1,0:T(8,128)(2,1)S(1)}, u32[]{:S(2)}, u32[]{:S(2)}) async-start(bf16[8,2,256,256]{3,2,1,0:T(8,128)(2,1)} %split_kv.1), calls=%async_computation | async-start | bytes 4194304 | tf_op jit(solution)/shard_map/all_to_all | solution.py:307
  9.9 0.6 copy.19
  10.5 3.6 split_rest.1
  14.2 11.5 %slots.1 = (s32[6,16,128]{2,1,0:T(8,128)}, f32[6,16,128]{2,1,0:T(8,128)}) custom-call(s32[6,16,128]{2,1,0:T(8,128)} %bitcast.19), custom_call_target="tpu_custom_call" | custom-call | flops 6000000000 | bytes 1000000 | tf_op jit(solution)/shard_map/slots/pallas_call | solution.py:374
  25.7 10.6 %all-to-all-done.key_ref.value_ref = bf16[8,2,256,256]{3,2,1,0:T(8,128)(2,1)S(1)} async-done(((bf16[8,2,256,256]{3,2,1,0:T(8,128)(2,1)}), bf16[8,2,256,256]{3,2,1,0:T(8,128)(2,1)S(1)}, u32[]{:S(2)}, u32[]{:S(2)}) %all-to-all-start) | async-done | bytes 2097184 | tf_op jit(solution)/shard_map/all_to_all | solution.py:307
  36.2 1.4 copy-done.2
  37.6 12.3 %pack_kv.1 = bf16[16,400,256]{2,1,0:T(8,128)(2,1)} custom-call(s32[6,16,128]{2,1,0:T(8,128)} %get-tuple-element.89.slot_ref.index_ref, f32[6,16,128]{2,1,0:T(8,128)} %get-tuple-element.122.count_ref, bf16[8,2,256,256]{3,2,1,0:T(8,128)(2,1)} %copy-done.2, bf16[8,2,256,256]{3,2,1,0:T(8,128)(2,1)} %copy-done.2), custom_call_target="tpu_custom_call" | custom-call | flops 6442450944 | bytes 8000000 | tf_op jit(solution)/shard_map/pack_kv/pallas_call | solution.py:393
  49.9 7.9 %all-to-all-start.1 = ((bf16[16,400,256]{2,1,0:T(8,128)(2,1)}), bf16[16,400,256]{2,1,0:T(8,128)(2,1)S(1)}, u32[]{:S(2)}, u32[]{:S(2)}) async-start(bf16[16,400,256]{2,1,0:T(8,128)(2,1)} %pack_kv.1), calls=%async_computation.1 | async-start | bytes 6553600 | tf_op jit(solution)/shard_map/all_to_all | solution.py:307
  57.8 1.2 collective-permute-start
  59.0 0.3 collective-permute-start.1
  59.3 1.4 collective-permute-start.2
  60.8 0.4 collective-permute-start.3
  61.2 2.9 collective-permute-start.4
  64.1 0.9 collective-permute-start.5
  64.9 2.0 collective-permute-start.6
  67.0 1.1 collective-permute-done.2.refs_3_
  68.1 2.5 collective-permute-done.3.refs_4_
  70.6 3.3 collective-permute-done.4.refs_5_
  73.8 2.2 collective-permute-done.5.refs_6_
  76.1 3.1 collective-permute-done.6.refs_7_
  79.3 2.0 collective-permute-start.9
  81.3 0.6 collective-permute-start.10
  81.9 2.4 collective-permute-start.11
  84.3 1.0 collective-permute-start.12
  85.3 0.3 collective-permute-done.8.refs_2_
  85.6 0.7 copy-done.10
  86.3 3.1 collective-permute-start.13
  89.4 7.1 %pack_last.1 = bf16[16,192,256]{2,1,0:T(8,128)(2,1)} custom-call(s32[1]{0:T(128)} %bitcast.1.me_ref, s32[6,16,128]{2,1,0:T(8,128)} %get-tuple-element.89.slot_ref.index_ref, bf16[2,256,128]{2,1,0:T(8,128)(2,1)} %get-tuple-element.140.refs_0_, bf16[2,256,128]{2,1,0:T(8,128)(2,1)} %copy-done.15, bf16[2,256,128]{2,1,0:T(8,128)(2,1)} %copy-done.16, ...), custom_call_target="tpu_custom_call" | custom-call | flops 3221225472 | bytes 3000000 | tf_op jit(solution)/shard_map/pack_last/pallas_call | solution.py:419
  96.6 3.0 collective-permute-done.11.refs_5_
  99.6 0.6 collective-permute-done.12.refs_6_
  100.3 0.7 copy-done.14
  101.0 4.3 %collective-permute-done.13.refs_7_ = bf16[256,384]{1,0:T(8,128)(2,1)} collective-permute-done((bf16[256,384]{1,0:T(8,128)(2,1)S(1)}, bf16[256,384]{1,0:T(8,128)(2,1)}, u32[]{:S(2)}, u32[]{:S(2)}) %collective-permute-start.13) | collective-permute-done | bytes 196640 | tf_op jit(solution)/shard_map/ppermute | solution.py:411
  105.3 0.5 all-to-all-done.1.in_ref.meta_ref
  105.8 6.2 %all-to-all-start.2 = ((bf16[16,192,256]{2,1,0:T(8,128)(2,1)}), bf16[16,192,256]{2,1,0:T(8,128)(2,1)}, u32[]{:S(2)}, u32[]{:S(2)}) async-start(bf16[16,192,256]{2,1,0:T(8,128)(2,1)} %pack_last.1), calls=%async_computation.2 | async-start | bytes 3145728 | tf_op jit(solution)/shard_map/all_to_all | solution.py:307
  112.0 16.1 %pack_q.1 = bf16[16,3,192,128]{3,2,1,0:T(8,128)(2,1)} custom-call(s32[1]{0:T(128)} %bitcast.1.me_ref, s32[6,16,128]{2,1,0:T(8,128)} %get-tuple-element.89.slot_ref.index_ref, bf16[256,384]{1,0:T(8,128)(2,1)} %get-tuple-element.156.refs_0_, bf16[256,384]{1,0:T(8,128)(2,1)} %copy-done.9, bf16[256,384]{1,0:T(8,128)(2,1)} %copy-done.10, ...), custom_call_target="tpu_custom_call" | custom-call | flops 9663676416 | bytes 4000000 | tf_op jit(solution)/shard_map/pack_q/pallas_call | solution.py:436
  128.1 9.6 %all-to-all-done.2.last_in_ref = bf16[16,192,256]{2,1,0:T(8,128)(2,1)} async-done(((bf16[16,192,256]{2,1,0:T(8,128)(2,1)}), bf16[16,192,256]{2,1,0:T(8,128)(2,1)}, u32[]{:S(2)}, u32[]{:S(2)}) %all-to-all-start.2) | async-done | bytes 1572896 | tf_op jit(solution)/shard_map/all_to_all | solution.py:307
  137.7 3.9 all-to-all-start.3
  141.7 0.2 copy.11
  141.8 0.2 reshape.35
  142.0 1.0 compare_reduce_fusion
  143.2 0.3 select_reduce_fusion.1
  143.5 0.7 copy.12.pick_ref
  144.2 22.5 %unpack_kv.1 = (bf16[16,2,4,128,256]{4,3,2,1,0:T(8,128)(2,1)}, bf16[16,1,4,128,256]{4,3,2,1,0:T(8,128)(2,1)}, s32[3,16,128]{2,1,0:T(8,128)}) custom-call(s32[3,16,4]{2,1,0:T(8,128)} %copy.12.pick_ref, bf16[16,400,256]{2,1,0:T(8,128)(2,1)} %copy-done, bf16[16,192,256]{2,1,0:T(8,128)(2,1)} %all-to-all-done.2.last_in_ref, bf16[16,400,256]{2,1,0:T(8,128)(2,1)} %copy-done), custom_call_target="tpu_custom_call" | custom-call | flops 9663676416 | bytes 18000000 | tf_op jit(solution)/shard_map/unpack_kv/pallas_call | solution.py:455
  166.7 8.7 %all-to-all-done.3.in_ref = bf16[16,3,192,128]{3,2,1,0:T(8,128)(2,1)S(1)} async-done(((bf16[16,3,192,128]{3,2,1,0:T(8,128)(2,1)}), bf16[16,3,192,128]{3,2,1,0:T(8,128)(2,1)S(1)}, u32[]{:S(2)}, u32[]{:S(2)}) %all-to-all-start.3) | async-done | bytes 2359328 | tf_op jit(solution)/shard_map/all_to_all | solution.py:307
  175.3 100.3 %all_to_all.45.recv_ref = bf16[16,2,4,128,256]{4,3,2,1,0:T(8,128)(2,1)} all-to-all(bf16[16,2,4,128,256]{4,3,2,1,0:T(8,128)(2,1)} %get-tuple-element.169), channel_id=1, replica_groups=mesh['seq'=16,'head'=8] {'seq'}, dimensions={0} | all-to-all | bytes 16777216 | tf_op jit(solution)/shard_map/all_to_all | solution.py:307
  275.6 4.5 %all-to-all-start.5 = ((bf16[16,1,4,128,256]{4,3,2,1,0:T(8,128)(2,1)}), bf16[16,1,4,128,256]{4,3,2,1,0:T(8,128)(2,1)}, u32[]{:S(2)}, u32[]{:S(2)}) async-start(bf16[16,1,4,128,256]{4,3,2,1,0:T(8,128)(2,1)} %get-tuple-element.172), calls=%async_computation.5 | async-start | bytes 8388608 | tf_op jit(solution)/shard_map/all_to_all | solution.py:307
  280.2 0.2 fusion.1
  280.7 0.3 select_reduce_fusion
  281.0 0.7 reshape.37.fetch_ref
  281.7 15.5 %unpack_q.1.query_ref = bf16[3,2048,128]{2,1,0:T(8,128)(2,1)} custom-call(s32[3,16,128]{2,1,0:T(8,128)} %get-tuple-element.170.index_ref, bf16[16,3,192,128]{3,2,1,0:T(8,128)(2,1)} %copy-done.1), custom_call_target="tpu_custom_call" | custom-call | flops 9663676416 | bytes 4000000 | tf_op jit(solution)/shard_map/unpack_q/pallas_call | solution.py:493
  297.2 31.3 %attend_0.1 = bf16[16,2,192,128]{3,2,1,0:T(8,128)(2,1)} custom-call(s32[3,16,16]{2,1,0:T(8,128)} %reshape.37.fetch_ref, s32[3,16,128]{2,1,0:T(8,128)} %get-tuple-element.170.index_ref, bf16[3,2048,128]{2,1,0:T(8,128)(2,1)} %unpack_q.1.query_ref, bf16[16,2,4,128,256]{4,3,2,1,0:T(8,128)(2,1)} %all_to_all.45.recv_ref), custom_call_target="tpu_custom_call" | custom-call | flops 4294967296 | bytes 12000000 | tf_op jit(solution)/shard_map/attend_0/pallas_call | solution.py:510
  328.5 5.3 %all-to-all-done.5.recv_ref = bf16[16,1,4,128,256]{4,3,2,1,0:T(8,128)(2,1)} async-done(((bf16[16,1,4,128,256]{4,3,2,1,0:T(8,128)(2,1)}), bf16[16,1,4,128,256]{4,3,2,1,0:T(8,128)(2,1)}, u32[]{:S(2)}, u32[]{:S(2)}) %all-to-all-start.5) | async-done | bytes 4194336 | tf_op jit(solution)/shard_map/all_to_all | solution.py:307
  333.8 6.7 %all-to-all-start.7 = ((bf16[16,2,192,128]{3,2,1,0:T(8,128)(2,1)}), bf16[16,2,192,128]{3,2,1,0:T(8,128)(2,1)S(1)}, u32[]{:S(2)}, u32[]{:S(2)}) async-start(bf16[16,2,192,128]{3,2,1,0:T(8,128)(2,1)} %attend_0.1), calls=%async_computation.7 | async-start | bytes 3145728 | tf_op jit(solution)/shard_map/all_to_all | solution.py:307
  340.5 18.3 %attend_2.1 = bf16[16,1,192,128]{3,2,1,0:T(8,128)(2,1)} custom-call(s32[3,16,16]{2,1,0:T(8,128)} %reshape.37.fetch_ref, s32[3,16,128]{2,1,0:T(8,128)} %get-tuple-element.170.index_ref, bf16[3,2048,128]{2,1,0:T(8,128)(2,1)} %unpack_q.1.query_ref, bf16[16,1,4,128,256]{4,3,2,1,0:T(8,128)(2,1)} %all-to-all-done.5.recv_ref), custom_call_target="tpu_custom_call" | custom-call | flops 2147483648 | bytes 6000000 | tf_op jit(solution)/shard_map/attend_2/pallas_call | solution.py:510
  358.7 2.1 all-to-all-done.7.in_ref
  360.8 5.4 %all-to-all-start.6 = ((bf16[16,1,192,128]{3,2,1,0:T(8,128)(2,1)}), bf16[16,1,192,128]{3,2,1,0:T(8,128)(2,1)S(1)}, u32[]{:S(2)}, u32[]{:S(2)}) async-start(bf16[16,1,192,128]{3,2,1,0:T(8,128)(2,1)} %attend_2.1), calls=%async_computation.6 | async-start | bytes 1572864 | tf_op jit(solution)/shard_map/all_to_all | solution.py:307
  366.2 11.0 %final_0.1.refs_0_ = bf16[8,256,384]{2,1,0:T(8,128)(2,1)} custom-call(s32[6,16,128]{2,1,0:T(8,128)} %get-tuple-element.89.slot_ref.index_ref, bf16[16,2,192,128]{3,2,1,0:T(8,128)(2,1)} %copy-done.3), custom_call_target="tpu_custom_call" | custom-call | flops 6442450944 | bytes 2000000 | tf_op jit(solution)/shard_map/final_0/pallas_call | solution.py:538
  377.2 1.3 all-to-all-done.6.in_ref
  378.5 0.9 copy-done.4
  379.4 6.5 %final_2.1 = bf16[8,256,384]{2,1,0:T(8,128)(2,1)} custom-call(s32[6,16,128]{2,1,0:T(8,128)} %get-tuple-element.89.slot_ref.index_ref, bf16[16,1,192,128]{3,2,1,0:T(8,128)(2,1)} %copy-done.4, bf16[8,256,384]{2,1,0:T(8,128)(2,1)} %final_0.1.refs_0_), custom_call_target="tpu_custom_call", output_to_operand_aliasing={{}: (2, {})} | custom-call | flops 3221225472 | bytes 2000000 | tf_op jit(solution)/shard_map/final_2/pallas_call | solution.py:538
  385.9 27.4 %all_to_all.46 = bf16[8,256,384]{2,1,0:T(8,128)(2,1)S(1)} all-to-all(bf16[8,256,384]{2,1,0:T(8,128)(2,1)} %final_2.1), channel_id=1, replica_groups=mesh['seq'=16,'head'=8] {'head'}, dimensions={0} | all-to-all | bytes 3145728 | tf_op jit(solution)/shard_map/all_to_all | solution.py:307
  413.3 0.7 copy.13
  414.0 1.7 copy.14
  (56 shorter events, 0.7 us)
Async XLA Ops:
  3.9 5.9 %copy-start.6 = (s32[3,2048]{1,0:T(4,128)S(1)}, s32[3,2048]{1,0:T(4,128)}, u32[]{:S(2)}) copy-start(s32[3,2048]{1,0:T(4,128)} %param.10) | copy-start | bytes 73732
  3.9 5.9 %copy-start.7 = (s32[3,2048]{1,0:T(4,128)S(1)}, s32[3,2048]{1,0:T(4,128)}, u32[]{:S(2)}) copy-start(s32[3,2048]{1,0:T(4,128)} %param.9) | copy-start | bytes 73732
  3.9 32.3 %all-to-all-start = ((bf16[8,2,256,256]{3,2,1,0:T(8,128)(2,1)}), bf16[8,2,256,256]{3,2,1,0:T(8,128)(2,1)S(1)}, u32[]{:S(2)}, u32[]{:S(2)}) async-start(bf16[8,2,256,256]{3,2,1,0:T(8,128)(2,1)} %split_kv.1), calls=%async_computation | async-start | bytes 4194304 | tf_op jit(solution)/shard_map/all_to_all | solution.py:307
  36.2 1.4 copy-start.2
  49.9 36.4 %copy-start.8 = (bf16[256,384]{1,0:T(8,128)(2,1)S(1)}, bf16[256,384]{1,0:T(8,128)(2,1)}, u32[]{:S(2)}) copy-start(bf16[256,384]{1,0:T(8,128)(2,1)} %get-tuple-element.155) | copy-start | bytes 589828
  49.9 55.9 %all-to-all-start.1 = ((bf16[16,400,256]{2,1,0:T(8,128)(2,1)}), bf16[16,400,256]{2,1,0:T(8,128)(2,1)S(1)}, u32[]{:S(2)}, u32[]{:S(2)}) async-start(bf16[16,400,256]{2,1,0:T(8,128)(2,1)} %pack_kv.1), calls=%async_computation.1 | async-start | bytes 6553600 | tf_op jit(solution)/shard_map/all_to_all | solution.py:307
  57.8 6.3 %collective-permute-start = (bf16[2,256,128]{2,1,0:T(8,128)(2,1)}, bf16[2,256,128]{2,1,0:T(8,128)(2,1)S(1)}, u32[]{:S(2)}, u32[]{:S(2)}) collective-permute-start(bf16[2,256,128]{2,1,0:T(8,128)(2,1)} %get-tuple-element.125), channel_id=1, source_target_pairs={{0,1},{1,0},{2,3},{3,2},{4,5},{5,4},{6,7},{7,6},{8,9},{9,8},{10,11... | collective-permute-start | bytes 393224 | tf_op jit(solution)/shard_map/ppermute | solution.py:411
  59.0 5.9 %collective-permute-start.1 = (bf16[2,256,128]{2,1,0:T(8,128)(2,1)}, bf16[2,256,128]{2,1,0:T(8,128)(2,1)S(1)}, u32[]{:S(2)}, u32[]{:S(2)}) collective-permute-start(bf16[2,256,128]{2,1,0:T(8,128)(2,1)} %get-tuple-element.126), channel_id=1, source_target_pairs={{0,2},{1,3},{2,0},{3,1},{4,6},{5,7},{6,4},{7,5},{8,10},{9,11},{10,... | collective-permute-start | bytes 393224 | tf_op jit(solution)/shard_map/ppermute | solution.py:411
  59.3 8.7 %collective-permute-start.2 = (bf16[2,256,128]{2,1,0:T(8,128)(2,1)}, bf16[2,256,128]{2,1,0:T(8,128)(2,1)S(1)}, u32[]{:S(2)}, u32[]{:S(2)}) collective-permute-start(bf16[2,256,128]{2,1,0:T(8,128)(2,1)} %get-tuple-element.127), channel_id=1, source_target_pairs={{0,3},{1,2},{2,1},{3,0},{4,7},{5,6},{6,5},{7,4},{8,11},{9,10},{10,... | collective-permute-start | bytes 393224 | tf_op jit(solution)/shard_map/ppermute | solution.py:411
  60.8 9.8 %collective-permute-start.3 = (bf16[2,256,128]{2,1,0:T(8,128)(2,1)}, bf16[2,256,128]{2,1,0:T(8,128)(2,1)S(1)}, u32[]{:S(2)}, u32[]{:S(2)}) collective-permute-start(bf16[2,256,128]{2,1,0:T(8,128)(2,1)} %get-tuple-element.128), channel_id=1, source_target_pairs={{0,4},{1,5},{2,6},{3,7},{4,0},{5,1},{6,2},{7,3},{8,12},{9,13},{10,... | collective-permute-start | bytes 393224 | tf_op jit(solution)/shard_map/ppermute | solution.py:411
  61.2 12.7 %collective-permute-start.4 = (bf16[2,256,128]{2,1,0:T(8,128)(2,1)}, bf16[2,256,128]{2,1,0:T(8,128)(2,1)S(1)}, u32[]{:S(2)}, u32[]{:S(2)}) collective-permute-start(bf16[2,256,128]{2,1,0:T(8,128)(2,1)} %get-tuple-element.129), channel_id=1, source_target_pairs={{0,5},{1,4},{2,7},{3,6},{4,1},{5,0},{6,3},{7,2},{8,13},{9,12},{10,... | collective-permute-start | bytes 393224 | tf_op jit(solution)/shard_map/ppermute | solution.py:411
  64.1 25.3 %copy-start.15 = (bf16[2,256,128]{2,1,0:T(8,128)(2,1)}, bf16[2,256,128]{2,1,0:T(8,128)(2,1)S(1)}, u32[]{:S(2)}) copy-start(bf16[2,256,128]{2,1,0:T(8,128)(2,1)S(1)} %collective-permute-done.refs_1_) | copy-start | bytes 393220
  64.1 12.0 %collective-permute-start.5 = (bf16[2,256,128]{2,1,0:T(8,128)(2,1)}, bf16[2,256,128]{2,1,0:T(8,128)(2,1)S(1)}, u32[]{:S(2)}, u32[]{:S(2)}) collective-permute-start(bf16[2,256,128]{2,1,0:T(8,128)(2,1)} %get-tuple-element.130), channel_id=1, source_target_pairs={{0,6},{1,7},{2,4},{3,5},{4,2},{5,3},{6,0},{7,1},{8,14},{9,15},{10,... | collective-permute-start | bytes 393224 | tf_op jit(solution)/shard_map/ppermute | solution.py:411
  64.9 24.4 %copy-start.16 = (bf16[2,256,128]{2,1,0:T(8,128)(2,1)}, bf16[2,256,128]{2,1,0:T(8,128)(2,1)S(1)}, u32[]{:S(2)}) copy-start(bf16[2,256,128]{2,1,0:T(8,128)(2,1)S(1)} %collective-permute-done.1.refs_2_) | copy-start | bytes 393220
  64.9 14.2 %collective-permute-start.6 = (bf16[2,256,128]{2,1,0:T(8,128)(2,1)}, bf16[2,256,128]{2,1,0:T(8,128)(2,1)S(1)}, u32[]{:S(2)}, u32[]{:S(2)}) collective-permute-start(bf16[2,256,128]{2,1,0:T(8,128)(2,1)} %get-tuple-element.131), channel_id=1, source_target_pairs={{0,7},{1,6},{2,5},{3,4},{4,3},{5,2},{6,1},{7,0},{8,15},{9,14},{10,... | collective-permute-start | bytes 393224 | tf_op jit(solution)/shard_map/ppermute | solution.py:411
  68.0 21.3 %copy-start.17 = (bf16[2,256,128]{2,1,0:T(8,128)(2,1)}, bf16[2,256,128]{2,1,0:T(8,128)(2,1)S(1)}, u32[]{:S(2)}) copy-start(bf16[2,256,128]{2,1,0:T(8,128)(2,1)S(1)} %collective-permute-done.2.refs_3_) | copy-start | bytes 393220
  70.6 18.8 %copy-start.18 = (bf16[2,256,128]{2,1,0:T(8,128)(2,1)}, bf16[2,256,128]{2,1,0:T(8,128)(2,1)S(1)}, u32[]{:S(2)}) copy-start(bf16[2,256,128]{2,1,0:T(8,128)(2,1)S(1)} %collective-permute-done.3.refs_4_) | copy-start | bytes 393220
  73.8 15.5 %copy-start.19 = (bf16[2,256,128]{2,1,0:T(8,128)(2,1)}, bf16[2,256,128]{2,1,0:T(8,128)(2,1)S(1)}, u32[]{:S(2)}) copy-start(bf16[2,256,128]{2,1,0:T(8,128)(2,1)S(1)} %collective-permute-done.4.refs_5_) | copy-start | bytes 393220
  76.1 13.3 %copy-start.20 = (bf16[2,256,128]{2,1,0:T(8,128)(2,1)}, bf16[2,256,128]{2,1,0:T(8,128)(2,1)S(1)}, u32[]{:S(2)}) copy-start(bf16[2,256,128]{2,1,0:T(8,128)(2,1)S(1)} %collective-permute-done.5.refs_6_) | copy-start | bytes 393220
  79.2 10.2 %copy-start.21 = (bf16[2,256,128]{2,1,0:T(8,128)(2,1)}, bf16[2,256,128]{2,1,0:T(8,128)(2,1)S(1)}, u32[]{:S(2)}) copy-start(bf16[2,256,128]{2,1,0:T(8,128)(2,1)S(1)} %collective-permute-done.6.refs_7_) | copy-start | bytes 393220
  79.2 5.1 %collective-permute-start.7 = (bf16[256,384]{1,0:T(8,128)(2,1)}, bf16[256,384]{1,0:T(8,128)(2,1)S(1)}, u32[]{:S(2)}, u32[]{:S(2)}) collective-permute-start(bf16[256,384]{1,0:T(8,128)(2,1)} %get-tuple-element.149), channel_id=1, source_target_pairs={{0,1},{1,0},{2,3},{3,2},{4,5},{5,4},{6,7},{7,6},{8,9},{9,8},{10,11... | collective-permute-start | bytes 589832 | tf_op jit(solution)/shard_map/ppermute | solution.py:411
  79.3 6.3 %collective-permute-start.8 = (bf16[256,384]{1,0:T(8,128)(2,1)}, bf16[256,384]{1,0:T(8,128)(2,1)S(1)}, u32[]{:S(2)}, u32[]{:S(2)}) collective-permute-start(bf16[256,384]{1,0:T(8,128)(2,1)} %get-tuple-element.150), channel_id=1, source_target_pairs={{0,2},{1,3},{2,0},{3,1},{4,6},{5,7},{6,4},{7,5},{8,10},{9,11},{10,... | collective-permute-start | bytes 589832 | tf_op jit(solution)/shard_map/ppermute | solution.py:411
  79.3 17.3 %collective-permute-start.9 = (bf16[256,384]{1,0:T(8,128)(2,1)}, bf16[256,384]{1,0:T(8,128)(2,1)S(1)}, u32[]{:S(2)}, u32[]{:S(2)}) collective-permute-start(bf16[256,384]{1,0:T(8,128)(2,1)} %get-tuple-element.151), channel_id=1, source_target_pairs={{0,3},{1,2},{2,1},{3,0},{4,7},{5,6},{6,5},{7,4},{8,11},{9,10},{10,... | collective-permute-start | bytes 589832 | tf_op jit(solution)/shard_map/ppermute | solution.py:411
  81.3 15.2 %collective-permute-start.10 = (bf16[256,384]{1,0:T(8,128)(2,1)}, bf16[256,384]{1,0:T(8,128)(2,1)S(1)}, u32[]{:S(2)}, u32[]{:S(2)}) collective-permute-start(bf16[256,384]{1,0:T(8,128)(2,1)} %get-tuple-element.152), channel_id=1, source_target_pairs={{0,4},{1,5},{2,6},{3,7},{4,0},{5,1},{6,2},{7,3},{8,12},{9,13},{10,... | collective-permute-start | bytes 589832 | tf_op jit(solution)/shard_map/ppermute | solution.py:411
  81.9 17.7 %collective-permute-start.11 = (bf16[256,384]{1,0:T(8,128)(2,1)}, bf16[256,384]{1,0:T(8,128)(2,1)S(1)}, u32[]{:S(2)}, u32[]{:S(2)}) collective-permute-start(bf16[256,384]{1,0:T(8,128)(2,1)} %get-tuple-element.153), channel_id=1, source_target_pairs={{0,5},{1,4},{2,7},{3,6},{4,1},{5,0},{6,3},{7,2},{8,13},{9,12},{10,... | collective-permute-start | bytes 589832 | tf_op jit(solution)/shard_map/ppermute | solution.py:411
  84.3 1.0 copy-start.9
  84.3 15.9 %collective-permute-start.12 = (bf16[256,384]{1,0:T(8,128)(2,1)}, bf16[256,384]{1,0:T(8,128)(2,1)S(1)}, u32[]{:S(2)}, u32[]{:S(2)}) collective-permute-start(bf16[256,384]{1,0:T(8,128)(2,1)} %get-tuple-element.154), channel_id=1, source_target_pairs={{0,6},{1,7},{2,4},{3,5},{4,2},{5,3},{6,0},{7,1},{8,14},{9,15},{10,... | collective-permute-start | bytes 589832 | tf_op jit(solution)/shard_map/ppermute | solution.py:411
  85.6 0.7 copy-start.10
  86.3 19.0 %collective-permute-start.13 = (bf16[256,384]{1,0:T(8,128)(2,1)S(1)}, bf16[256,384]{1,0:T(8,128)(2,1)}, u32[]{:S(2)}, u32[]{:S(2)}) collective-permute-start(bf16[256,384]{1,0:T(8,128)(2,1)S(1)} %copy-done.8), channel_id=1, source_target_pairs={{0,7},{1,6},{2,5},{3,4},{4,3},{5,2},{6,1},{7,0},{8,15},{9,14},{10,... | collective-permute-start | bytes 589832 | tf_op jit(solution)/shard_map/ppermute | solution.py:411
  96.6 3.6 copy-start.11
  96.6 3.6 copy-start.12
  99.6 0.7 copy-start.13
  100.3 0.7 copy-start.14
  105.8 22.3 %copy-start = (bf16[16,400,256]{2,1,0:T(8,128)(2,1)}, bf16[16,400,256]{2,1,0:T(8,128)(2,1)S(1)}, u32[]{:S(2)}) copy-start(bf16[16,400,256]{2,1,0:T(8,128)(2,1)S(1)} %all-to-all-done.1.in_ref.meta_ref) | copy-start | bytes 9830404
  105.8 31.9 %all-to-all-start.2 = ((bf16[16,192,256]{2,1,0:T(8,128)(2,1)}), bf16[16,192,256]{2,1,0:T(8,128)(2,1)}, u32[]{:S(2)}, u32[]{:S(2)}) async-start(bf16[16,192,256]{2,1,0:T(8,128)(2,1)} %pack_last.1), calls=%async_computation.2 | async-start | bytes 3145728 | tf_op jit(solution)/shard_map/all_to_all | solution.py:307
  128.1 13.6 %copy-start.5 = (s32[3,256,16]{1,2,0:T(8,128)S(1)}, s32[3,256,16]{1,2,0:T(8,128)}, u32[]{:S(2)}) copy-start(s32[3,256,16]{1,2,0:T(8,128)} %param.11) | copy-start | bytes 147460
  137.7 37.6 %all-to-all-start.3 = ((bf16[16,3,192,128]{3,2,1,0:T(8,128)(2,1)}), bf16[16,3,192,128]{3,2,1,0:T(8,128)(2,1)S(1)}, u32[]{:S(2)}, u32[]{:S(2)}) async-start(bf16[16,3,192,128]{3,2,1,0:T(8,128)(2,1)} %pack_q.1), calls=%async_computation.3 | async-start | bytes 4718592 | tf_op jit(solution)/shard_map/all_to_all | solution.py:307
  175.3 100.3 %copy-start.1 = (bf16[16,3,192,128]{3,2,1,0:T(8,128)(2,1)}, bf16[16,3,192,128]{3,2,1,0:T(8,128)(2,1)S(1)}, u32[]{:S(2)}) copy-start(bf16[16,3,192,128]{3,2,1,0:T(8,128)(2,1)S(1)} %all-to-all-done.3.in_ref) | copy-start | bytes 7077892
  275.6 58.2 %all-to-all-start.5 = ((bf16[16,1,4,128,256]{4,3,2,1,0:T(8,128)(2,1)}), bf16[16,1,4,128,256]{4,3,2,1,0:T(8,128)(2,1)}, u32[]{:S(2)}, u32[]{:S(2)}) async-start(bf16[16,1,4,128,256]{4,3,2,1,0:T(8,128)(2,1)} %get-tuple-element.172), calls=%async_computation.5 | async-start | bytes 8388608 | tf_op jit(solution)/shard_map/all_to_all | solution.py:307
  333.8 27.1 %all-to-all-start.7 = ((bf16[16,2,192,128]{3,2,1,0:T(8,128)(2,1)}), bf16[16,2,192,128]{3,2,1,0:T(8,128)(2,1)S(1)}, u32[]{:S(2)}, u32[]{:S(2)}) async-start(bf16[16,2,192,128]{3,2,1,0:T(8,128)(2,1)} %attend_0.1), calls=%async_computation.7 | async-start | bytes 3145728 | tf_op jit(solution)/shard_map/all_to_all | solution.py:307
  360.8 5.4 %copy-start.3 = (bf16[16,2,192,128]{3,2,1,0:T(8,128)(2,1)}, bf16[16,2,192,128]{3,2,1,0:T(8,128)(2,1)S(1)}, u32[]{:S(2)}) copy-start(bf16[16,2,192,128]{3,2,1,0:T(8,128)(2,1)S(1)} %all-to-all-done.7.in_ref) | copy-start | bytes 4718596
  360.8 17.7 %all-to-all-start.6 = ((bf16[16,1,192,128]{3,2,1,0:T(8,128)(2,1)}), bf16[16,1,192,128]{3,2,1,0:T(8,128)(2,1)S(1)}, u32[]{:S(2)}, u32[]{:S(2)}) async-start(bf16[16,1,192,128]{3,2,1,0:T(8,128)(2,1)} %attend_2.1), calls=%async_computation.6 | async-start | bytes 1572864 | tf_op jit(solution)/shard_map/all_to_all | solution.py:307
  378.5 0.9 copy-start.4

commit v5 on v4

--- a/solution.py
+++ b/solution.py
@@ -80,12 +80,24 @@
             turned[:, i : i + 1], (LANES, LANES)
         ).astype(I32)
     lane = iota((step, LANES), 1)
-    tiles = packed.shape[0] // LANES
+    narrow = packed.shape[1] == LANES
+    depth = packed.shape[0] // 2 if narrow else packed.shape[0]
+    if narrow:
+        packed = jnp.concatenate([packed[:depth], packed[depth:]], axis=1)
 
     def body(i, carry):
-        wide = wide_ref[pl.ds(pl.multiple_of(i * step, step), step), :] - lane
-        onehot = jnp.concatenate([(wide == t * LANES).astype(BF16) for t in range(tiles)], axis=1)
-        store(i, dot(onehot, packed).astype(BF16))
+        wide = wide_ref[pl.ds(pl.multiple_of(i * step, step), step), :]
+        second = wide >= depth
+        if narrow:
+            wide = jnp.where(second, wide - depth, wide)
+        wide = wide - lane
+        onehot = jnp.concatenate(
+            [(wide == t * LANES).astype(BF16) for t in range(depth // LANES)], axis=1
+        )
+        block = dot(onehot, packed)
+        if narrow:
+            block = jnp.where(second, block[:, LANES:], block[:, :LANES])
+        store(i, block.astype(BF16))
         return carry
 
     lax.fori_loop(0, chunks * LANES // step, body, 0)
@@ -133,12 +145,13 @@
     keys = key_ref[:, 0].reshape(tokens, LANES)
     values = value_ref[:, 0].reshape(tokens, LANES)
     at = pl.ds(pl.multiple_of(head * capacity, META), capacity)
-
-    def store(i, block):
-        out_ref[pl.ds(2 * i, 2), at, :] = block.reshape(2, capacity, 2 * LANES)
+    per = groups // 2
+
+    def store(i, block):
+        out_ref[pl.ds(per * i, per), at, :] = block.reshape(per, capacity, 2 * LANES)
 
     both = jnp.concatenate([keys, values], axis=1)
-    spread(slot_ref[0], both, store, groups * capacity, 2 * capacity)
+    spread(slot_ref[0], both, store, groups * capacity, per * capacity)
 
     @pl.when(head == heads - 1)
     def _():
@@ -157,12 +170,13 @@
     index = partner_order(me_ref[0], slot_ref[0], len(part_refs))
     keys = jnp.concatenate([ref[0] for ref in part_refs], axis=0)
     values = jnp.concatenate([ref[1] for ref in part_refs], axis=0)
-
-    def store(i, block):
-        out_ref[pl.ds(2 * i, 2)] = block.reshape(2, capacity, 2 * LANES)
+    per = groups // 2
+
+    def store(i, block):
+        out_ref[pl.ds(per * i, per)] = block.reshape(per, capacity, 2 * LANES)
 
     both = jnp.concatenate([keys, values], axis=1)
-    spread(index, both, store, groups * capacity, 2 * capacity)
+    spread(index, both, store, groups * capacity, per * capacity)
 
 
 def pack_q_kernel(me_ref, slot_ref, *refs):
@@ -170,11 +184,12 @@
     groups, _, capacity, _ = out_ref.shape
     index = partner_order(me_ref[0], slot_ref[0], len(part_refs))
     queries = jnp.concatenate([ref[...] for ref in part_refs], axis=0)
-
-    def store(i, block):
-        out_ref[pl.ds(2 * i, 2), 0] = block.reshape(2, capacity, LANES)
-
-    spread(index, queries, store, groups * capacity, 2 * capacity)
+    per = groups // 2
+
+    def store(i, block):
+        out_ref[pl.ds(per * i, per), 0] = block.reshape(per, capacity, LANES)
+
+    spread(index, queries, store, groups * capacity, per * capacity)
 
 
 def sources(counts, capacity):
@@ -214,11 +229,11 @@
     key_source = sources(counts[:, :LANES], capacity)
 
     def store(i, block):
-        sorted_ref[pl.ds(4 * i, 4)] = block.reshape(4, BLOCK, 2 * LANES)
+        sorted_ref[pl.ds(8 * i, 8)] = block.reshape(8, BLOCK, 2 * LANES)
 
     def send(packed_ref, out_ref):
         packed = packed_ref[...].reshape(groups * capacity, 2 * LANES)
-        collect(key_source, packed, wide_ref, store, 4 * BLOCK)
+        collect(key_source, packed, wide_ref, store, 8 * BLOCK)
 
         def copy(i, carry):
             for j in range(KCAP):
@@ -239,7 +254,7 @@
 def unpack_q_kernel(index_ref, in_ref, out_ref, wide_ref):
     groups, _, capacity, _ = in_ref.shape
     packed = in_ref[:, 0].reshape(groups * capacity, LANES)
-    step = 4 * BLOCK
+    step = 8 * BLOCK
 
     def store(i, block):
         out_ref[0, pl.ds(pl.multiple_of(i * step, step), step), :] = block
@@ -254,9 +269,9 @@
     part = out_ref.shape[1]
 
     def store(i, block):
-        out_ref[pl.ds(2 * i, 2)] = block.reshape(2, part, LANES)
-
-    collect(index_ref[0], packed, wide_ref, store, 2 * part)
+        out_ref[pl.ds(4 * i, 4)] = block.reshape(4, part, LANES)
+
+    collect(index_ref[0], packed, wide_ref, store, 4 * part)
 
 
 def attend_kernel(fetch_ref, index_ref, query_ref, recv_ref, out_ref, attended_ref, *, first):
@@ -289,10 +304,12 @@
 
     lax.fori_loop(0, owned // 4, body, 0)
 
-    def store(i, block):
-        out_ref[pl.ds(2 * i, 2), 0] = block.reshape(2, capacity, LANES)
-
-    spread(index_ref[0], attended_ref[...], store, groups * capacity, 2 * capacity)
+    per = groups // 2
+
+    def store(i, block):
+        out_ref[pl.ds(per * i, per), 0] = block.reshape(per, capacity, LANES)
+
+    spread(index_ref[0], attended_ref[...], store, groups * capacity, per * capacity)
 
 
 def shape_of(shape, dtype):

time: 417 us -> 413 us (level)
  Pallas kernels: 160 us -> 138 us
  waiting for transfers between devices: 58.5 us -> 76.6 us
    all_to_all x7, waiting for transfers between devices: 38.1 us -> 55.2 us  [exchange(): return lax.all_to_all(array, axis, split_axis=0, concat_axis=0, tiled=True)]
    pallas_call x2, Pallas kernels: 17.5 us -> 11.5 us  [per_device(): pl.pallas_call(final_kernel, grid=(count_heads,), in_specs=[pl.BlockSpec(...]
    pallas_call x1, Pallas kernels: 15.5 us -> 9.48 us  [per_device(): pl.pallas_call(unpack_q_kernel, grid=(heads,), in_specs=[pl.BlockSpec((1,...]
  transfers between devices with their start and end apart: 21 -> 21, of which waited for: 16 -> 16; matrix products, arithmetic and copies ran while one was open for 1% -> 1% of each run, Pallas kernels for 33% -> 29%
where the time goes in v5:
time: 413 us; the launch traced here: 412 us
  Pallas kernels  138 us (33%)
  blocking collectives  128 us (31%)
  waiting for transfers between devices  76.6 us (19%)
  starting transfers between devices  59 us (14%)
  local copies, waits for them, and re-layouts  8.84 us (2%)
    all_to_all x2, blocking collectives, exchange(): return lax.all_to_all(array, axis, split_axis=0, concat_axis=0, tiled=True)  128 us
    all_to_all x7, waiting for transfers between devices, exchange(): return lax.all_to_all(array, axis, split_axis=0, concat_axis=0, tiled=True)  55.2 us
    pallas_call x2, Pallas kernels, per_device(): pl.pallas_call(functools.partial(attend_kernel, first=first), grid_spec=p...  46.5 us
    all_to_all x7, starting transfers between devices, exchange(): return lax.all_to_all(array, axis, split_axis=0, concat_axis=0, tiled=True)  40.6 us
    ppermute x14, waiting for transfers between devices, to_partner(): return lax.ppermute(array, 'head', [(i, i ^ k) for i in range(parts)])  21.4 us
    pallas_call x1, Pallas kernels, per_device(): pl.pallas_call(unpack_kv_kernel, grid_spec=pltpu.PrefetchScalarGridSpec(n...  21.4 us
    ppermute x14, starting transfers between devices, to_partner(): return lax.ppermute(array, 'head', [(i, i ^ k) for i in range(parts)])  18.4 us
    pallas_call x1, Pallas kernels, per_device(): pl.pallas_call(pack_q_kernel, grid_spec=pltpu.PrefetchScalarGridSpec(num_...  13.1 us
  transfers between devices with their start and end apart: 21, of which 16 were waited for; matrix products, arithmetic and copies ran while one was open for 1% of the time, Pallas kernels for 29%

profile of v5, /device:TPU:1, one launch (start us, length us, event | category | flops | bytes accessed | tf_op | source)
XLA Modules:
  0.0 411.8 jit_solution(18443796172310484670)
XLA Ops:
  0.0 3.9 split_kv.1
  3.9 5.9 %all-to-all-start = ((bf16[8,2,256,256]{3,2,1,0:T(8,128)(2,1)}), bf16[8,2,256,256]{3,2,1,0:T(8,128)(2,1)S(1)}, u32[]{:S(2)}, u32[]{:S(2)}) async-start(bf16[8,2,256,256]{3,2,1,0:T(8,128)(2,1)} %split_kv.1), calls=%async_computation | async-start | bytes 4194304 | tf_op jit(solution)/shard_map/all_to_all | solution.py:324
  9.9 0.6 copy.19
  10.5 3.6 split_rest.1
  14.2 11.5 %slots.1 = (s32[6,16,128]{2,1,0:T(8,128)}, f32[6,16,128]{2,1,0:T(8,128)}) custom-call(s32[6,16,128]{2,1,0:T(8,128)} %bitcast.19), custom_call_target="tpu_custom_call" | custom-call | flops 6000000000 | bytes 1000000 | tf_op jit(solution)/shard_map/slots/pallas_call | solution.py:391
  25.7 10.6 %all-to-all-done.key_ref.value_ref = bf16[8,2,256,256]{3,2,1,0:T(8,128)(2,1)S(1)} async-done(((bf16[8,2,256,256]{3,2,1,0:T(8,128)(2,1)}), bf16[8,2,256,256]{3,2,1,0:T(8,128)(2,1)S(1)}, u32[]{:S(2)}, u32[]{:S(2)}) %all-to-all-start) | async-done | bytes 2097184 | tf_op jit(solution)/shard_map/all_to_all | solution.py:324
  36.2 1.4 copy-done.2
  37.6 10.4 %pack_kv.1 = bf16[16,400,256]{2,1,0:T(8,128)(2,1)} custom-call(s32[6,16,128]{2,1,0:T(8,128)} %get-tuple-element.89.slot_ref.index_ref, f32[6,16,128]{2,1,0:T(8,128)} %get-tuple-element.122.count_ref, bf16[8,2,256,256]{3,2,1,0:T(8,128)(2,1)} %copy-done.2, bf16[8,2,256,256]{3,2,1,0:T(8,128)(2,1)} %copy-done.2), custom_call_target="tpu_custom_call" | custom-call | flops 6442450944 | bytes 8000000 | tf_op jit(solution)/shard_map/pack_kv/pallas_call | solution.py:410
  47.9 7.9 %all-to-all-start.1 = ((bf16[16,400,256]{2,1,0:T(8,128)(2,1)}), bf16[16,400,256]{2,1,0:T(8,128)(2,1)S(1)}, u32[]{:S(2)}, u32[]{:S(2)}) async-start(bf16[16,400,256]{2,1,0:T(8,128)(2,1)} %pack_kv.1), calls=%async_computation.1 | async-start | bytes 6553600 | tf_op jit(solution)/shard_map/all_to_all | solution.py:324
  55.8 1.2 collective-permute-start
  57.1 0.3 collective-permute-start.1
  57.4 1.4 collective-permute-start.2
  58.8 0.4 collective-permute-start.3
  59.2 2.9 collective-permute-start.4
  62.1 0.9 collective-permute-start.5
  63.0 2.0 collective-permute-start.6
  65.0 1.1 collective-permute-done.2.refs_3_
  66.1 2.5 collective-permute-done.3.refs_4_
  68.6 3.3 collective-permute-done.4.refs_5_
  71.9 2.2 collective-permute-done.5.refs_6_
  74.1 3.1 collective-permute-done.6.refs_7_
  77.3 2.0 collective-permute-start.9
  79.4 0.6 collective-permute-start.10
  80.0 2.4 collective-permute-start.11
  82.3 1.0 collective-permute-start.12
  83.4 0.3 collective-permute-done.8.refs_2_
  83.6 0.7 copy-done.10
  84.3 3.1 collective-permute-start.13
  87.5 6.1 %pack_last.1 = bf16[16,192,256]{2,1,0:T(8,128)(2,1)} custom-call(s32[1]{0:T(128)} %bitcast.1.me_ref, s32[6,16,128]{2,1,0:T(8,128)} %get-tuple-element.89.slot_ref.index_ref, bf16[2,256,128]{2,1,0:T(8,128)(2,1)} %get-tuple-element.140.refs_0_, bf16[2,256,128]{2,1,0:T(8,128)(2,1)} %copy-done.15, bf16[2,256,128]{2,1,0:T(8,128)(2,1)} %copy-done.16, ...), custom_call_target="tpu_custom_call" | custom-call | flops 3221225472 | bytes 3000000 | tf_op jit(solution)/shard_map/pack_last/pallas_call | solution.py:436
  93.6 4.0 collective-permute-done.11.refs_5_
  97.7 0.6 collective-permute-done.12.refs_6_
  98.3 0.7 copy-done.14
  99.0 4.3 %collective-permute-done.13.refs_7_ = bf16[256,384]{1,0:T(8,128)(2,1)} collective-permute-done((bf16[256,384]{1,0:T(8,128)(2,1)S(1)}, bf16[256,384]{1,0:T(8,128)(2,1)}, u32[]{:S(2)}, u32[]{:S(2)}) %collective-permute-start.13) | collective-permute-done | bytes 196640 | tf_op jit(solution)/shard_map/ppermute | solution.py:428
  103.3 0.5 all-to-all-done.1.in_ref.meta_ref
  103.9 6.2 %all-to-all-start.2 = ((bf16[16,192,256]{2,1,0:T(8,128)(2,1)}), bf16[16,192,256]{2,1,0:T(8,128)(2,1)}, u32[]{:S(2)}, u32[]{:S(2)}) async-start(bf16[16,192,256]{2,1,0:T(8,128)(2,1)} %pack_last.1), calls=%async_computation.2 | async-start | bytes 3145728 | tf_op jit(solution)/shard_map/all_to_all | solution.py:324
  110.1 13.1 %pack_q.1 = bf16[16,3,192,128]{3,2,1,0:T(8,128)(2,1)} custom-call(s32[1]{0:T(128)} %bitcast.1.me_ref, s32[6,16,128]{2,1,0:T(8,128)} %get-tuple-element.89.slot_ref.index_ref, bf16[256,384]{1,0:T(8,128)(2,1)} %get-tuple-element.156.refs_0_, bf16[256,384]{1,0:T(8,128)(2,1)} %copy-done.9, bf16[256,384]{1,0:T(8,128)(2,1)} %copy-done.10, ...), custom_call_target="tpu_custom_call" | custom-call | flops 9663676416 | bytes 4000000 | tf_op jit(solution)/shard_map/pack_q/pallas_call | solution.py:453
  123.2 12.6 %all-to-all-done.2.last_in_ref = bf16[16,192,256]{2,1,0:T(8,128)(2,1)} async-done(((bf16[16,192,256]{2,1,0:T(8,128)(2,1)}), bf16[16,192,256]{2,1,0:T(8,128)(2,1)}, u32[]{:S(2)}, u32[]{:S(2)}) %all-to-all-start.2) | async-done | bytes 1572896 | tf_op jit(solution)/shard_map/all_to_all | solution.py:324
  135.8 3.7 all-to-all-start.3
  139.5 0.2 copy.11
  139.7 0.2 reshape.35
  139.9 1.0 compare_reduce_fusion
  141.0 0.3 select_reduce_fusion.1
  141.3 0.7 copy.12.pick_ref
  142.0 21.4 %unpack_kv.1 = (bf16[16,2,4,128,256]{4,3,2,1,0:T(8,128)(2,1)}, bf16[16,1,4,128,256]{4,3,2,1,0:T(8,128)(2,1)}, s32[3,16,128]{2,1,0:T(8,128)}) custom-call(s32[3,16,4]{2,1,0:T(8,128)} %copy.12.pick_ref, bf16[16,400,256]{2,1,0:T(8,128)(2,1)} %copy-done, bf16[16,192,256]{2,1,0:T(8,128)(2,1)} %all-to-all-done.2.last_in_ref, bf16[16,400,256]{2,1,0:T(8,128)(2,1)} %copy-done), custom_call_target="tpu_custom_call" | custom-call | flops 9663676416 | bytes 18000000 | tf_op jit(solution)/shard_map/unpack_kv/pallas_call | solution.py:472
  163.4 10.0 %all-to-all-done.3.in_ref = bf16[16,3,192,128]{3,2,1,0:T(8,128)(2,1)S(1)} async-done(((bf16[16,3,192,128]{3,2,1,0:T(8,128)(2,1)}), bf16[16,3,192,128]{3,2,1,0:T(8,128)(2,1)S(1)}, u32[]{:S(2)}, u32[]{:S(2)}) %all-to-all-start.3) | async-done | bytes 2359328 | tf_op jit(solution)/shard_map/all_to_all | solution.py:324
  173.4 100.3 %all_to_all.45.recv_ref = bf16[16,2,4,128,256]{4,3,2,1,0:T(8,128)(2,1)} all-to-all(bf16[16,2,4,128,256]{4,3,2,1,0:T(8,128)(2,1)} %get-tuple-element.169), channel_id=1, replica_groups=mesh['seq'=16,'head'=8] {'seq'}, dimensions={0} | all-to-all | bytes 16777216 | tf_op jit(solution)/shard_map/all_to_all | solution.py:324
  273.7 4.8 %all-to-all-start.5 = ((bf16[16,1,4,128,256]{4,3,2,1,0:T(8,128)(2,1)}), bf16[16,1,4,128,256]{4,3,2,1,0:T(8,128)(2,1)}, u32[]{:S(2)}, u32[]{:S(2)}) async-start(bf16[16,1,4,128,256]{4,3,2,1,0:T(8,128)(2,1)} %get-tuple-element.172), calls=%async_computation.5 | async-start | bytes 8388608 | tf_op jit(solution)/shard_map/all_to_all | solution.py:324
  278.5 0.2 fusion.1
  279.0 0.3 select_reduce_fusion
  279.3 0.7 reshape.37.fetch_ref
  280.0 9.5 %unpack_q.1.query_ref = bf16[3,2048,128]{2,1,0:T(8,128)(2,1)} custom-call(s32[3,16,128]{2,1,0:T(8,128)} %get-tuple-element.170.index_ref, bf16[16,3,192,128]{3,2,1,0:T(8,128)(2,1)} %copy-done.1), custom_call_target="tpu_custom_call" | custom-call | flops 9663676416 | bytes 4000000 | tf_op jit(solution)/shard_map/unpack_q/pallas_call | solution.py:510
  289.5 29.2 %attend_0.1 = bf16[16,2,192,128]{3,2,1,0:T(8,128)(2,1)} custom-call(s32[3,16,16]{2,1,0:T(8,128)} %reshape.37.fetch_ref, s32[3,16,128]{2,1,0:T(8,128)} %get-tuple-element.170.index_ref, bf16[3,2048,128]{2,1,0:T(8,128)(2,1)} %unpack_q.1.query_ref, bf16[16,2,4,128,256]{4,3,2,1,0:T(8,128)(2,1)} %all_to_all.45.recv_ref), custom_call_target="tpu_custom_call" | custom-call | flops 4294967296 | bytes 12000000 | tf_op jit(solution)/shard_map/attend_0/pallas_call | solution.py:527
  318.7 13.1 %all-to-all-done.5.recv_ref = bf16[16,1,4,128,256]{4,3,2,1,0:T(8,128)(2,1)} async-done(((bf16[16,1,4,128,256]{4,3,2,1,0:T(8,128)(2,1)}), bf16[16,1,4,128,256]{4,3,2,1,0:T(8,128)(2,1)}, u32[]{:S(2)}, u32[]{:S(2)}) %all-to-all-start.5) | async-done | bytes 4194336 | tf_op jit(solution)/shard_map/all_to_all | solution.py:324
  331.8 6.7 %all-to-all-start.7 = ((bf16[16,2,192,128]{3,2,1,0:T(8,128)(2,1)}), bf16[16,2,192,128]{3,2,1,0:T(8,128)(2,1)S(1)}, u32[]{:S(2)}, u32[]{:S(2)}) async-start(bf16[16,2,192,128]{3,2,1,0:T(8,128)(2,1)} %attend_0.1), calls=%async_computation.7 | async-start | bytes 3145728 | tf_op jit(solution)/shard_map/all_to_all | solution.py:324
  338.5 17.3 %attend_2.1 = bf16[16,1,192,128]{3,2,1,0:T(8,128)(2,1)} custom-call(s32[3,16,16]{2,1,0:T(8,128)} %reshape.37.fetch_ref, s32[3,16,128]{2,1,0:T(8,128)} %get-tuple-element.170.index_ref, bf16[3,2048,128]{2,1,0:T(8,128)(2,1)} %unpack_q.1.query_ref, bf16[16,1,4,128,256]{4,3,2,1,0:T(8,128)(2,1)} %all-to-all-done.5.recv_ref), custom_call_target="tpu_custom_call" | custom-call | flops 2147483648 | bytes 6000000 | tf_op jit(solution)/shard_map/attend_2/pallas_call | solution.py:527
  355.8 3.1 all-to-all-done.7.in_ref
  358.9 5.4 %all-to-all-start.6 = ((bf16[16,1,192,128]{3,2,1,0:T(8,128)(2,1)}), bf16[16,1,192,128]{3,2,1,0:T(8,128)(2,1)S(1)}, u32[]{:S(2)}, u32[]{:S(2)}) async-start(bf16[16,1,192,128]{3,2,1,0:T(8,128)(2,1)} %attend_2.1), calls=%async_computation.6 | async-start | bytes 1572864 | tf_op jit(solution)/shard_map/all_to_all | solution.py:324
  364.3 7.0 %final_0.1.refs_0_ = bf16[8,256,384]{2,1,0:T(8,128)(2,1)} custom-call(s32[6,16,128]{2,1,0:T(8,128)} %get-tuple-element.89.slot_ref.index_ref, bf16[16,2,192,128]{3,2,1,0:T(8,128)(2,1)} %copy-done.3), custom_call_target="tpu_custom_call" | custom-call | flops 6442450944 | bytes 2000000 | tf_op jit(solution)/shard_map/final_0/pallas_call | solution.py:555
  371.3 5.3 %all-to-all-done.6.in_ref = bf16[16,1,192,128]{3,2,1,0:T(8,128)(2,1)S(1)} async-done(((bf16[16,1,192,128]{3,2,1,0:T(8,128)(2,1)}), bf16[16,1,192,128]{3,2,1,0:T(8,128)(2,1)S(1)}, u32[]{:S(2)}, u32[]{:S(2)}) %all-to-all-start.6) | async-done | bytes 786464 | tf_op jit(solution)/shard_map/all_to_all | solution.py:324
  376.6 0.9 copy-done.4
  377.5 4.5 %final_2.1 = bf16[8,256,384]{2,1,0:T(8,128)(2,1)} custom-call(s32[6,16,128]{2,1,0:T(8,128)} %get-tuple-element.89.slot_ref.index_ref, bf16[16,1,192,128]{3,2,1,0:T(8,128)(2,1)} %copy-done.4, bf16[8,256,384]{2,1,0:T(8,128)(2,1)} %final_0.1.refs_0_), custom_call_target="tpu_custom_call", output_to_operand_aliasing={{}: (2, {})} | custom-call | flops 3221225472 | bytes 2000000 | tf_op jit(solution)/shard_map/final_2/pallas_call | solution.py:555
  382.0 27.3 %all_to_all.46 = bf16[8,256,384]{2,1,0:T(8,128)(2,1)S(1)} all-to-all(bf16[8,256,384]{2,1,0:T(8,128)(2,1)} %final_2.1), channel_id=1, replica_groups=mesh['seq'=16,'head'=8] {'head'}, dimensions={0} | all-to-all | bytes 3145728 | tf_op jit(solution)/shard_map/all_to_all | solution.py:324
  409.3 0.7 copy.13
  410.0 1.7 copy.14
  (56 shorter events, 0.7 us)
Async XLA Ops:
  3.9 5.9 %copy-start.6 = (s32[3,2048]{1,0:T(4,128)S(1)}, s32[3,2048]{1,0:T(4,128)}, u32[]{:S(2)}) copy-start(s32[3,2048]{1,0:T(4,128)} %param.10) | copy-start | bytes 73732
  3.9 5.9 %copy-start.7 = (s32[3,2048]{1,0:T(4,128)S(1)}, s32[3,2048]{1,0:T(4,128)}, u32[]{:S(2)}) copy-start(s32[3,2048]{1,0:T(4,128)} %param.9) | copy-start | bytes 73732
  3.9 32.3 %all-to-all-start = ((bf16[8,2,256,256]{3,2,1,0:T(8,128)(2,1)}), bf16[8,2,256,256]{3,2,1,0:T(8,128)(2,1)S(1)}, u32[]{:S(2)}, u32[]{:S(2)}) async-start(bf16[8,2,256,256]{3,2,1,0:T(8,128)(2,1)} %split_kv.1), calls=%async_computation | async-start | bytes 4194304 | tf_op jit(solution)/shard_map/all_to_all | solution.py:324
  36.2 1.4 copy-start.2
  47.9 36.4 %copy-start.8 = (bf16[256,384]{1,0:T(8,128)(2,1)S(1)}, bf16[256,384]{1,0:T(8,128)(2,1)}, u32[]{:S(2)}) copy-start(bf16[256,384]{1,0:T(8,128)(2,1)} %get-tuple-element.155) | copy-start | bytes 589828
  47.9 55.9 %all-to-all-start.1 = ((bf16[16,400,256]{2,1,0:T(8,128)(2,1)}), bf16[16,400,256]{2,1,0:T(8,128)(2,1)S(1)}, u32[]{:S(2)}, u32[]{:S(2)}) async-start(bf16[16,400,256]{2,1,0:T(8,128)(2,1)} %pack_kv.1), calls=%async_computation.1 | async-start | bytes 6553600 | tf_op jit(solution)/shard_map/all_to_all | solution.py:324
  55.8 6.3 %collective-permute-start = (bf16[2,256,128]{2,1,0:T(8,128)(2,1)}, bf16[2,256,128]{2,1,0:T(8,128)(2,1)S(1)}, u32[]{:S(2)}, u32[]{:S(2)}) collective-permute-start(bf16[2,256,128]{2,1,0:T(8,128)(2,1)} %get-tuple-element.125), channel_id=1, source_target_pairs={{0,1},{1,0},{2,3},{3,2},{4,5},{5,4},{6,7},{7,6},{8,9},{9,8},{10,11... | collective-permute-start | bytes 393224 | tf_op jit(solution)/shard_map/ppermute | solution.py:428
  57.1 5.9 %collective-permute-start.1 = (bf16[2,256,128]{2,1,0:T(8,128)(2,1)}, bf16[2,256,128]{2,1,0:T(8,128)(2,1)S(1)}, u32[]{:S(2)}, u32[]{:S(2)}) collective-permute-start(bf16[2,256,128]{2,1,0:T(8,128)(2,1)} %get-tuple-element.126), channel_id=1, source_target_pairs={{0,2},{1,3},{2,0},{3,1},{4,6},{5,7},{6,4},{7,5},{8,10},{9,11},{10,... | collective-permute-start | bytes 393224 | tf_op jit(solution)/shard_map/ppermute | solution.py:428
  57.4 8.7 %collective-permute-start.2 = (bf16[2,256,128]{2,1,0:T(8,128)(2,1)}, bf16[2,256,128]{2,1,0:T(8,128)(2,1)S(1)}, u32[]{:S(2)}, u32[]{:S(2)}) collective-permute-start(bf16[2,256,128]{2,1,0:T(8,128)(2,1)} %get-tuple-element.127), channel_id=1, source_target_pairs={{0,3},{1,2},{2,1},{3,0},{4,7},{5,6},{6,5},{7,4},{8,11},{9,10},{10,... | collective-permute-start | bytes 393224 | tf_op jit(solution)/shard_map/ppermute | solution.py:428
  58.8 9.8 %collective-permute-start.3 = (bf16[2,256,128]{2,1,0:T(8,128)(2,1)}, bf16[2,256,128]{2,1,0:T(8,128)(2,1)S(1)}, u32[]{:S(2)}, u32[]{:S(2)}) collective-permute-start(bf16[2,256,128]{2,1,0:T(8,128)(2,1)} %get-tuple-element.128), channel_id=1, source_target_pairs={{0,4},{1,5},{2,6},{3,7},{4,0},{5,1},{6,2},{7,3},{8,12},{9,13},{10,... | collective-permute-start | bytes 393224 | tf_op jit(solution)/shard_map/ppermute | solution.py:428
  59.2 12.7 %collective-permute-start.4 = (bf16[2,256,128]{2,1,0:T(8,128)(2,1)}, bf16[2,256,128]{2,1,0:T(8,128)(2,1)S(1)}, u32[]{:S(2)}, u32[]{:S(2)}) collective-permute-start(bf16[2,256,128]{2,1,0:T(8,128)(2,1)} %get-tuple-element.129), channel_id=1, source_target_pairs={{0,5},{1,4},{2,7},{3,6},{4,1},{5,0},{6,3},{7,2},{8,13},{9,12},{10,... | collective-permute-start | bytes 393224 | tf_op jit(solution)/shard_map/ppermute | solution.py:428
  62.1 25.3 %copy-start.15 = (bf16[2,256,128]{2,1,0:T(8,128)(2,1)}, bf16[2,256,128]{2,1,0:T(8,128)(2,1)S(1)}, u32[]{:S(2)}) copy-start(bf16[2,256,128]{2,1,0:T(8,128)(2,1)S(1)} %collective-permute-done.refs_1_) | copy-start | bytes 393220
  62.1 12.0 %collective-permute-start.5 = (bf16[2,256,128]{2,1,0:T(8,128)(2,1)}, bf16[2,256,128]{2,1,0:T(8,128)(2,1)S(1)}, u32[]{:S(2)}, u32[]{:S(2)}) collective-permute-start(bf16[2,256,128]{2,1,0:T(8,128)(2,1)} %get-tuple-element.130), channel_id=1, source_target_pairs={{0,6},{1,7},{2,4},{3,5},{4,2},{5,3},{6,0},{7,1},{8,14},{9,15},{10,... | collective-permute-start | bytes 393224 | tf_op jit(solution)/shard_map/ppermute | solution.py:428
  63.0 24.4 %copy-start.16 = (bf16[2,256,128]{2,1,0:T(8,128)(2,1)}, bf16[2,256,128]{2,1,0:T(8,128)(2,1)S(1)}, u32[]{:S(2)}) copy-start(bf16[2,256,128]{2,1,0:T(8,128)(2,1)S(1)} %collective-permute-done.1.refs_2_) | copy-start | bytes 393220
  63.0 14.2 %collective-permute-start.6 = (bf16[2,256,128]{2,1,0:T(8,128)(2,1)}, bf16[2,256,128]{2,1,0:T(8,128)(2,1)S(1)}, u32[]{:S(2)}, u32[]{:S(2)}) collective-permute-start(bf16[2,256,128]{2,1,0:T(8,128)(2,1)} %get-tuple-element.131), channel_id=1, source_target_pairs={{0,7},{1,6},{2,5},{3,4},{4,3},{5,2},{6,1},{7,0},{8,15},{9,14},{10,... | collective-permute-start | bytes 393224 | tf_op jit(solution)/shard_map/ppermute | solution.py:428
  66.1 21.3 %copy-start.17 = (bf16[2,256,128]{2,1,0:T(8,128)(2,1)}, bf16[2,256,128]{2,1,0:T(8,128)(2,1)S(1)}, u32[]{:S(2)}) copy-start(bf16[2,256,128]{2,1,0:T(8,128)(2,1)S(1)} %collective-permute-done.2.refs_3_) | copy-start | bytes 393220
  68.6 18.8 %copy-start.18 = (bf16[2,256,128]{2,1,0:T(8,128)(2,1)}, bf16[2,256,128]{2,1,0:T(8,128)(2,1)S(1)}, u32[]{:S(2)}) copy-start(bf16[2,256,128]{2,1,0:T(8,128)(2,1)S(1)} %collective-permute-done.3.refs_4_) | copy-start | bytes 393220
  71.9 15.5 %copy-start.19 = (bf16[2,256,128]{2,1,0:T(8,128)(2,1)}, bf16[2,256,128]{2,1,0:T(8,128)(2,1)S(1)}, u32[]{:S(2)}) copy-start(bf16[2,256,128]{2,1,0:T(8,128)(2,1)S(1)} %collective-permute-done.4.refs_5_) | copy-start | bytes 393220
  74.1 13.3 %copy-start.20 = (bf16[2,256,128]{2,1,0:T(8,128)(2,1)}, bf16[2,256,128]{2,1,0:T(8,128)(2,1)S(1)}, u32[]{:S(2)}) copy-start(bf16[2,256,128]{2,1,0:T(8,128)(2,1)S(1)} %collective-permute-done.5.refs_6_) | copy-start | bytes 393220
  77.2 10.2 %copy-start.21 = (bf16[2,256,128]{2,1,0:T(8,128)(2,1)}, bf16[2,256,128]{2,1,0:T(8,128)(2,1)S(1)}, u32[]{:S(2)}) copy-start(bf16[2,256,128]{2,1,0:T(8,128)(2,1)S(1)} %collective-permute-done.6.refs_7_) | copy-start | bytes 393220
  77.2 5.1 %collective-permute-start.7 = (bf16[256,384]{1,0:T(8,128)(2,1)}, bf16[256,384]{1,0:T(8,128)(2,1)S(1)}, u32[]{:S(2)}, u32[]{:S(2)}) collective-permute-start(bf16[256,384]{1,0:T(8,128)(2,1)} %get-tuple-element.149), channel_id=1, source_target_pairs={{0,1},{1,0},{2,3},{3,2},{4,5},{5,4},{6,7},{7,6},{8,9},{9,8},{10,11... | collective-permute-start | bytes 589832 | tf_op jit(solution)/shard_map/ppermute | solution.py:428
  77.3 6.3 %collective-permute-start.8 = (bf16[256,384]{1,0:T(8,128)(2,1)}, bf16[256,384]{1,0:T(8,128)(2,1)S(1)}, u32[]{:S(2)}, u32[]{:S(2)}) collective-permute-start(bf16[256,384]{1,0:T(8,128)(2,1)} %get-tuple-element.150), channel_id=1, source_target_pairs={{0,2},{1,3},{2,0},{3,1},{4,6},{5,7},{6,4},{7,5},{8,10},{9,11},{10,... | collective-permute-start | bytes 589832 | tf_op jit(solution)/shard_map/ppermute | solution.py:428
  77.3 16.3 %collective-permute-start.9 = (bf16[256,384]{1,0:T(8,128)(2,1)}, bf16[256,384]{1,0:T(8,128)(2,1)S(1)}, u32[]{:S(2)}, u32[]{:S(2)}) collective-permute-start(bf16[256,384]{1,0:T(8,128)(2,1)} %get-tuple-element.151), channel_id=1, source_target_pairs={{0,3},{1,2},{2,1},{3,0},{4,7},{5,6},{6,5},{7,4},{8,11},{9,10},{10,... | collective-permute-start | bytes 589832 | tf_op jit(solution)/shard_map/ppermute | solution.py:428
  79.4 14.2 %collective-permute-start.10 = (bf16[256,384]{1,0:T(8,128)(2,1)}, bf16[256,384]{1,0:T(8,128)(2,1)S(1)}, u32[]{:S(2)}, u32[]{:S(2)}) collective-permute-start(bf16[256,384]{1,0:T(8,128)(2,1)} %get-tuple-element.152), channel_id=1, source_target_pairs={{0,4},{1,5},{2,6},{3,7},{4,0},{5,1},{6,2},{7,3},{8,12},{9,13},{10,... | collective-permute-start | bytes 589832 | tf_op jit(solution)/shard_map/ppermute | solution.py:428
  80.0 17.7 %collective-permute-start.11 = (bf16[256,384]{1,0:T(8,128)(2,1)}, bf16[256,384]{1,0:T(8,128)(2,1)S(1)}, u32[]{:S(2)}, u32[]{:S(2)}) collective-permute-start(bf16[256,384]{1,0:T(8,128)(2,1)} %get-tuple-element.153), channel_id=1, source_target_pairs={{0,5},{1,4},{2,7},{3,6},{4,1},{5,0},{6,3},{7,2},{8,13},{9,12},{10,... | collective-permute-start | bytes 589832 | tf_op jit(solution)/shard_map/ppermute | solution.py:428
  82.3 1.0 copy-start.9
  82.3 15.9 %collective-permute-start.12 = (bf16[256,384]{1,0:T(8,128)(2,1)}, bf16[256,384]{1,0:T(8,128)(2,1)S(1)}, u32[]{:S(2)}, u32[]{:S(2)}) collective-permute-start(bf16[256,384]{1,0:T(8,128)(2,1)} %get-tuple-element.154), channel_id=1, source_target_pairs={{0,6},{1,7},{2,4},{3,5},{4,2},{5,3},{6,0},{7,1},{8,14},{9,15},{10,... | collective-permute-start | bytes 589832 | tf_op jit(solution)/shard_map/ppermute | solution.py:428
  83.6 0.7 copy-start.10
  84.3 19.0 %collective-permute-start.13 = (bf16[256,384]{1,0:T(8,128)(2,1)S(1)}, bf16[256,384]{1,0:T(8,128)(2,1)}, u32[]{:S(2)}, u32[]{:S(2)}) collective-permute-start(bf16[256,384]{1,0:T(8,128)(2,1)S(1)} %copy-done.8), channel_id=1, source_target_pairs={{0,7},{1,6},{2,5},{3,4},{4,3},{5,2},{6,1},{7,0},{8,15},{9,14},{10,... | collective-permute-start | bytes 589832 | tf_op jit(solution)/shard_map/ppermute | solution.py:428
  93.6 4.6 %copy-start.11 = (bf16[256,384]{1,0:T(8,128)(2,1)}, bf16[256,384]{1,0:T(8,128)(2,1)S(1)}, u32[]{:S(2)}) copy-start(bf16[256,384]{1,0:T(8,128)(2,1)S(1)} %collective-permute-done.9.refs_3_) | copy-start | bytes 589828
  93.6 4.6 %copy-start.12 = (bf16[256,384]{1,0:T(8,128)(2,1)}, bf16[256,384]{1,0:T(8,128)(2,1)S(1)}, u32[]{:S(2)}) copy-start(bf16[256,384]{1,0:T(8,128)(2,1)S(1)} %collective-permute-done.10.refs_4_) | copy-start | bytes 589828
  97.7 0.7 copy-start.13
  98.3 0.7 copy-start.14
  103.9 19.3 %copy-start = (bf16[16,400,256]{2,1,0:T(8,128)(2,1)}, bf16[16,400,256]{2,1,0:T(8,128)(2,1)S(1)}, u32[]{:S(2)}) copy-start(bf16[16,400,256]{2,1,0:T(8,128)(2,1)S(1)} %all-to-all-done.1.in_ref.meta_ref) | copy-start | bytes 9830404
  103.9 31.9 %all-to-all-start.2 = ((bf16[16,192,256]{2,1,0:T(8,128)(2,1)}), bf16[16,192,256]{2,1,0:T(8,128)(2,1)}, u32[]{:S(2)}, u32[]{:S(2)}) async-start(bf16[16,192,256]{2,1,0:T(8,128)(2,1)} %pack_last.1), calls=%async_computation.2 | async-start | bytes 3145728 | tf_op jit(solution)/shard_map/all_to_all | solution.py:324
  123.2 16.3 %copy-start.5 = (s32[3,256,16]{1,2,0:T(8,128)S(1)}, s32[3,256,16]{1,2,0:T(8,128)}, u32[]{:S(2)}) copy-start(s32[3,256,16]{1,2,0:T(8,128)} %param.11) | copy-start | bytes 147460
  135.8 37.6 %all-to-all-start.3 = ((bf16[16,3,192,128]{3,2,1,0:T(8,128)(2,1)}), bf16[16,3,192,128]{3,2,1,0:T(8,128)(2,1)S(1)}, u32[]{:S(2)}, u32[]{:S(2)}) async-start(bf16[16,3,192,128]{3,2,1,0:T(8,128)(2,1)} %pack_q.1), calls=%async_computation.3 | async-start | bytes 4718592 | tf_op jit(solution)/shard_map/all_to_all | solution.py:324
  173.4 100.3 %copy-start.1 = (bf16[16,3,192,128]{3,2,1,0:T(8,128)(2,1)}, bf16[16,3,192,128]{3,2,1,0:T(8,128)(2,1)S(1)}, u32[]{:S(2)}) copy-start(bf16[16,3,192,128]{3,2,1,0:T(8,128)(2,1)S(1)} %all-to-all-done.3.in_ref) | copy-start | bytes 7077892
  273.7 58.2 %all-to-all-start.5 = ((bf16[16,1,4,128,256]{4,3,2,1,0:T(8,128)(2,1)}), bf16[16,1,4,128,256]{4,3,2,1,0:T(8,128)(2,1)}, u32[]{:S(2)}, u32[]{:S(2)}) async-start(bf16[16,1,4,128,256]{4,3,2,1,0:T(8,128)(2,1)} %get-tuple-element.172), calls=%async_computation.5 | async-start | bytes 8388608 | tf_op jit(solution)/shard_map/all_to_all | solution.py:324
  331.8 27.1 %all-to-all-start.7 = ((bf16[16,2,192,128]{3,2,1,0:T(8,128)(2,1)}), bf16[16,2,192,128]{3,2,1,0:T(8,128)(2,1)S(1)}, u32[]{:S(2)}, u32[]{:S(2)}) async-start(bf16[16,2,192,128]{3,2,1,0:T(8,128)(2,1)} %attend_0.1), calls=%async_computation.7 | async-start | bytes 3145728 | tf_op jit(solution)/shard_map/all_to_all | solution.py:324
  358.9 5.4 %copy-start.3 = (bf16[16,2,192,128]{3,2,1,0:T(8,128)(2,1)}, bf16[16,2,192,128]{3,2,1,0:T(8,128)(2,1)S(1)}, u32[]{:S(2)}) copy-start(bf16[16,2,192,128]{3,2,1,0:T(8,128)(2,1)S(1)} %all-to-all-done.7.in_ref) | copy-start | bytes 4718596
  358.9 17.7 %all-to-all-start.6 = ((bf16[16,1,192,128]{3,2,1,0:T(8,128)(2,1)}), bf16[16,1,192,128]{3,2,1,0:T(8,128)(2,1)S(1)}, u32[]{:S(2)}, u32[]{:S(2)}) async-start(bf16[16,1,192,128]{3,2,1,0:T(8,128)(2,1)} %attend_2.1), calls=%async_computation.6 | async-start | bytes 1572864 | tf_op jit(solution)/shard_map/all_to_all | solution.py:324
  376.6 0.9 copy-start.4

commit v6 on v5

--- a/solution.py
+++ b/solution.py
@@ -13,7 +13,7 @@
 KCAP = 4
 LANES = 128
 META = 16
-VMEM_LIMIT = 56 * 1024 * 1024
+VMEM_LIMIT = 63 * 1024 * 1024
 BF16 = jnp.bfloat16
 F32 = jnp.float32
 I32 = jnp.int32

time: 413 us -> 412 us (level)
  transfers between devices with their start and end apart: 21 -> 21, of which waited for: 16 -> 15; matrix products, arithmetic and copies ran while one was open for 1% -> 1% of each run, Pallas kernels for 29% -> 29%
where the time goes in v6:
time: 412 us; the launch traced here: 411 us
  Pallas kernels  138 us (33%)
  blocking collectives  128 us (31%)
  waiting for transfers between devices  76.5 us (19%)
  starting transfers between devices  59.8 us (15%)
  local copies, waits for them, and re-layouts  6.79 us (2%)
    all_to_all x2, blocking collectives, exchange(): return lax.all_to_all(array, axis, split_axis=0, concat_axis=0, tiled=True)  128 us
    all_to_all x7, waiting for transfers between devices, exchange(): return lax.all_to_all(array, axis, split_axis=0, concat_axis=0, tiled=True)  54.6 us
    pallas_call x2, Pallas kernels, per_device(): pl.pallas_call(functools.partial(attend_kernel, first=first), grid_spec=p...  46.5 us
    all_to_all x7, starting transfers between devices, exchange(): return lax.all_to_all(array, axis, split_axis=0, concat_axis=0, tiled=True)  41.1 us
    ppermute x14, waiting for transfers between devices, to_partner(): return lax.ppermute(array, 'head', [(i, i ^ k) for i in range(parts)])  21.9 us
    pallas_call x1, Pallas kernels, per_device(): pl.pallas_call(unpack_kv_kernel, grid_spec=pltpu.PrefetchScalarGridSpec(n...  21.4 us
    ppermute x14, starting transfers between devices, to_partner(): return lax.ppermute(array, 'head', [(i, i ^ k) for i in range(parts)])  18.7 us
    pallas_call x1, Pallas kernels, per_device(): pl.pallas_call(pack_q_kernel, grid_spec=pltpu.PrefetchScalarGridSpec(num_...  13.1 us
  transfers between devices with their start and end apart: 21, of which 15 were waited for; matrix products, arithmetic and copies ran while one was open for 1% of the time, Pallas kernels for 29%

profile of v6, /device:TPU:1, one launch (start us, length us, event | category | flops | bytes accessed | tf_op | source)
XLA Modules:
  0.0 410.9 jit_solution(12854858603718882049)
XLA Ops:
  0.0 4.0 split_kv.1
  4.0 5.9 %all-to-all-start = ((bf16[8,2,256,256]{3,2,1,0:T(8,128)(2,1)}), bf16[8,2,256,256]{3,2,1,0:T(8,128)(2,1)}, u32[]{:S(2)}, u32[]{:S(2)}) async-start(bf16[8,2,256,256]{3,2,1,0:T(8,128)(2,1)} %split_kv.1), calls=%async_computation | async-start | bytes 4194304 | tf_op jit(solution)/shard_map/all_to_all | solution.py:324
  10.0 0.6 copy.19
  10.6 3.7 split_rest.1
  14.3 11.5 %slots.1 = (s32[6,16,128]{2,1,0:T(8,128)}, f32[6,16,128]{2,1,0:T(8,128)}) custom-call(s32[6,16,128]{2,1,0:T(8,128)} %bitcast.19), custom_call_target="tpu_custom_call" | custom-call | flops 6000000000 | bytes 1000000 | tf_op jit(solution)/shard_map/slots/pallas_call | solution.py:391
  25.7 10.7 %all-to-all-done.key_ref.value_ref = bf16[8,2,256,256]{3,2,1,0:T(8,128)(2,1)} async-done(((bf16[8,2,256,256]{3,2,1,0:T(8,128)(2,1)}), bf16[8,2,256,256]{3,2,1,0:T(8,128)(2,1)}, u32[]{:S(2)}, u32[]{:S(2)}) %all-to-all-start) | async-done | bytes 2097184 | tf_op jit(solution)/shard_map/all_to_all | solution.py:324
  36.4 10.4 %pack_kv.1 = bf16[16,400,256]{2,1,0:T(8,128)(2,1)} custom-call(s32[6,16,128]{2,1,0:T(8,128)} %get-tuple-element.89.slot_ref.index_ref, f32[6,16,128]{2,1,0:T(8,128)} %get-tuple-element.122.count_ref, bf16[8,2,256,256]{3,2,1,0:T(8,128)(2,1)} %all-to-all-done.key_ref.value_ref, bf16[8,2,256,256]{3,2,1,0:T(8,128)(2,1)} %all-to-all-done.key_ref.value_ref), custom_call_target="tpu_custom_call" | custom-call | flops 6442450944 | bytes 8000000 | tf_op jit(solution)/shard_map/pack_kv/pallas_call | solution.py:410
  46.9 8.0 %all-to-all-start.1 = ((bf16[16,400,256]{2,1,0:T(8,128)(2,1)}), bf16[16,400,256]{2,1,0:T(8,128)(2,1)}, u32[]{:S(2)}, u32[]{:S(2)}) async-start(bf16[16,400,256]{2,1,0:T(8,128)(2,1)} %pack_kv.1), calls=%async_computation.1 | async-start | bytes 6553600 | tf_op jit(solution)/shard_map/all_to_all | solution.py:324
  54.9 1.2 collective-permute-start
  56.1 0.3 collective-permute-start.1
  56.4 1.4 collective-permute-start.2
  57.8 0.5 collective-permute-start.3
  58.3 2.8 collective-permute-start.4
  61.1 1.0 collective-permute-start.5
  62.1 2.1 collective-permute-start.6
  64.2 0.8 collective-permute-done.2.refs_3_
  65.0 2.5 collective-permute-done.3.refs_4_
  67.5 3.3 collective-permute-done.4.refs_5_
  70.8 2.3 collective-permute-done.5.refs_6_
  73.1 3.1 collective-permute-done.6.refs_7_
  76.4 2.0 collective-permute-start.9
  78.4 0.7 collective-permute-start.10
  79.1 2.3 collective-permute-start.11
  81.4 1.2 collective-permute-start.12
  82.7 0.7 copy-done.12
  83.4 2.9 collective-permute-start.13
  86.3 6.1 %pack_last.1 = bf16[16,192,256]{2,1,0:T(8,128)(2,1)} custom-call(s32[1]{0:T(128)} %bitcast.1.me_ref, s32[6,16,128]{2,1,0:T(8,128)} %get-tuple-element.89.slot_ref.index_ref, bf16[2,256,128]{2,1,0:T(8,128)(2,1)} %get-tuple-element.140.refs_0_, bf16[2,256,128]{2,1,0:T(8,128)(2,1)} %copy-done.13, bf16[2,256,128]{2,1,0:T(8,128)(2,1)} %copy-done.14, ...), custom_call_target="tpu_custom_call" | custom-call | flops 3221225472 | bytes 3000000 | tf_op jit(solution)/shard_map/pack_last/pallas_call | solution.py:436
  92.5 4.3 %collective-permute-done.11.refs_5_ = bf16[256,384]{1,0:T(8,128)(2,1)} collective-permute-done((bf16[256,384]{1,0:T(8,128)(2,1)S(1)}, bf16[256,384]{1,0:T(8,128)(2,1)}, u32[]{:S(2)}, u32[]{:S(2)}) %collective-permute-start.11) | collective-permute-done | bytes 196640 | tf_op jit(solution)/shard_map/ppermute | solution.py:428
  96.7 0.5 collective-permute-done.12.refs_6_
  97.3 5.1 %collective-permute-done.13.refs_7_ = bf16[256,384]{1,0:T(8,128)(2,1)} collective-permute-done((bf16[256,384]{1,0:T(8,128)(2,1)S(1)}, bf16[256,384]{1,0:T(8,128)(2,1)}, u32[]{:S(2)}, u32[]{:S(2)}) %collective-permute-start.13) | collective-permute-done | bytes 196640 | tf_op jit(solution)/shard_map/ppermute | solution.py:428
  102.3 0.6 all-to-all-done.1.in_ref.meta_ref
  102.9 6.0 %all-to-all-start.2 = ((bf16[16,192,256]{2,1,0:T(8,128)(2,1)}), bf16[16,192,256]{2,1,0:T(8,128)(2,1)}, u32[]{:S(2)}, u32[]{:S(2)}) async-start(bf16[16,192,256]{2,1,0:T(8,128)(2,1)} %pack_last.1), calls=%async_computation.2 | async-start | bytes 3145728 | tf_op jit(solution)/shard_map/all_to_all | solution.py:324
  108.9 13.1 %pack_q.1 = bf16[16,3,192,128]{3,2,1,0:T(8,128)(2,1)} custom-call(s32[1]{0:T(128)} %bitcast.1.me_ref, s32[6,16,128]{2,1,0:T(8,128)} %get-tuple-element.89.slot_ref.index_ref, bf16[256,384]{1,0:T(8,128)(2,1)} %get-tuple-element.156.refs_0_, bf16[256,384]{1,0:T(8,128)(2,1)} %copy-done.11, bf16[256,384]{1,0:T(8,128)(2,1)} %copy-done.12, ...), custom_call_target="tpu_custom_call" | custom-call | flops 9663676416 | bytes 4000000 | tf_op jit(solution)/shard_map/pack_q/pallas_call | solution.py:453
  122.0 11.8 %all-to-all-done.2.last_in_ref = bf16[16,192,256]{2,1,0:T(8,128)(2,1)} async-done(((bf16[16,192,256]{2,1,0:T(8,128)(2,1)}), bf16[16,192,256]{2,1,0:T(8,128)(2,1)}, u32[]{:S(2)}, u32[]{:S(2)}) %all-to-all-start.2) | async-done | bytes 1572896 | tf_op jit(solution)/shard_map/all_to_all | solution.py:324
  133.9 4.5 %all-to-all-start.3 = ((bf16[16,3,192,128]{3,2,1,0:T(8,128)(2,1)}), bf16[16,3,192,128]{3,2,1,0:T(8,128)(2,1)}, u32[]{:S(2)}, u32[]{:S(2)}) async-start(bf16[16,3,192,128]{3,2,1,0:T(8,128)(2,1)} %pack_q.1), calls=%async_computation.3 | async-start | bytes 4718592 | tf_op jit(solution)/shard_map/all_to_all | solution.py:324
  138.4 0.2 copy.11
  138.5 0.2 reshape.35
  138.7 1.0 compare_reduce_fusion
  139.7 0.1 convolution_convert_fusion
  139.8 0.3 select_reduce_fusion.1
  140.1 0.7 copy.12.pick_ref
  140.9 21.4 %unpack_kv.1 = (bf16[16,2,4,128,256]{4,3,2,1,0:T(8,128)(2,1)}, bf16[16,1,4,128,256]{4,3,2,1,0:T(8,128)(2,1)}, s32[3,16,128]{2,1,0:T(8,128)}) custom-call(s32[3,16,4]{2,1,0:T(8,128)} %copy.12.pick_ref, bf16[16,400,256]{2,1,0:T(8,128)(2,1)} %all-to-all-done.1.in_ref.meta_ref, bf16[16,192,256]{2,1,0:T(8,128)(2,1)} %all-to-all-done.2.last_in_ref, ...), custom_call_target="tpu_custom_call" | custom-call | flops 9663676416 | bytes 18000000 | tf_op jit(solution)/shard_map/unpack_kv/pallas_call | solution.py:472
  162.2 9.6 %all-to-all-done.3.in_ref = bf16[16,3,192,128]{3,2,1,0:T(8,128)(2,1)} async-done(((bf16[16,3,192,128]{3,2,1,0:T(8,128)(2,1)}), bf16[16,3,192,128]{3,2,1,0:T(8,128)(2,1)}, u32[]{:S(2)}, u32[]{:S(2)}) %all-to-all-start.3) | async-done | bytes 2359328 | tf_op jit(solution)/shard_map/all_to_all | solution.py:324
  171.8 99.8 %all_to_all.45.recv_ref = bf16[16,2,4,128,256]{4,3,2,1,0:T(8,128)(2,1)} all-to-all(bf16[16,2,4,128,256]{4,3,2,1,0:T(8,128)(2,1)} %get-tuple-element.169), channel_id=1, replica_groups=mesh['seq'=16,'head'=8] {'seq'}, dimensions={0} | all-to-all | bytes 16777216 | tf_op jit(solution)/shard_map/all_to_all | solution.py:324
  271.6 4.8 %all-to-all-start.5 = ((bf16[16,1,4,128,256]{4,3,2,1,0:T(8,128)(2,1)}), bf16[16,1,4,128,256]{4,3,2,1,0:T(8,128)(2,1)}, u32[]{:S(2)}, u32[]{:S(2)}) async-start(bf16[16,1,4,128,256]{4,3,2,1,0:T(8,128)(2,1)} %get-tuple-element.172), calls=%async_computation.5 | async-start | bytes 8388608 | tf_op jit(solution)/shard_map/all_to_all | solution.py:324
  276.4 0.2 fusion.1
  276.6 0.1 reshape.36
  276.8 0.1 broadcast_in_dim.30
  276.9 0.3 select_reduce_fusion
  277.3 0.7 reshape.37.fetch_ref
  278.0 9.5 %unpack_q.1.query_ref = bf16[3,2048,128]{2,1,0:T(8,128)(2,1)} custom-call(s32[3,16,128]{2,1,0:T(8,128)} %get-tuple-element.170.index_ref, bf16[16,3,192,128]{3,2,1,0:T(8,128)(2,1)} %all-to-all-done.3.in_ref), custom_call_target="tpu_custom_call" | custom-call | flops 9663676416 | bytes 4000000 | tf_op jit(solution)/shard_map/unpack_q/pallas_call | solution.py:510
  287.4 29.2 %attend_0.1 = bf16[16,2,192,128]{3,2,1,0:T(8,128)(2,1)} custom-call(s32[3,16,16]{2,1,0:T(8,128)} %reshape.37.fetch_ref, s32[3,16,128]{2,1,0:T(8,128)} %get-tuple-element.170.index_ref, bf16[3,2048,128]{2,1,0:T(8,128)(2,1)} %unpack_q.1.query_ref, bf16[16,2,4,128,256]{4,3,2,1,0:T(8,128)(2,1)} %all_to_all.45.recv_ref), custom_call_target="tpu_custom_call" | custom-call | flops 4294967296 | bytes 12000000 | tf_op jit(solution)/shard_map/attend_0/pallas_call | solution.py:527
  316.6 14.3 %all-to-all-done.5.recv_ref = bf16[16,1,4,128,256]{4,3,2,1,0:T(8,128)(2,1)} async-done(((bf16[16,1,4,128,256]{4,3,2,1,0:T(8,128)(2,1)}), bf16[16,1,4,128,256]{4,3,2,1,0:T(8,128)(2,1)}, u32[]{:S(2)}, u32[]{:S(2)}) %all-to-all-start.5) | async-done | bytes 4194336 | tf_op jit(solution)/shard_map/all_to_all | solution.py:324
  330.9 6.1 %all-to-all-start.7 = ((bf16[16,2,192,128]{3,2,1,0:T(8,128)(2,1)}), bf16[16,2,192,128]{3,2,1,0:T(8,128)(2,1)}, u32[]{:S(2)}, u32[]{:S(2)}) async-start(bf16[16,2,192,128]{3,2,1,0:T(8,128)(2,1)} %attend_0.1), calls=%async_computation.7 | async-start | bytes 3145728 | tf_op jit(solution)/shard_map/all_to_all | solution.py:324
  337.0 17.3 %attend_2.1 = bf16[16,1,192,128]{3,2,1,0:T(8,128)(2,1)} custom-call(s32[3,16,16]{2,1,0:T(8,128)} %reshape.37.fetch_ref, s32[3,16,128]{2,1,0:T(8,128)} %get-tuple-element.170.index_ref, bf16[3,2048,128]{2,1,0:T(8,128)(2,1)} %unpack_q.1.query_ref, bf16[16,1,4,128,256]{4,3,2,1,0:T(8,128)(2,1)} %all-to-all-done.5.recv_ref), custom_call_target="tpu_custom_call" | custom-call | flops 2147483648 | bytes 6000000 | tf_op jit(solution)/shard_map/attend_2/pallas_call | solution.py:527
  354.4 2.6 all-to-all-done.7.in_ref
  356.9 5.9 %all-to-all-start.6 = ((bf16[16,1,192,128]{3,2,1,0:T(8,128)(2,1)}), bf16[16,1,192,128]{3,2,1,0:T(8,128)(2,1)S(1)}, u32[]{:S(2)}, u32[]{:S(2)}) async-start(bf16[16,1,192,128]{3,2,1,0:T(8,128)(2,1)} %attend_2.1), calls=%async_computation.6 | async-start | bytes 1572864 | tf_op jit(solution)/shard_map/all_to_all | solution.py:324
  362.9 7.0 %final_0.1.refs_0_ = bf16[8,256,384]{2,1,0:T(8,128)(2,1)} custom-call(s32[6,16,128]{2,1,0:T(8,128)} %get-tuple-element.89.slot_ref.index_ref, bf16[16,2,192,128]{3,2,1,0:T(8,128)(2,1)} %all-to-all-done.7.in_ref), custom_call_target="tpu_custom_call" | custom-call | flops 6442450944 | bytes 2000000 | tf_op jit(solution)/shard_map/final_0/pallas_call | solution.py:555
  369.8 5.1 %all-to-all-done.6.in_ref = bf16[16,1,192,128]{3,2,1,0:T(8,128)(2,1)S(1)} async-done(((bf16[16,1,192,128]{3,2,1,0:T(8,128)(2,1)}), bf16[16,1,192,128]{3,2,1,0:T(8,128)(2,1)S(1)}, u32[]{:S(2)}, u32[]{:S(2)}) %all-to-all-start.6) | async-done | bytes 786464 | tf_op jit(solution)/shard_map/all_to_all | solution.py:324
  375.0 0.9 copy-done
  375.8 4.4 %final_2.1 = bf16[8,256,384]{2,1,0:T(8,128)(2,1)} custom-call(s32[6,16,128]{2,1,0:T(8,128)} %get-tuple-element.89.slot_ref.index_ref, bf16[16,1,192,128]{3,2,1,0:T(8,128)(2,1)} %copy-done, bf16[8,256,384]{2,1,0:T(8,128)(2,1)} %final_0.1.refs_0_), custom_call_target="tpu_custom_call", output_to_operand_aliasing={{}: (2, {})} | custom-call | flops 3221225472 | bytes 2000000 | tf_op jit(solution)/shard_map/final_2/pallas_call | solution.py:555
  380.3 28.1 %all_to_all.46 = bf16[8,256,384]{2,1,0:T(8,128)(2,1)S(1)} all-to-all(bf16[8,256,384]{2,1,0:T(8,128)(2,1)} %final_2.1), channel_id=1, replica_groups=mesh['seq'=16,'head'=8] {'head'}, dimensions={0} | all-to-all | bytes 3145728 | tf_op jit(solution)/shard_map/all_to_all | solution.py:324
  408.4 0.7 copy.13
  409.1 1.7 copy.14
  (66 shorter events, 0.4 us)
Async XLA Ops:
  4.0 5.9 %copy-start.2 = (s32[3,2048]{1,0:T(4,128)S(1)}, s32[3,2048]{1,0:T(4,128)}, u32[]{:S(2)}) copy-start(s32[3,2048]{1,0:T(4,128)} %param.10) | copy-start | bytes 73732
  4.0 5.9 %copy-start.3 = (s32[3,2048]{1,0:T(4,128)S(1)}, s32[3,2048]{1,0:T(4,128)}, u32[]{:S(2)}) copy-start(s32[3,2048]{1,0:T(4,128)} %param.9) | copy-start | bytes 73732
  4.0 32.4 %all-to-all-start = ((bf16[8,2,256,256]{3,2,1,0:T(8,128)(2,1)}), bf16[8,2,256,256]{3,2,1,0:T(8,128)(2,1)}, u32[]{:S(2)}, u32[]{:S(2)}) async-start(bf16[8,2,256,256]{3,2,1,0:T(8,128)(2,1)} %split_kv.1), calls=%async_computation | async-start | bytes 4194304 | tf_op jit(solution)/shard_map/all_to_all | solution.py:324
  46.8 8.1 %copy-start.26 = (bf16[2,256,128]{2,1,0:T(8,128)(2,1)S(1)}, bf16[2,256,128]{2,1,0:T(8,128)(2,1)}, u32[]{:S(2)}) copy-start(bf16[2,256,128]{2,1,0:T(8,128)(2,1)} %get-tuple-element.125) | copy-start | bytes 393220
  46.8 9.3 %copy-start.25 = (bf16[2,256,128]{2,1,0:T(8,128)(2,1)S(1)}, bf16[2,256,128]{2,1,0:T(8,128)(2,1)}, u32[]{:S(2)}) copy-start(bf16[2,256,128]{2,1,0:T(8,128)(2,1)} %get-tuple-element.126) | copy-start | bytes 393220
  46.8 9.6 %copy-start.23 = (bf16[2,256,128]{2,1,0:T(8,128)(2,1)S(1)}, bf16[2,256,128]{2,1,0:T(8,128)(2,1)}, u32[]{:S(2)}) copy-start(bf16[2,256,128]{2,1,0:T(8,128)(2,1)} %get-tuple-element.127) | copy-start | bytes 393220
  46.8 11.1 %copy-start.21 = (bf16[2,256,128]{2,1,0:T(8,128)(2,1)S(1)}, bf16[2,256,128]{2,1,0:T(8,128)(2,1)}, u32[]{:S(2)}) copy-start(bf16[2,256,128]{2,1,0:T(8,128)(2,1)} %get-tuple-element.128) | copy-start | bytes 393220
  46.8 11.5 %copy-start.20 = (bf16[2,256,128]{2,1,0:T(8,128)(2,1)S(1)}, bf16[2,256,128]{2,1,0:T(8,128)(2,1)}, u32[]{:S(2)}) copy-start(bf16[2,256,128]{2,1,0:T(8,128)(2,1)} %get-tuple-element.129) | copy-start | bytes 393220
  46.8 14.3 %copy-start.19 = (bf16[2,256,128]{2,1,0:T(8,128)(2,1)S(1)}, bf16[2,256,128]{2,1,0:T(8,128)(2,1)}, u32[]{:S(2)}) copy-start(bf16[2,256,128]{2,1,0:T(8,128)(2,1)} %get-tuple-element.130) | copy-start | bytes 393220
  46.8 15.3 %copy-start.17 = (bf16[2,256,128]{2,1,0:T(8,128)(2,1)S(1)}, bf16[2,256,128]{2,1,0:T(8,128)(2,1)}, u32[]{:S(2)}) copy-start(bf16[2,256,128]{2,1,0:T(8,128)(2,1)} %get-tuple-element.131) | copy-start | bytes 393220
  46.8 29.4 %copy-start.10 = (bf16[256,384]{1,0:T(8,128)(2,1)S(1)}, bf16[256,384]{1,0:T(8,128)(2,1)}, u32[]{:S(2)}) copy-start(bf16[256,384]{1,0:T(8,128)(2,1)} %get-tuple-element.149) | copy-start | bytes 589828
  46.8 29.5 %copy-start.9 = (bf16[256,384]{1,0:T(8,128)(2,1)S(1)}, bf16[256,384]{1,0:T(8,128)(2,1)}, u32[]{:S(2)}) copy-start(bf16[256,384]{1,0:T(8,128)(2,1)} %get-tuple-element.150) | copy-start | bytes 589828
  46.8 29.6 %copy-start.8 = (bf16[256,384]{1,0:T(8,128)(2,1)S(1)}, bf16[256,384]{1,0:T(8,128)(2,1)}, u32[]{:S(2)}) copy-start(bf16[256,384]{1,0:T(8,128)(2,1)} %get-tuple-element.151) | copy-start | bytes 589828
  46.8 31.6 %copy-start.7 = (bf16[256,384]{1,0:T(8,128)(2,1)S(1)}, bf16[256,384]{1,0:T(8,128)(2,1)}, u32[]{:S(2)}) copy-start(bf16[256,384]{1,0:T(8,128)(2,1)} %get-tuple-element.152) | copy-start | bytes 589828
  46.9 32.3 %copy-start.6 = (bf16[256,384]{1,0:T(8,128)(2,1)S(1)}, bf16[256,384]{1,0:T(8,128)(2,1)}, u32[]{:S(2)}) copy-start(bf16[256,384]{1,0:T(8,128)(2,1)} %get-tuple-element.153) | copy-start | bytes 589828
  46.9 34.5 %copy-start.5 = (bf16[256,384]{1,0:T(8,128)(2,1)S(1)}, bf16[256,384]{1,0:T(8,128)(2,1)}, u32[]{:S(2)}) copy-start(bf16[256,384]{1,0:T(8,128)(2,1)} %get-tuple-element.154) | copy-start | bytes 589828
  46.9 36.5 %copy-start.4 = (bf16[256,384]{1,0:T(8,128)(2,1)S(1)}, bf16[256,384]{1,0:T(8,128)(2,1)}, u32[]{:S(2)}) copy-start(bf16[256,384]{1,0:T(8,128)(2,1)} %get-tuple-element.155) | copy-start | bytes 589828
  46.9 56.0 %all-to-all-start.1 = ((bf16[16,400,256]{2,1,0:T(8,128)(2,1)}), bf16[16,400,256]{2,1,0:T(8,128)(2,1)}, u32[]{:S(2)}, u32[]{:S(2)}) async-start(bf16[16,400,256]{2,1,0:T(8,128)(2,1)} %pack_kv.1), calls=%async_computation.1 | async-start | bytes 6553600 | tf_op jit(solution)/shard_map/all_to_all | solution.py:324
  54.9 6.3 %collective-permute-start = (bf16[2,256,128]{2,1,0:T(8,128)(2,1)S(1)}, bf16[2,256,128]{2,1,0:T(8,128)(2,1)S(1)}, u32[]{:S(2)}, u32[]{:S(2)}) collective-permute-start(bf16[2,256,128]{2,1,0:T(8,128)(2,1)S(1)} %copy-done.26), channel_id=1, source_target_pairs={{0,1},{1,0},{2,3},{3,2},{4,5},{5,4},{6,7},{7,6},{8,9},{9,8},{10,11... | collective-permute-start | bytes 393224 | tf_op jit(solution)/shard_map/ppermute | solution.py:428
  56.1 6.0 %collective-permute-start.1 = (bf16[2,256,128]{2,1,0:T(8,128)(2,1)S(1)}, bf16[2,256,128]{2,1,0:T(8,128)(2,1)S(1)}, u32[]{:S(2)}, u32[]{:S(2)}) collective-permute-start(bf16[2,256,128]{2,1,0:T(8,128)(2,1)S(1)} %copy-done.25), channel_id=1, source_target_pairs={{0,2},{1,3},{2,0},{3,1},{4,6},{5,7},{6,4},{7,5},{8,10},{9,11},{10,... | collective-permute-start | bytes 393224 | tf_op jit(solution)/shard_map/ppermute | solution.py:428
  56.4 8.6 %collective-permute-start.2 = (bf16[2,256,128]{2,1,0:T(8,128)(2,1)S(1)}, bf16[2,256,128]{2,1,0:T(8,128)(2,1)S(1)}, u32[]{:S(2)}, u32[]{:S(2)}) collective-permute-start(bf16[2,256,128]{2,1,0:T(8,128)(2,1)S(1)} %copy-done.23), channel_id=1, source_target_pairs={{0,3},{1,2},{2,1},{3,0},{4,7},{5,6},{6,5},{7,4},{8,11},{9,10},{10,... | collective-permute-start | bytes 393224 | tf_op jit(solution)/shard_map/ppermute | solution.py:428
  57.8 9.7 %collective-permute-start.3 = (bf16[2,256,128]{2,1,0:T(8,128)(2,1)S(1)}, bf16[2,256,128]{2,1,0:T(8,128)(2,1)S(1)}, u32[]{:S(2)}, u32[]{:S(2)}) collective-permute-start(bf16[2,256,128]{2,1,0:T(8,128)(2,1)S(1)} %copy-done.21), channel_id=1, source_target_pairs={{0,4},{1,5},{2,6},{3,7},{4,0},{5,1},{6,2},{7,3},{8,12},{9,13},{10,... | collective-permute-start | bytes 393224 | tf_op jit(solution)/shard_map/ppermute | solution.py:428
  58.3 12.5 %collective-permute-start.4 = (bf16[2,256,128]{2,1,0:T(8,128)(2,1)S(1)}, bf16[2,256,128]{2,1,0:T(8,128)(2,1)S(1)}, u32[]{:S(2)}, u32[]{:S(2)}) collective-permute-start(bf16[2,256,128]{2,1,0:T(8,128)(2,1)S(1)} %copy-done.20), channel_id=1, source_target_pairs={{0,5},{1,4},{2,7},{3,6},{4,1},{5,0},{6,3},{7,2},{8,13},{9,12},{10,... | collective-permute-start | bytes 393224 | tf_op jit(solution)/shard_map/ppermute | solution.py:428
  61.1 12.0 %copy-start.13 = (bf16[2,256,128]{2,1,0:T(8,128)(2,1)}, bf16[2,256,128]{2,1,0:T(8,128)(2,1)S(1)}, u32[]{:S(2)}) copy-start(bf16[2,256,128]{2,1,0:T(8,128)(2,1)S(1)} %collective-permute-done.refs_1_) | copy-start | bytes 393220
  61.1 12.0 %collective-permute-start.5 = (bf16[2,256,128]{2,1,0:T(8,128)(2,1)S(1)}, bf16[2,256,128]{2,1,0:T(8,128)(2,1)S(1)}, u32[]{:S(2)}, u32[]{:S(2)}) collective-permute-start(bf16[2,256,128]{2,1,0:T(8,128)(2,1)S(1)} %copy-done.19), channel_id=1, source_target_pairs={{0,6},{1,7},{2,4},{3,5},{4,2},{5,3},{6,0},{7,1},{8,14},{9,15},{10,... | collective-permute-start | bytes 393224 | tf_op jit(solution)/shard_map/ppermute | solution.py:428
  62.1 11.0 %copy-start.14 = (bf16[2,256,128]{2,1,0:T(8,128)(2,1)}, bf16[2,256,128]{2,1,0:T(8,128)(2,1)S(1)}, u32[]{:S(2)}) copy-start(bf16[2,256,128]{2,1,0:T(8,128)(2,1)S(1)} %collective-permute-done.1.refs_2_) | copy-start | bytes 393220
  62.1 14.1 %collective-permute-start.6 = (bf16[2,256,128]{2,1,0:T(8,128)(2,1)S(1)}, bf16[2,256,128]{2,1,0:T(8,128)(2,1)S(1)}, u32[]{:S(2)}, u32[]{:S(2)}) collective-permute-start(bf16[2,256,128]{2,1,0:T(8,128)(2,1)S(1)} %copy-done.17), channel_id=1, source_target_pairs={{0,7},{1,6},{2,5},{3,4},{4,3},{5,2},{6,1},{7,0},{8,15},{9,14},{10,... | collective-permute-start | bytes 393224 | tf_op jit(solution)/shard_map/ppermute | solution.py:428
  65.0 11.2 %copy-start.15 = (bf16[2,256,128]{2,1,0:T(8,128)(2,1)}, bf16[2,256,128]{2,1,0:T(8,128)(2,1)S(1)}, u32[]{:S(2)}) copy-start(bf16[2,256,128]{2,1,0:T(8,128)(2,1)S(1)} %collective-permute-done.2.refs_3_) | copy-start | bytes 393220
  67.5 15.1 %copy-start.16 = (bf16[2,256,128]{2,1,0:T(8,128)(2,1)}, bf16[2,256,128]{2,1,0:T(8,128)(2,1)S(1)}, u32[]{:S(2)}) copy-start(bf16[2,256,128]{2,1,0:T(8,128)(2,1)S(1)} %collective-permute-done.3.refs_4_) | copy-start | bytes 393220
  70.8 11.8 %copy-start.18 = (bf16[2,256,128]{2,1,0:T(8,128)(2,1)}, bf16[2,256,128]{2,1,0:T(8,128)(2,1)S(1)}, u32[]{:S(2)}) copy-start(bf16[2,256,128]{2,1,0:T(8,128)(2,1)S(1)} %collective-permute-done.4.refs_5_) | copy-start | bytes 393220
  73.1 9.6 %copy-start.22 = (bf16[2,256,128]{2,1,0:T(8,128)(2,1)}, bf16[2,256,128]{2,1,0:T(8,128)(2,1)S(1)}, u32[]{:S(2)}) copy-start(bf16[2,256,128]{2,1,0:T(8,128)(2,1)S(1)} %collective-permute-done.5.refs_6_) | copy-start | bytes 393220
  76.2 6.5 %copy-start.24 = (bf16[2,256,128]{2,1,0:T(8,128)(2,1)}, bf16[2,256,128]{2,1,0:T(8,128)(2,1)S(1)}, u32[]{:S(2)}) copy-start(bf16[2,256,128]{2,1,0:T(8,128)(2,1)S(1)} %collective-permute-done.6.refs_7_) | copy-start | bytes 393220
  76.2 5.2 %collective-permute-start.7 = (bf16[256,384]{1,0:T(8,128)(2,1)S(1)}, bf16[256,384]{1,0:T(8,128)(2,1)S(1)}, u32[]{:S(2)}, u32[]{:S(2)}) collective-permute-start(bf16[256,384]{1,0:T(8,128)(2,1)S(1)} %copy-done.10), channel_id=1, source_target_pairs={{0,1},{1,0},{2,3},{3,2},{4,5},{5,4},{6,7},{7,6},{8,9},{9,8},{10,11... | collective-permute-start | bytes 589832 | tf_op jit(solution)/shard_map/ppermute | solution.py:428
  76.3 6.3 %collective-permute-start.8 = (bf16[256,384]{1,0:T(8,128)(2,1)S(1)}, bf16[256,384]{1,0:T(8,128)(2,1)S(1)}, u32[]{:S(2)}, u32[]{:S(2)}) collective-permute-start(bf16[256,384]{1,0:T(8,128)(2,1)S(1)} %copy-done.9), channel_id=1, source_target_pairs={{0,2},{1,3},{2,0},{3,1},{4,6},{5,7},{6,4},{7,5},{8,10},{9,11},{10,... | collective-permute-start | bytes 589832 | tf_op jit(solution)/shard_map/ppermute | solution.py:428
  76.4 16.0 %collective-permute-start.9 = (bf16[256,384]{1,0:T(8,128)(2,1)S(1)}, bf16[256,384]{1,0:T(8,128)(2,1)}, u32[]{:S(2)}, u32[]{:S(2)}) collective-permute-start(bf16[256,384]{1,0:T(8,128)(2,1)S(1)} %copy-done.8), channel_id=1, source_target_pairs={{0,3},{1,2},{2,1},{3,0},{4,7},{5,6},{6,5},{7,4},{8,11},{9,10},{10,... | collective-permute-start | bytes 589832 | tf_op jit(solution)/shard_map/ppermute | solution.py:428
  78.4 14.0 %collective-permute-start.10 = (bf16[256,384]{1,0:T(8,128)(2,1)S(1)}, bf16[256,384]{1,0:T(8,128)(2,1)}, u32[]{:S(2)}, u32[]{:S(2)}) collective-permute-start(bf16[256,384]{1,0:T(8,128)(2,1)S(1)} %copy-done.7), channel_id=1, source_target_pairs={{0,4},{1,5},{2,6},{3,7},{4,0},{5,1},{6,2},{7,3},{8,12},{9,13},{10,... | collective-permute-start | bytes 589832 | tf_op jit(solution)/shard_map/ppermute | solution.py:428
  79.1 17.6 %collective-permute-start.11 = (bf16[256,384]{1,0:T(8,128)(2,1)S(1)}, bf16[256,384]{1,0:T(8,128)(2,1)}, u32[]{:S(2)}, u32[]{:S(2)}) collective-permute-start(bf16[256,384]{1,0:T(8,128)(2,1)S(1)} %copy-done.6), channel_id=1, source_target_pairs={{0,5},{1,4},{2,7},{3,6},{4,1},{5,0},{6,3},{7,2},{8,13},{9,12},{10,... | collective-permute-start | bytes 589832 | tf_op jit(solution)/shard_map/ppermute | solution.py:428
  81.4 1.3 copy-start.11
  81.4 15.9 %collective-permute-start.12 = (bf16[256,384]{1,0:T(8,128)(2,1)S(1)}, bf16[256,384]{1,0:T(8,128)(2,1)}, u32[]{:S(2)}, u32[]{:S(2)}) collective-permute-start(bf16[256,384]{1,0:T(8,128)(2,1)S(1)} %copy-done.5), channel_id=1, source_target_pairs={{0,6},{1,7},{2,4},{3,5},{4,2},{5,3},{6,0},{7,1},{8,14},{9,15},{10,... | collective-permute-start | bytes 589832 | tf_op jit(solution)/shard_map/ppermute | solution.py:428
  82.7 0.7 copy-start.12
  83.4 19.0 %collective-permute-start.13 = (bf16[256,384]{1,0:T(8,128)(2,1)S(1)}, bf16[256,384]{1,0:T(8,128)(2,1)}, u32[]{:S(2)}, u32[]{:S(2)}) collective-permute-start(bf16[256,384]{1,0:T(8,128)(2,1)S(1)} %copy-done.4), channel_id=1, source_target_pairs={{0,7},{1,6},{2,5},{3,4},{4,3},{5,2},{6,1},{7,0},{8,15},{9,14},{10,... | collective-permute-start | bytes 589832 | tf_op jit(solution)/shard_map/ppermute | solution.py:428
  102.9 30.9 %all-to-all-start.2 = ((bf16[16,192,256]{2,1,0:T(8,128)(2,1)}), bf16[16,192,256]{2,1,0:T(8,128)(2,1)}, u32[]{:S(2)}, u32[]{:S(2)}) async-start(bf16[16,192,256]{2,1,0:T(8,128)(2,1)} %pack_last.1), calls=%async_computation.2 | async-start | bytes 3145728 | tf_op jit(solution)/shard_map/all_to_all | solution.py:324
  122.0 16.3 %copy-start.1 = (s32[3,256,16]{1,2,0:T(8,128)S(1)}, s32[3,256,16]{1,2,0:T(8,128)}, u32[]{:S(2)}) copy-start(s32[3,256,16]{1,2,0:T(8,128)} %param.11) | copy-start | bytes 147460
  133.9 38.0 %all-to-all-start.3 = ((bf16[16,3,192,128]{3,2,1,0:T(8,128)(2,1)}), bf16[16,3,192,128]{3,2,1,0:T(8,128)(2,1)}, u32[]{:S(2)}, u32[]{:S(2)}) async-start(bf16[16,3,192,128]{3,2,1,0:T(8,128)(2,1)} %pack_q.1), calls=%async_computation.3 | async-start | bytes 4718592 | tf_op jit(solution)/shard_map/all_to_all | solution.py:324
  271.6 59.3 %all-to-all-start.5 = ((bf16[16,1,4,128,256]{4,3,2,1,0:T(8,128)(2,1)}), bf16[16,1,4,128,256]{4,3,2,1,0:T(8,128)(2,1)}, u32[]{:S(2)}, u32[]{:S(2)}) async-start(bf16[16,1,4,128,256]{4,3,2,1,0:T(8,128)(2,1)} %get-tuple-element.172), calls=%async_computation.5 | async-start | bytes 8388608 | tf_op jit(solution)/shard_map/all_to_all | solution.py:324
  330.9 26.0 %all-to-all-start.7 = ((bf16[16,2,192,128]{3,2,1,0:T(8,128)(2,1)}), bf16[16,2,192,128]{3,2,1,0:T(8,128)(2,1)}, u32[]{:S(2)}, u32[]{:S(2)}) async-start(bf16[16,2,192,128]{3,2,1,0:T(8,128)(2,1)} %attend_0.1), calls=%async_computation.7 | async-start | bytes 3145728 | tf_op jit(solution)/shard_map/all_to_all | solution.py:324
  356.9 18.0 %all-to-all-start.6 = ((bf16[16,1,192,128]{3,2,1,0:T(8,128)(2,1)}), bf16[16,1,192,128]{3,2,1,0:T(8,128)(2,1)S(1)}, u32[]{:S(2)}, u32[]{:S(2)}) async-start(bf16[16,1,192,128]{3,2,1,0:T(8,128)(2,1)} %attend_2.1), calls=%async_computation.6 | async-start | bytes 1572864 | tf_op jit(solution)/shard_map/all_to_all | solution.py:324
  375.0 0.9 copy-start

commit v7 on v5

--- a/solution.py
+++ b/solution.py
@@ -362,9 +362,9 @@
 
     kv_sent = pl.pallas_call(
         split_kernel,
-        grid=(4,),
-        in_specs=[pl.BlockSpec((part // 4, parts * width), lambda i: (i, 0))] * 2,
-        out_specs=pl.BlockSpec((parts, 2, part // 4, most * LANES), lambda i: (0, 0, i, 0)),
+        grid=(8,),
+        in_specs=[pl.BlockSpec((part // 8, parts * width), lambda i: (i, 0))] * 2,
+        out_specs=pl.BlockSpec((parts, 2, part // 8, most * LANES), lambda i: (0, 0, i, 0)),
         out_shape=shape_of((parts, 2, part, most * LANES), BF16),
         compiler_params=params(),
         cost_estimate=cost(0, 6e6),

time: 413 us -> 415 us (level)
  no operation moved by 1% of the time
where the time goes in v7:
time: 415 us; the launch traced here: 414 us
  Pallas kernels  140 us (34%)
  blocking collectives  128 us (31%)
  waiting for transfers between devices  76.8 us (19%)
  starting transfers between devices  58.7 us (14%)
  local copies, waits for them, and re-layouts  8.84 us (2%)
    all_to_all x2, blocking collectives, exchange(): return lax.all_to_all(array, axis, split_axis=0, concat_axis=0, tiled=True)  128 us
    all_to_all x7, waiting for transfers between devices, exchange(): return lax.all_to_all(array, axis, split_axis=0, concat_axis=0, tiled=True)  55.4 us
    pallas_call x2, Pallas kernels, per_device(): pl.pallas_call(functools.partial(attend_kernel, first=first), grid_spec=p...  46.5 us
    all_to_all x7, starting transfers between devices, exchange(): return lax.all_to_all(array, axis, split_axis=0, concat_axis=0, tiled=True)  40.3 us
    ppermute x14, waiting for transfers between devices, to_partner(): return lax.ppermute(array, 'head', [(i, i ^ k) for i in range(parts)])  21.4 us
    pallas_call x1, Pallas kernels, per_device(): pl.pallas_call(unpack_kv_kernel, grid_spec=pltpu.PrefetchScalarGridSpec(n...  21.4 us
    ppermute x14, starting transfers between devices, to_partner(): return lax.ppermute(array, 'head', [(i, i ^ k) for i in range(parts)])  18.4 us
    pallas_call x1, Pallas kernels, per_device(): pl.pallas_call(pack_q_kernel, grid_spec=pltpu.PrefetchScalarGridSpec(num_...  13.1 us
  transfers between devices with their start and end apart: 21, of which 16 were waited for; matrix products, arithmetic and copies ran while one was open for 1% of the time, Pallas kernels for 29%

profile of v7, /device:TPU:1, one launch (start us, length us, event | category | flops | bytes accessed | tf_op | source)
XLA Modules:
  0.0 413.8 jit_solution(522349209899647491)
XLA Ops:
  0.0 6.0 %split_kv.1 = bf16[8,2,256,256]{3,2,1,0:T(8,128)(2,1)} custom-call(bf16[256,3072]{1,0:T(8,128)(2,1)} %key_ref.3, bf16[256,3072]{1,0:T(8,128)(2,1)} %value_ref.3), custom_call_target="tpu_custom_call" | custom-call | bytes 6000000 | tf_op jit(solution)/shard_map/split_kv/pallas_call | solution.py:363
  6.0 5.9 %all-to-all-start = ((bf16[8,2,256,256]{3,2,1,0:T(8,128)(2,1)}), bf16[8,2,256,256]{3,2,1,0:T(8,128)(2,1)S(1)}, u32[]{:S(2)}, u32[]{:S(2)}) async-start(bf16[8,2,256,256]{3,2,1,0:T(8,128)(2,1)} %split_kv.1), calls=%async_computation | async-start | bytes 4194304 | tf_op jit(solution)/shard_map/all_to_all | solution.py:324
  12.0 0.6 copy.19
  12.6 3.6 split_rest.1
  16.3 11.5 %slots.1 = (s32[6,16,128]{2,1,0:T(8,128)}, f32[6,16,128]{2,1,0:T(8,128)}) custom-call(s32[6,16,128]{2,1,0:T(8,128)} %bitcast.19), custom_call_target="tpu_custom_call" | custom-call | flops 6000000000 | bytes 1000000 | tf_op jit(solution)/shard_map/slots/pallas_call | solution.py:391
  27.7 10.6 %all-to-all-done.key_ref.value_ref = bf16[8,2,256,256]{3,2,1,0:T(8,128)(2,1)S(1)} async-done(((bf16[8,2,256,256]{3,2,1,0:T(8,128)(2,1)}), bf16[8,2,256,256]{3,2,1,0:T(8,128)(2,1)S(1)}, u32[]{:S(2)}, u32[]{:S(2)}) %all-to-all-start) | async-done | bytes 2097184 | tf_op jit(solution)/shard_map/all_to_all | solution.py:324
  38.3 1.4 copy-done.2
  39.6 10.4 %pack_kv.1 = bf16[16,400,256]{2,1,0:T(8,128)(2,1)} custom-call(s32[6,16,128]{2,1,0:T(8,128)} %get-tuple-element.89.slot_ref.index_ref, f32[6,16,128]{2,1,0:T(8,128)} %get-tuple-element.122.count_ref, bf16[8,2,256,256]{3,2,1,0:T(8,128)(2,1)} %copy-done.2, bf16[8,2,256,256]{3,2,1,0:T(8,128)(2,1)} %copy-done.2), custom_call_target="tpu_custom_call" | custom-call | flops 6442450944 | bytes 8000000 | tf_op jit(solution)/shard_map/pack_kv/pallas_call | solution.py:410
  50.0 7.9 %all-to-all-start.1 = ((bf16[16,400,256]{2,1,0:T(8,128)(2,1)}), bf16[16,400,256]{2,1,0:T(8,128)(2,1)S(1)}, u32[]{:S(2)}, u32[]{:S(2)}) async-start(bf16[16,400,256]{2,1,0:T(8,128)(2,1)} %pack_kv.1), calls=%async_computation.1 | async-start | bytes 6553600 | tf_op jit(solution)/shard_map/all_to_all | solution.py:324
  57.9 1.2 collective-permute-start
  59.1 0.3 collective-permute-start.1
  59.4 1.4 collective-permute-start.2
  60.9 0.4 collective-permute-start.3
  61.3 2.9 collective-permute-start.4
  64.2 0.9 collective-permute-start.5
  65.1 2.0 collective-permute-start.6
  67.1 1.1 collective-permute-done.2.refs_3_
  68.2 2.5 collective-permute-done.3.refs_4_
  70.7 3.3 collective-permute-done.4.refs_5_
  74.0 2.2 collective-permute-done.5.refs_6_
  76.2 3.1 collective-permute-done.6.refs_7_
  79.4 2.0 collective-permute-start.9
  81.4 0.6 collective-permute-start.10
  82.0 2.4 collective-permute-start.11
  84.4 1.0 collective-permute-start.12
  85.4 0.3 collective-permute-done.8.refs_2_
  85.7 0.7 copy-done.10
  86.4 3.1 collective-permute-start.13
  89.5 6.1 %pack_last.1 = bf16[16,192,256]{2,1,0:T(8,128)(2,1)} custom-call(s32[1]{0:T(128)} %bitcast.1.me_ref, s32[6,16,128]{2,1,0:T(8,128)} %get-tuple-element.89.slot_ref.index_ref, bf16[2,256,128]{2,1,0:T(8,128)(2,1)} %get-tuple-element.140.refs_0_, bf16[2,256,128]{2,1,0:T(8,128)(2,1)} %copy-done.15, bf16[2,256,128]{2,1,0:T(8,128)(2,1)} %copy-done.16, ...), custom_call_target="tpu_custom_call" | custom-call | flops 3221225472 | bytes 3000000 | tf_op jit(solution)/shard_map/pack_last/pallas_call | solution.py:436
  95.7 4.0 collective-permute-done.11.refs_5_
  99.7 0.6 collective-permute-done.12.refs_6_
  100.4 0.7 copy-done.14
  101.1 4.3 %collective-permute-done.13.refs_7_ = bf16[256,384]{1,0:T(8,128)(2,1)} collective-permute-done((bf16[256,384]{1,0:T(8,128)(2,1)S(1)}, bf16[256,384]{1,0:T(8,128)(2,1)}, u32[]{:S(2)}, u32[]{:S(2)}) %collective-permute-start.13) | collective-permute-done | bytes 196640 | tf_op jit(solution)/shard_map/ppermute | solution.py:428
  105.4 0.5 all-to-all-done.1.in_ref.meta_ref
  106.0 6.2 %all-to-all-start.2 = ((bf16[16,192,256]{2,1,0:T(8,128)(2,1)}), bf16[16,192,256]{2,1,0:T(8,128)(2,1)}, u32[]{:S(2)}, u32[]{:S(2)}) async-start(bf16[16,192,256]{2,1,0:T(8,128)(2,1)} %pack_last.1), calls=%async_computation.2 | async-start | bytes 3145728 | tf_op jit(solution)/shard_map/all_to_all | solution.py:324
  112.1 13.1 %pack_q.1 = bf16[16,3,192,128]{3,2,1,0:T(8,128)(2,1)} custom-call(s32[1]{0:T(128)} %bitcast.1.me_ref, s32[6,16,128]{2,1,0:T(8,128)} %get-tuple-element.89.slot_ref.index_ref, bf16[256,384]{1,0:T(8,128)(2,1)} %get-tuple-element.156.refs_0_, bf16[256,384]{1,0:T(8,128)(2,1)} %copy-done.9, bf16[256,384]{1,0:T(8,128)(2,1)} %copy-done.10, ...), custom_call_target="tpu_custom_call" | custom-call | flops 9663676416 | bytes 4000000 | tf_op jit(solution)/shard_map/pack_q/pallas_call | solution.py:453
  125.3 12.6 %all-to-all-done.2.last_in_ref = bf16[16,192,256]{2,1,0:T(8,128)(2,1)} async-done(((bf16[16,192,256]{2,1,0:T(8,128)(2,1)}), bf16[16,192,256]{2,1,0:T(8,128)(2,1)}, u32[]{:S(2)}, u32[]{:S(2)}) %all-to-all-start.2) | async-done | bytes 1572896 | tf_op jit(solution)/shard_map/all_to_all | solution.py:324
  137.9 3.7 all-to-all-start.3
  141.6 0.2 copy.11
  141.8 0.2 reshape.35
  142.0 1.0 compare_reduce_fusion
  143.1 0.3 select_reduce_fusion.1
  143.4 0.7 copy.12.pick_ref
  144.1 21.4 %unpack_kv.1 = (bf16[16,2,4,128,256]{4,3,2,1,0:T(8,128)(2,1)}, bf16[16,1,4,128,256]{4,3,2,1,0:T(8,128)(2,1)}, s32[3,16,128]{2,1,0:T(8,128)}) custom-call(s32[3,16,4]{2,1,0:T(8,128)} %copy.12.pick_ref, bf16[16,400,256]{2,1,0:T(8,128)(2,1)} %copy-done, bf16[16,192,256]{2,1,0:T(8,128)(2,1)} %all-to-all-done.2.last_in_ref, bf16[16,400,256]{2,1,0:T(8,128)(2,1)} %copy-done), custom_call_target="tpu_custom_call" | custom-call | flops 9663676416 | bytes 18000000 | tf_op jit(solution)/shard_map/unpack_kv/pallas_call | solution.py:472
  165.5 10.0 %all-to-all-done.3.in_ref = bf16[16,3,192,128]{3,2,1,0:T(8,128)(2,1)S(1)} async-done(((bf16[16,3,192,128]{3,2,1,0:T(8,128)(2,1)}), bf16[16,3,192,128]{3,2,1,0:T(8,128)(2,1)S(1)}, u32[]{:S(2)}, u32[]{:S(2)}) %all-to-all-start.3) | async-done | bytes 2359328 | tf_op jit(solution)/shard_map/all_to_all | solution.py:324
  175.5 100.3 %all_to_all.45.recv_ref = bf16[16,2,4,128,256]{4,3,2,1,0:T(8,128)(2,1)} all-to-all(bf16[16,2,4,128,256]{4,3,2,1,0:T(8,128)(2,1)} %get-tuple-element.169), channel_id=1, replica_groups=mesh['seq'=16,'head'=8] {'seq'}, dimensions={0} | all-to-all | bytes 16777216 | tf_op jit(solution)/shard_map/all_to_all | solution.py:324
  275.7 4.5 %all-to-all-start.5 = ((bf16[16,1,4,128,256]{4,3,2,1,0:T(8,128)(2,1)}), bf16[16,1,4,128,256]{4,3,2,1,0:T(8,128)(2,1)}, u32[]{:S(2)}, u32[]{:S(2)}) async-start(bf16[16,1,4,128,256]{4,3,2,1,0:T(8,128)(2,1)} %get-tuple-element.172), calls=%async_computation.5 | async-start | bytes 8388608 | tf_op jit(solution)/shard_map/all_to_all | solution.py:324
  280.3 0.2 fusion.1
  280.8 0.3 select_reduce_fusion
  281.1 0.7 reshape.37.fetch_ref
  281.8 9.5 %unpack_q.1.query_ref = bf16[3,2048,128]{2,1,0:T(8,128)(2,1)} custom-call(s32[3,16,128]{2,1,0:T(8,128)} %get-tuple-element.170.index_ref, bf16[16,3,192,128]{3,2,1,0:T(8,128)(2,1)} %copy-done.1), custom_call_target="tpu_custom_call" | custom-call | flops 9663676416 | bytes 4000000 | tf_op jit(solution)/shard_map/unpack_q/pallas_call | solution.py:510
  291.3 29.2 %attend_0.1 = bf16[16,2,192,128]{3,2,1,0:T(8,128)(2,1)} custom-call(s32[3,16,16]{2,1,0:T(8,128)} %reshape.37.fetch_ref, s32[3,16,128]{2,1,0:T(8,128)} %get-tuple-element.170.index_ref, bf16[3,2048,128]{2,1,0:T(8,128)(2,1)} %unpack_q.1.query_ref, bf16[16,2,4,128,256]{4,3,2,1,0:T(8,128)(2,1)} %all_to_all.45.recv_ref), custom_call_target="tpu_custom_call" | custom-call | flops 4294967296 | bytes 12000000 | tf_op jit(solution)/shard_map/attend_0/pallas_call | solution.py:527
  320.5 13.4 %all-to-all-done.5.recv_ref = bf16[16,1,4,128,256]{4,3,2,1,0:T(8,128)(2,1)} async-done(((bf16[16,1,4,128,256]{4,3,2,1,0:T(8,128)(2,1)}), bf16[16,1,4,128,256]{4,3,2,1,0:T(8,128)(2,1)}, u32[]{:S(2)}, u32[]{:S(2)}) %all-to-all-start.5) | async-done | bytes 4194336 | tf_op jit(solution)/shard_map/all_to_all | solution.py:324
  333.9 6.7 %all-to-all-start.7 = ((bf16[16,2,192,128]{3,2,1,0:T(8,128)(2,1)}), bf16[16,2,192,128]{3,2,1,0:T(8,128)(2,1)S(1)}, u32[]{:S(2)}, u32[]{:S(2)}) async-start(bf16[16,2,192,128]{3,2,1,0:T(8,128)(2,1)} %attend_0.1), calls=%async_computation.7 | async-start | bytes 3145728 | tf_op jit(solution)/shard_map/all_to_all | solution.py:324
  340.6 17.3 %attend_2.1 = bf16[16,1,192,128]{3,2,1,0:T(8,128)(2,1)} custom-call(s32[3,16,16]{2,1,0:T(8,128)} %reshape.37.fetch_ref, s32[3,16,128]{2,1,0:T(8,128)} %get-tuple-element.170.index_ref, bf16[3,2048,128]{2,1,0:T(8,128)(2,1)} %unpack_q.1.query_ref, bf16[16,1,4,128,256]{4,3,2,1,0:T(8,128)(2,1)} %all-to-all-done.5.recv_ref), custom_call_target="tpu_custom_call" | custom-call | flops 2147483648 | bytes 6000000 | tf_op jit(solution)/shard_map/attend_2/pallas_call | solution.py:527
  357.9 3.1 all-to-all-done.7.in_ref
  361.0 5.4 %all-to-all-start.6 = ((bf16[16,1,192,128]{3,2,1,0:T(8,128)(2,1)}), bf16[16,1,192,128]{3,2,1,0:T(8,128)(2,1)S(1)}, u32[]{:S(2)}, u32[]{:S(2)}) async-start(bf16[16,1,192,128]{3,2,1,0:T(8,128)(2,1)} %attend_2.1), calls=%async_computation.6 | async-start | bytes 1572864 | tf_op jit(solution)/shard_map/all_to_all | solution.py:324
  366.4 7.0 %final_0.1.refs_0_ = bf16[8,256,384]{2,1,0:T(8,128)(2,1)} custom-call(s32[6,16,128]{2,1,0:T(8,128)} %get-tuple-element.89.slot_ref.index_ref, bf16[16,2,192,128]{3,2,1,0:T(8,128)(2,1)} %copy-done.3), custom_call_target="tpu_custom_call" | custom-call | flops 6442450944 | bytes 2000000 | tf_op jit(solution)/shard_map/final_0/pallas_call | solution.py:555
  373.4 5.3 %all-to-all-done.6.in_ref = bf16[16,1,192,128]{3,2,1,0:T(8,128)(2,1)S(1)} async-done(((bf16[16,1,192,128]{3,2,1,0:T(8,128)(2,1)}), bf16[16,1,192,128]{3,2,1,0:T(8,128)(2,1)S(1)}, u32[]{:S(2)}, u32[]{:S(2)}) %all-to-all-start.6) | async-done | bytes 786464 | tf_op jit(solution)/shard_map/all_to_all | solution.py:324
  378.6 0.9 copy-done.4
  379.5 4.5 %final_2.1 = bf16[8,256,384]{2,1,0:T(8,128)(2,1)} custom-call(s32[6,16,128]{2,1,0:T(8,128)} %get-tuple-element.89.slot_ref.index_ref, bf16[16,1,192,128]{3,2,1,0:T(8,128)(2,1)} %copy-done.4, bf16[8,256,384]{2,1,0:T(8,128)(2,1)} %final_0.1.refs_0_), custom_call_target="tpu_custom_call", output_to_operand_aliasing={{}: (2, {})} | custom-call | flops 3221225472 | bytes 2000000 | tf_op jit(solution)/shard_map/final_2/pallas_call | solution.py:555
  384.0 27.3 %all_to_all.46 = bf16[8,256,384]{2,1,0:T(8,128)(2,1)S(1)} all-to-all(bf16[8,256,384]{2,1,0:T(8,128)(2,1)} %final_2.1), channel_id=1, replica_groups=mesh['seq'=16,'head'=8] {'head'}, dimensions={0} | all-to-all | bytes 3145728 | tf_op jit(solution)/shard_map/all_to_all | solution.py:324
  411.3 0.7 copy.13
  412.1 1.7 copy.14
  (56 shorter events, 0.7 us)
Async XLA Ops:
  6.0 5.9 %copy-start.6 = (s32[3,2048]{1,0:T(4,128)S(1)}, s32[3,2048]{1,0:T(4,128)}, u32[]{:S(2)}) copy-start(s32[3,2048]{1,0:T(4,128)} %param.10) | copy-start | bytes 73732
  6.0 5.9 %copy-start.7 = (s32[3,2048]{1,0:T(4,128)S(1)}, s32[3,2048]{1,0:T(4,128)}, u32[]{:S(2)}) copy-start(s32[3,2048]{1,0:T(4,128)} %param.9) | copy-start | bytes 73732
  6.0 32.3 %all-to-all-start = ((bf16[8,2,256,256]{3,2,1,0:T(8,128)(2,1)}), bf16[8,2,256,256]{3,2,1,0:T(8,128)(2,1)S(1)}, u32[]{:S(2)}, u32[]{:S(2)}) async-start(bf16[8,2,256,256]{3,2,1,0:T(8,128)(2,1)} %split_kv.1), calls=%async_computation | async-start | bytes 4194304 | tf_op jit(solution)/shard_map/all_to_all | solution.py:324
  38.3 1.4 copy-start.2
  50.0 36.4 %copy-start.8 = (bf16[256,384]{1,0:T(8,128)(2,1)S(1)}, bf16[256,384]{1,0:T(8,128)(2,1)}, u32[]{:S(2)}) copy-start(bf16[256,384]{1,0:T(8,128)(2,1)} %get-tuple-element.155) | copy-start | bytes 589828
  50.0 55.9 %all-to-all-start.1 = ((bf16[16,400,256]{2,1,0:T(8,128)(2,1)}), bf16[16,400,256]{2,1,0:T(8,128)(2,1)S(1)}, u32[]{:S(2)}, u32[]{:S(2)}) async-start(bf16[16,400,256]{2,1,0:T(8,128)(2,1)} %pack_kv.1), calls=%async_computation.1 | async-start | bytes 6553600 | tf_op jit(solution)/shard_map/all_to_all | solution.py:324
  57.9 6.3 %collective-permute-start = (bf16[2,256,128]{2,1,0:T(8,128)(2,1)}, bf16[2,256,128]{2,1,0:T(8,128)(2,1)S(1)}, u32[]{:S(2)}, u32[]{:S(2)}) collective-permute-start(bf16[2,256,128]{2,1,0:T(8,128)(2,1)} %get-tuple-element.125), channel_id=1, source_target_pairs={{0,1},{1,0},{2,3},{3,2},{4,5},{5,4},{6,7},{7,6},{8,9},{9,8},{10,11... | collective-permute-start | bytes 393224 | tf_op jit(solution)/shard_map/ppermute | solution.py:428
  59.1 5.9 %collective-permute-start.1 = (bf16[2,256,128]{2,1,0:T(8,128)(2,1)}, bf16[2,256,128]{2,1,0:T(8,128)(2,1)S(1)}, u32[]{:S(2)}, u32[]{:S(2)}) collective-permute-start(bf16[2,256,128]{2,1,0:T(8,128)(2,1)} %get-tuple-element.126), channel_id=1, source_target_pairs={{0,2},{1,3},{2,0},{3,1},{4,6},{5,7},{6,4},{7,5},{8,10},{9,11},{10,... | collective-permute-start | bytes 393224 | tf_op jit(solution)/shard_map/ppermute | solution.py:428
  59.4 8.7 %collective-permute-start.2 = (bf16[2,256,128]{2,1,0:T(8,128)(2,1)}, bf16[2,256,128]{2,1,0:T(8,128)(2,1)S(1)}, u32[]{:S(2)}, u32[]{:S(2)}) collective-permute-start(bf16[2,256,128]{2,1,0:T(8,128)(2,1)} %get-tuple-element.127), channel_id=1, source_target_pairs={{0,3},{1,2},{2,1},{3,0},{4,7},{5,6},{6,5},{7,4},{8,11},{9,10},{10,... | collective-permute-start | bytes 393224 | tf_op jit(solution)/shard_map/ppermute | solution.py:428
  60.9 9.8 %collective-permute-start.3 = (bf16[2,256,128]{2,1,0:T(8,128)(2,1)}, bf16[2,256,128]{2,1,0:T(8,128)(2,1)S(1)}, u32[]{:S(2)}, u32[]{:S(2)}) collective-permute-start(bf16[2,256,128]{2,1,0:T(8,128)(2,1)} %get-tuple-element.128), channel_id=1, source_target_pairs={{0,4},{1,5},{2,6},{3,7},{4,0},{5,1},{6,2},{7,3},{8,12},{9,13},{10,... | collective-permute-start | bytes 393224 | tf_op jit(solution)/shard_map/ppermute | solution.py:428
  61.3 12.7 %collective-permute-start.4 = (bf16[2,256,128]{2,1,0:T(8,128)(2,1)}, bf16[2,256,128]{2,1,0:T(8,128)(2,1)S(1)}, u32[]{:S(2)}, u32[]{:S(2)}) collective-permute-start(bf16[2,256,128]{2,1,0:T(8,128)(2,1)} %get-tuple-element.129), channel_id=1, source_target_pairs={{0,5},{1,4},{2,7},{3,6},{4,1},{5,0},{6,3},{7,2},{8,13},{9,12},{10,... | collective-permute-start | bytes 393224 | tf_op jit(solution)/shard_map/ppermute | solution.py:428
  64.2 25.3 %copy-start.15 = (bf16[2,256,128]{2,1,0:T(8,128)(2,1)}, bf16[2,256,128]{2,1,0:T(8,128)(2,1)S(1)}, u32[]{:S(2)}) copy-start(bf16[2,256,128]{2,1,0:T(8,128)(2,1)S(1)} %collective-permute-done.refs_1_) | copy-start | bytes 393220
  64.2 12.0 %collective-permute-start.5 = (bf16[2,256,128]{2,1,0:T(8,128)(2,1)}, bf16[2,256,128]{2,1,0:T(8,128)(2,1)S(1)}, u32[]{:S(2)}, u32[]{:S(2)}) collective-permute-start(bf16[2,256,128]{2,1,0:T(8,128)(2,1)} %get-tuple-element.130), channel_id=1, source_target_pairs={{0,6},{1,7},{2,4},{3,5},{4,2},{5,3},{6,0},{7,1},{8,14},{9,15},{10,... | collective-permute-start | bytes 393224 | tf_op jit(solution)/shard_map/ppermute | solution.py:428
  65.1 24.4 %copy-start.16 = (bf16[2,256,128]{2,1,0:T(8,128)(2,1)}, bf16[2,256,128]{2,1,0:T(8,128)(2,1)S(1)}, u32[]{:S(2)}) copy-start(bf16[2,256,128]{2,1,0:T(8,128)(2,1)S(1)} %collective-permute-done.1.refs_2_) | copy-start | bytes 393220
  65.1 14.2 %collective-permute-start.6 = (bf16[2,256,128]{2,1,0:T(8,128)(2,1)}, bf16[2,256,128]{2,1,0:T(8,128)(2,1)S(1)}, u32[]{:S(2)}, u32[]{:S(2)}) collective-permute-start(bf16[2,256,128]{2,1,0:T(8,128)(2,1)} %get-tuple-element.131), channel_id=1, source_target_pairs={{0,7},{1,6},{2,5},{3,4},{4,3},{5,2},{6,1},{7,0},{8,15},{9,14},{10,... | collective-permute-start | bytes 393224 | tf_op jit(solution)/shard_map/ppermute | solution.py:428
  68.2 21.3 %copy-start.17 = (bf16[2,256,128]{2,1,0:T(8,128)(2,1)}, bf16[2,256,128]{2,1,0:T(8,128)(2,1)S(1)}, u32[]{:S(2)}) copy-start(bf16[2,256,128]{2,1,0:T(8,128)(2,1)S(1)} %collective-permute-done.2.refs_3_) | copy-start | bytes 393220
  70.7 18.8 %copy-start.18 = (bf16[2,256,128]{2,1,0:T(8,128)(2,1)}, bf16[2,256,128]{2,1,0:T(8,128)(2,1)S(1)}, u32[]{:S(2)}) copy-start(bf16[2,256,128]{2,1,0:T(8,128)(2,1)S(1)} %collective-permute-done.3.refs_4_) | copy-start | bytes 393220
  74.0 15.5 %copy-start.19 = (bf16[2,256,128]{2,1,0:T(8,128)(2,1)}, bf16[2,256,128]{2,1,0:T(8,128)(2,1)S(1)}, u32[]{:S(2)}) copy-start(bf16[2,256,128]{2,1,0:T(8,128)(2,1)S(1)} %collective-permute-done.4.refs_5_) | copy-start | bytes 393220
  76.2 13.3 %copy-start.20 = (bf16[2,256,128]{2,1,0:T(8,128)(2,1)}, bf16[2,256,128]{2,1,0:T(8,128)(2,1)S(1)}, u32[]{:S(2)}) copy-start(bf16[2,256,128]{2,1,0:T(8,128)(2,1)S(1)} %collective-permute-done.5.refs_6_) | copy-start | bytes 393220
  79.3 10.2 %copy-start.21 = (bf16[2,256,128]{2,1,0:T(8,128)(2,1)}, bf16[2,256,128]{2,1,0:T(8,128)(2,1)S(1)}, u32[]{:S(2)}) copy-start(bf16[2,256,128]{2,1,0:T(8,128)(2,1)S(1)} %collective-permute-done.6.refs_7_) | copy-start | bytes 393220
  79.3 5.1 %collective-permute-start.7 = (bf16[256,384]{1,0:T(8,128)(2,1)}, bf16[256,384]{1,0:T(8,128)(2,1)S(1)}, u32[]{:S(2)}, u32[]{:S(2)}) collective-permute-start(bf16[256,384]{1,0:T(8,128)(2,1)} %get-tuple-element.149), channel_id=1, source_target_pairs={{0,1},{1,0},{2,3},{3,2},{4,5},{5,4},{6,7},{7,6},{8,9},{9,8},{10,11... | collective-permute-start | bytes 589832 | tf_op jit(solution)/shard_map/ppermute | solution.py:428
  79.4 6.3 %collective-permute-start.8 = (bf16[256,384]{1,0:T(8,128)(2,1)}, bf16[256,384]{1,0:T(8,128)(2,1)S(1)}, u32[]{:S(2)}, u32[]{:S(2)}) collective-permute-start(bf16[256,384]{1,0:T(8,128)(2,1)} %get-tuple-element.150), channel_id=1, source_target_pairs={{0,2},{1,3},{2,0},{3,1},{4,6},{5,7},{6,4},{7,5},{8,10},{9,11},{10,... | collective-permute-start | bytes 589832 | tf_op jit(solution)/shard_map/ppermute | solution.py:428
  79.4 16.3 %collective-permute-start.9 = (bf16[256,384]{1,0:T(8,128)(2,1)}, bf16[256,384]{1,0:T(8,128)(2,1)S(1)}, u32[]{:S(2)}, u32[]{:S(2)}) collective-permute-start(bf16[256,384]{1,0:T(8,128)(2,1)} %get-tuple-element.151), channel_id=1, source_target_pairs={{0,3},{1,2},{2,1},{3,0},{4,7},{5,6},{6,5},{7,4},{8,11},{9,10},{10,... | collective-permute-start | bytes 589832 | tf_op jit(solution)/shard_map/ppermute | solution.py:428
  81.4 14.2 %collective-permute-start.10 = (bf16[256,384]{1,0:T(8,128)(2,1)}, bf16[256,384]{1,0:T(8,128)(2,1)S(1)}, u32[]{:S(2)}, u32[]{:S(2)}) collective-permute-start(bf16[256,384]{1,0:T(8,128)(2,1)} %get-tuple-element.152), channel_id=1, source_target_pairs={{0,4},{1,5},{2,6},{3,7},{4,0},{5,1},{6,2},{7,3},{8,12},{9,13},{10,... | collective-permute-start | bytes 589832 | tf_op jit(solution)/shard_map/ppermute | solution.py:428
  82.0 17.7 %collective-permute-start.11 = (bf16[256,384]{1,0:T(8,128)(2,1)}, bf16[256,384]{1,0:T(8,128)(2,1)S(1)}, u32[]{:S(2)}, u32[]{:S(2)}) collective-permute-start(bf16[256,384]{1,0:T(8,128)(2,1)} %get-tuple-element.153), channel_id=1, source_target_pairs={{0,5},{1,4},{2,7},{3,6},{4,1},{5,0},{6,3},{7,2},{8,13},{9,12},{10,... | collective-permute-start | bytes 589832 | tf_op jit(solution)/shard_map/ppermute | solution.py:428
  84.4 1.0 copy-start.9
  84.4 15.9 %collective-permute-start.12 = (bf16[256,384]{1,0:T(8,128)(2,1)}, bf16[256,384]{1,0:T(8,128)(2,1)S(1)}, u32[]{:S(2)}, u32[]{:S(2)}) collective-permute-start(bf16[256,384]{1,0:T(8,128)(2,1)} %get-tuple-element.154), channel_id=1, source_target_pairs={{0,6},{1,7},{2,4},{3,5},{4,2},{5,3},{6,0},{7,1},{8,14},{9,15},{10,... | collective-permute-start | bytes 589832 | tf_op jit(solution)/shard_map/ppermute | solution.py:428
  85.7 0.7 copy-start.10
  86.4 19.0 %collective-permute-start.13 = (bf16[256,384]{1,0:T(8,128)(2,1)S(1)}, bf16[256,384]{1,0:T(8,128)(2,1)}, u32[]{:S(2)}, u32[]{:S(2)}) collective-permute-start(bf16[256,384]{1,0:T(8,128)(2,1)S(1)} %copy-done.8), channel_id=1, source_target_pairs={{0,7},{1,6},{2,5},{3,4},{4,3},{5,2},{6,1},{7,0},{8,15},{9,14},{10,... | collective-permute-start | bytes 589832 | tf_op jit(solution)/shard_map/ppermute | solution.py:428
  95.7 4.6 %copy-start.11 = (bf16[256,384]{1,0:T(8,128)(2,1)}, bf16[256,384]{1,0:T(8,128)(2,1)S(1)}, u32[]{:S(2)}) copy-start(bf16[256,384]{1,0:T(8,128)(2,1)S(1)} %collective-permute-done.9.refs_3_) | copy-start | bytes 589828
  95.7 4.6 %copy-start.12 = (bf16[256,384]{1,0:T(8,128)(2,1)}, bf16[256,384]{1,0:T(8,128)(2,1)S(1)}, u32[]{:S(2)}) copy-start(bf16[256,384]{1,0:T(8,128)(2,1)S(1)} %collective-permute-done.10.refs_4_) | copy-start | bytes 589828
  99.7 0.7 copy-start.13
  100.4 0.7 copy-start.14
  105.9 19.3 %copy-start = (bf16[16,400,256]{2,1,0:T(8,128)(2,1)}, bf16[16,400,256]{2,1,0:T(8,128)(2,1)S(1)}, u32[]{:S(2)}) copy-start(bf16[16,400,256]{2,1,0:T(8,128)(2,1)S(1)} %all-to-all-done.1.in_ref.meta_ref) | copy-start | bytes 9830404
  106.0 31.9 %all-to-all-start.2 = ((bf16[16,192,256]{2,1,0:T(8,128)(2,1)}), bf16[16,192,256]{2,1,0:T(8,128)(2,1)}, u32[]{:S(2)}, u32[]{:S(2)}) async-start(bf16[16,192,256]{2,1,0:T(8,128)(2,1)} %pack_last.1), calls=%async_computation.2 | async-start | bytes 3145728 | tf_op jit(solution)/shard_map/all_to_all | solution.py:324
  125.3 16.3 %copy-start.5 = (s32[3,256,16]{1,2,0:T(8,128)S(1)}, s32[3,256,16]{1,2,0:T(8,128)}, u32[]{:S(2)}) copy-start(s32[3,256,16]{1,2,0:T(8,128)} %param.11) | copy-start | bytes 147460
  137.9 37.6 %all-to-all-start.3 = ((bf16[16,3,192,128]{3,2,1,0:T(8,128)(2,1)}), bf16[16,3,192,128]{3,2,1,0:T(8,128)(2,1)S(1)}, u32[]{:S(2)}, u32[]{:S(2)}) async-start(bf16[16,3,192,128]{3,2,1,0:T(8,128)(2,1)} %pack_q.1), calls=%async_computation.3 | async-start | bytes 4718592 | tf_op jit(solution)/shard_map/all_to_all | solution.py:324
  175.5 100.3 %copy-start.1 = (bf16[16,3,192,128]{3,2,1,0:T(8,128)(2,1)}, bf16[16,3,192,128]{3,2,1,0:T(8,128)(2,1)S(1)}, u32[]{:S(2)}) copy-start(bf16[16,3,192,128]{3,2,1,0:T(8,128)(2,1)S(1)} %all-to-all-done.3.in_ref) | copy-start | bytes 7077892
  275.7 58.2 %all-to-all-start.5 = ((bf16[16,1,4,128,256]{4,3,2,1,0:T(8,128)(2,1)}), bf16[16,1,4,128,256]{4,3,2,1,0:T(8,128)(2,1)}, u32[]{:S(2)}, u32[]{:S(2)}) async-start(bf16[16,1,4,128,256]{4,3,2,1,0:T(8,128)(2,1)} %get-tuple-element.172), calls=%async_computation.5 | async-start | bytes 8388608 | tf_op jit(solution)/shard_map/all_to_all | solution.py:324
  333.9 27.1 %all-to-all-start.7 = ((bf16[16,2,192,128]{3,2,1,0:T(8,128)(2,1)}), bf16[16,2,192,128]{3,2,1,0:T(8,128)(2,1)S(1)}, u32[]{:S(2)}, u32[]{:S(2)}) async-start(bf16[16,2,192,128]{3,2,1,0:T(8,128)(2,1)} %attend_0.1), calls=%async_computation.7 | async-start | bytes 3145728 | tf_op jit(solution)/shard_map/all_to_all | solution.py:324
  361.0 5.4 %copy-start.3 = (bf16[16,2,192,128]{3,2,1,0:T(8,128)(2,1)}, bf16[16,2,192,128]{3,2,1,0:T(8,128)(2,1)S(1)}, u32[]{:S(2)}) copy-start(bf16[16,2,192,128]{3,2,1,0:T(8,128)(2,1)S(1)} %all-to-all-done.7.in_ref) | copy-start | bytes 4718596
  361.0 17.7 %all-to-all-start.6 = ((bf16[16,1,192,128]{3,2,1,0:T(8,128)(2,1)}), bf16[16,1,192,128]{3,2,1,0:T(8,128)(2,1)S(1)}, u32[]{:S(2)}, u32[]{:S(2)}) async-start(bf16[16,1,192,128]{3,2,1,0:T(8,128)(2,1)} %attend_2.1), calls=%async_computation.6 | async-start | bytes 1572864 | tf_op jit(solution)/shard_map/all_to_all | solution.py:324
  378.6 0.9 copy-start.4
